TPU v7x, 128 devices: a whole 4x4x4 slice. The times are simulated.
128 devices in a mesh: row: 16 (over x, z_hi, core), col: 8 (over y, z_lo).
Axes of the slice: x: 4, y: 4, z: 4 (z_hi: 2, z_lo: 2; z = z_hi * 2 + z_lo), core: 2. Of those that a mesh axis runs over, the one named last changes fastest.
Arguments:
- front: float32 [48, 16, 128, 2, 8, 128], P(None, 'row', None, None, 'col')
- child_tiles: float32 [16, 8, 128, 128, 128], P('row', 'col'), may hold values from -1.5 to 1.5
- child_rows: int32 [16, 8, 128], P('row', 'col'), may hold values from 0 to 767, as said below
- child_cols: int32 [16, 8, 128], P('row', 'col'), may hold values from 0 to 15, as said below
Outputs:
- factored: float32 [48, 16, 128, 2, 8, 128], P(None, 'row', None, None, 'col')
Inputs may be any that keep to these rules, and one draw needn't show every extreme that they name: `child_rows`: parent block row of each child block. The owner of front block (i, j) is device (i mod 16, j mod 8); from one device at most 2 child blocks go to one owner, and some owners receive exactly 2 from every device. `child_cols`: parent block column of each child block, among the 2048 columns held; same owner bound as for child_rows.
All inputs are finite; a program needn't handle non-finite values.
Results may differ from a plain program's by a relative error of at most 0.00005.
Values sent between devices are 32-bit elements; how exact they have to be, the bound alone decides.
No kernel may reach another device: no remote copies, remote signals or barrier semaphores. Data moves between devices by JAX's collectives and lax.ppermute only.
A program may use at most 192 MiB of HBM per device.

v0:
```python
import jax
import jax.numpy as jnp
from jax import lax
from jax.sharding import PartitionSpec as P

CAP = 2


def broadcast(value, axis, source):
    kept = jnp.where(lax.axis_index(axis) == source, value, 0).astype(value.dtype)
    return lax.psum(kept, axis)


def factor_of(corner):
    return jnp.linalg.cholesky(0.5 * (corner + corner.T))


def solve_panel(factor, column):
    row_blocks, tile_size = (column.shape[0], column.shape[1])
    flattened = column.reshape(-1, tile_size)
    solved = jax.scipy.linalg.solve_triangular(factor, flattened.T, lower=True).T
    return solved.reshape(row_blocks, tile_size, tile_size)


def per_device(front, child_tiles, child_rows, child_cols):
    row_count = lax.axis_size("row")
    col_count = lax.axis_size("col")
    row_index = lax.axis_index("row")
    col_index = lax.axis_index("col")
    row_blocks, tile_size, col_blocks = (front.shape[0], front.shape[2], front.shape[3])
    local_front = front.reshape(row_blocks, tile_size, col_blocks, tile_size)
    flat_tiles = child_tiles.reshape(-1, tile_size, tile_size)
    parent_rows = child_rows.reshape(-1)
    parent_cols = child_cols.reshape(-1)
    devices = row_count * col_count
    slot_total = devices * CAP
    owners = parent_rows % row_count * col_count + parent_cols % col_count
    one_hot = (owners[:, None] == jnp.arange(devices, dtype=jnp.int32)[None, :]).astype(jnp.int32)
    before = jnp.sum(jnp.cumsum(one_hot, axis=0) * one_hot, axis=1) - 1
    send_slot = owners * CAP + before
    target = parent_rows // row_count * col_blocks + parent_cols // col_count
    send_tiles = (
        jnp.zeros((slot_total, tile_size, tile_size), jnp.float32).at[send_slot].set(flat_tiles)
    )
    send_index = jnp.full((slot_total,), -1, jnp.int32).at[send_slot].set(target)
    arrived_tiles, arrived_index = (
        lax.all_to_all(send_tiles, ("row", "col"), split_axis=0, concat_axis=0, tiled=True),
        lax.all_to_all(send_index, ("row", "col"), split_axis=0, concat_axis=0, tiled=True),
    )
    selector = (
        arrived_index[None, :] == jnp.arange(row_blocks * col_blocks, dtype=jnp.int32)[:, None]
    ).astype(jnp.float32)
    selector = selector.reshape(row_blocks, col_blocks, slot_total)
    assembled = local_front + jnp.einsum(
        "ams,spq->apmq", selector, arrived_tiles, precision=lax.Precision.HIGHEST
    )
    column = assembled[:, :, 0, :]
    corner = broadcast(column[0], "row", 0)
    panel_rows = solve_panel(factor_of(corner), column)
    panel_rows = broadcast(panel_rows, "col", 0)
    window_blocks = col_blocks * col_count // row_count
    window = lax.all_gather(panel_rows[:window_blocks][:, None], "row", axis=1, tiled=True)
    window = window.reshape(col_blocks, col_count, tile_size, tile_size)
    own_window = lax.dynamic_index_in_dim(window, col_index, axis=1, keepdims=False)
    update = jnp.einsum("apk,mqk->apmq", panel_rows, own_window, precision=lax.Precision.HIGHEST)
    global_rows = (jnp.arange(row_blocks, dtype=jnp.int32) * row_count + row_index)[
        :, None, None, None
    ]
    global_cols = (jnp.arange(col_blocks, dtype=jnp.int32) * col_count + col_index)[
        None, None, :, None
    ]
    result = assembled - jnp.where(global_rows > 0, update, jnp.zeros_like(update))
    result = jnp.where(global_cols == 0, panel_rows[:, :, None, :], result)
    return result.reshape(front.shape)


def solution(mesh):
    in_specs = (
        P(None, "row", None, None, "col", None),
        P("row", "col", None, None, None),
        P("row", "col", None),
        P("row", "col", None),
    )
    out_specs = P(None, "row", None, None, "col", None)
    return jax.shard_map(
        per_device, mesh=mesh, in_specs=in_specs, out_specs=out_specs, check_vma=False
    )
```

profile of v0, /device:TPU:0, one launch (start us, length us, event | category | flops | bytes accessed | tf_op | source)
XLA Modules:
  0.0 711.5 jit_solution(14597959788341730785)
XLA Ops:
  8.4 1.0 scatter_custom_fusion.1
  10.1 11.1 %all-to-all-start.1 = ((s32[128,2,1]{1,2,0:T(1,128)}), s32[128,2,1]{1,2,0:T(1,128)S(1)}, u32[]{:S(2)}, u32[]{:S(2)}) async-start(s32[128,2,1]{1,2,0:T(1,128)} %bitcast.9), calls=%async_computation.1 | async-start | bytes 131072 | tf_op jit(solution)/shard_map/all_to_all | solution.py:48
  21.3 7.8 %broadcast_in_dim.58 = f32[256,128,128]{2,1,0:T(8,128)} broadcast(f32[]{:T(128)} %constant.112.clone.1), dimensions={} | broadcast | bytes 16777220 | tf_op jit(solution)/shard_map/broadcast_in_dim | solution.py:43
  29.1 23.4 %scatter_fusion = f32[256,128,128]{2,1,0:T(8,128)} fusion(f32[256,128,128]{2,1,0:T(8,128)} %broadcast_in_dim.58, s32[128]{0:T(128)S(1)} %fusion.26, f32[128,128,128]{2,1,0:T(8,128)} %bitcast.97), kind=kCustom, calls=%fused_computation | custom fusion | bytes 25166336 | tf_op jit(solution)/shard_map/scatter | solution.py:43
  52.5 10.3 %all-to-all-start = ((f32[256,128,128]{2,1,0:T(8,128)}), f32[256,128,128]{2,1,0:T(8,128)}, u32[]{:S(2)}, u32[]{:S(2)}) async-start(f32[256,128,128]{2,1,0:T(8,128)} %scatter_fusion), calls=%async_computation | async-start | bytes 33554432 | tf_op jit(solution)/shard_map/all_to_all | solution.py:47
  63.0 14.1 %copy.25 = f32[48,1,128,2,1,128]{2,5,3,0,4,1:T(8,128)} copy(f32[48,1,128,2,1,128]{5,4,3,2,1,0:T(1,128)} %param.4) | data formatting | bytes 12582912 | tf_op args[0]
  77.6 0.8 reduce.9
  78.6 209.9 %all-to-all-done = f32[256,128,128]{2,1,0:T(8,128)} async-done(((f32[256,128,128]{2,1,0:T(8,128)}), f32[256,128,128]{2,1,0:T(8,128)}, u32[]{:S(2)}, u32[]{:S(2)}) %all-to-all-start) | async-done | bytes 16777248 | tf_op jit(solution)/shard_map/all_to_all | solution.py:47
  288.5 22.8 %fusion = f32[128,128,48,2]{1,2,3,0:T(8,128)} fusion(f32[256,128,128,1]{2,1,0,3:T(8,128)} %bitcast.8, s32[48,2]{0,1:T(2,128)S(1)} %multiply_add_fusion, s32[256]{0:T(256)S(1)} %eq.57), kind=kOutput, calls=%fused_computation.2 | convolution fusion | flops 4831862784 | bytes 23070080 | tf_op jit(solution)/shard_map/ams,spq->apmq/dot_general | solution.py:54
  311.2 6.6 copy.28
  317.9 5.9 bitcast_add_fusion
  323.8 2.7 copy-done
  327.4 131.3 %all-reduce.3.cloned.1.call-done = f32[128,128]{0,1:T(8,128)} async-done(((f32[128,128]{0,1:T(8,128)}), f32[128,128]{0,1:T(8,128)}) %all-reduce.3.cloned.1.call-update) | async-done | bytes 65552 | tf_op jit(solution)/shard_map/psum | solution.py:11
  458.7 0.9 copy.29
  459.6 0.9 fusion.16
  460.6 11.7 %cholesky.15 = f32[128,128]{1,0:T(8,128)S(1)} custom-call(f32[128,128]{1,0:T(8,128)S(1)} %fusion.15), custom_call_target="Cholesky" | custom-call | tf_op jit(solution)/shard_map/jit(cholesky)/cholesky | solution.py:15
  473.8 9.8 %custom-call.7 = f32[1,128,128]{1,2,0:T(8,128)S(1)} custom-call(f32[1,128,128]{2,1,0:T(8,128)S(1)} %fusion.12), custom_call_target="InvertDiagBlocksLowerTriangular" | custom-call | tf_op jit(solution)/shard_map/jit(_solve_triangular)/triangular_solve | solution.py:21
  483.6 7.9 %fusion.7 = f32[48,128,128]{2,1,0:T(8,128)} fusion(f32[48,128,2,128]{1,3,2,0:T(8,128)} %copy-done, pred[]{:T(512)S(6)} %eq.53, f32[1,128,128]{1,2,0:T(8,128)S(1)} %custom-call.7), kind=kOutput, calls=%fused_computation.10 | convolution fusion | flops 1208745984 | bytes 6356993 | tf_op jit(solution)/shard_map/jit(_solve_triangular)/triangular_solve | solution.py:21
  491.8 140.6 %all-reduce.5.cloned.1.call-done = f32[48,128,128]{2,1,0:T(8,128)} async-done(((f32[48,128,128]{2,1,0:T(8,128)}), f32[48,128,128]{2,1,0:T(8,128)}) %all-reduce.5.cloned.1.call-update) | async-done | bytes 3145744 | tf_op jit(solution)/shard_map/psum | solution.py:11
  632.4 1.6 slice.28
  634.0 3.7 copy.33
  637.7 43.4 %all-gather.3.cloned.1.call-done = f32[16,128,128]{2,1,0:T(8,128)} async-done(((f32[1,128,128]{2,1,0:T(8,128)}), f32[16,128,128]{2,1,0:T(8,128)}) %all-gather.3.cloned.1.call-update) | async-done | bytes 1048592 | tf_op jit(solution)/shard_map/all_gather | solution.py:62
  681.1 9.8 %select_bitcast_fusion = f32[48,1,128,2,1,128]{2,5,3,0,4,1:T(8,128)} fusion(f32[48,128,2,128]{1,3,2,0:T(8,128)} %copy-done, f32[48,128,128]{1,2,0:T(8,128)} %copy.33, pred[48]{0:T(512)(128)(4,1)S(1)} %add_compare_fusion, pred[2]{0:T(512)(128)(4,1)S(1)} %add_compare_fusion.1, f32[48,128,128]{2,1,0:T(8,128)S(1)} %copy-done.1, f32[2,8,128,128]{3,2,1,0:T(8,128)} %bitcast.98, ...), kind=kOutput, calls=%fused_computation.5 | convolution fusion | flops 2420637696 | bytes 19005494 | tf_op jit(solution)/shard_map/apk,mqk->apmq/dot_general | solution.py:65
  690.9 14.1 %copy.36 = f32[48,1,128,2,1,128]{5,4,3,2,1,0:T(1,128)} copy(f32[48,1,128,2,1,128]{2,5,3,0,4,1:T(8,128)} %select_bitcast_fusion) | data formatting | bytes 12582912 | tf_op jit(solution)/shard_map/reshape | solution.py:74
  (27 shorter events, 6.3 us)
Async XLA Ops:
  10.1 42.4 %all-to-all-start.1 = ((s32[128,2,1]{1,2,0:T(1,128)}), s32[128,2,1]{1,2,0:T(1,128)S(1)}, u32[]{:S(2)}, u32[]{:S(2)}) async-start(s32[128,2,1]{1,2,0:T(1,128)} %bitcast.9), calls=%async_computation.1 | async-start | bytes 131072 | tf_op jit(solution)/shard_map/all_to_all | solution.py:48
  52.5 235.9 %all-to-all-start = ((f32[256,128,128]{2,1,0:T(8,128)}), f32[256,128,128]{2,1,0:T(8,128)}, u32[]{:S(2)}, u32[]{:S(2)}) async-start(f32[256,128,128]{2,1,0:T(8,128)} %scatter_fusion), calls=%async_computation | async-start | bytes 33554432 | tf_op jit(solution)/shard_map/all_to_all | solution.py:47
  62.8 395.9 %all-reduce.3.cloned.1.call-start = ((), (), s32[]{:S(2)}) async-start(), calls=%async_computation.2 | async-start | bytes 131072 | tf_op jit(solution)/shard_map/psum | solution.py:11
  323.8 2.7 copy-start
  327.2 305.2 %all-reduce.5.cloned.1.call-start = ((), (), s32[]{:S(2)}) async-start(), calls=%async_computation.3 | async-start | bytes 6291456 | tf_op jit(solution)/shard_map/psum | solution.py:11
  491.5 189.6 %all-gather.3.cloned.1.call-start = ((), (), s32[]{:S(2)}) async-start(), calls=%async_computation.4 | async-start | bytes 1114112 | tf_op jit(solution)/shard_map/all_gather | solution.py:62
  632.4 48.7 %copy-start.1 = (f32[48,128,128]{2,1,0:T(8,128)S(1)}, f32[48,128,128]{2,1,0:T(8,128)}, u32[]{:S(2)}) copy-start(f32[48,128,128]{2,1,0:T(8,128)} %all-reduce.5.cloned.1.call-done) | copy-start | bytes 9437188
Sparse Core Ops, SparseCore 0:
  327.3 131.3 all-reduce.2
  491.6 140.7 all-reduce.4
  635.0 45.9 all-gather.2
where the time goes:
time: 714 us; the launch traced here: 711 us
  waiting for transfers between devices  525 us (74%)
  local copies, waits for them, and re-layouts  77.5 us (11%)
  matrix products  40.4 us (6%)
  other arithmetic  33 us (5%)
  starting transfers between devices  22.2 us (3%)
  between operations  13.2 us (2%)
    psum x2, waiting for transfers between devices, broadcast(): return lax.psum(kept, axis)  272 us
    all_to_all x1, waiting for transfers between devices, per_device(): lax.all_to_all(send_tiles, ('row', 'col'), split_axis=0, concat_axis=0, t...  210 us
    all_gather x1, waiting for transfers between devices, per_device(): lax.all_gather(panel_rows[:window_blocks][:, None], 'row', axis=1, tiled=...  43.4 us
    scatter x1, local copies, waits for them, and re-layouts, per_device(): jnp.zeros((slot_total, tile_size, tile_size), jnp.float32).at[send_slot]  23.4 us
    dot_general x1, matrix products, per_device(): jnp.einsum('ams,spq->apmq', selector, arrived_tiles, precision=lax.Precis...  22.8 us
    unnamed x5, local copies, waits for them, and re-layouts  16.8 us
  transfers between devices with their start and end apart: 5, of which 4 were waited for; matrix products, arithmetic and copies ran while one was open for 7% of the time, Pallas kernels for 0%

commit v1 on v0

v1 whole, which is shorter than its diff:
```python
import functools

import jax
import jax.numpy as jnp
from jax import lax
from jax.experimental import pallas as pl
from jax.experimental.pallas import tpu as pltpu
from jax.sharding import PartitionSpec as P

CAP = 2
HIGH = lax.Precision.HIGHEST
SMEM = pltpu.SMEM
VMEM = pltpu.VMEM


def tables(parent_rows, parent_cols, row_index, row_count, col_count):
    devices = row_count * col_count
    tiles = parent_rows.shape[0]
    order = jnp.arange(tiles, dtype=jnp.int32)
    row_of = parent_rows % row_count
    owners = row_of * col_count + parent_cols % col_count
    same = (owners[:, None] == owners[None, :]) & (order[None, :] < order[:, None])
    before = jnp.sum(same.astype(jnp.int32), axis=1)
    slot = owners * CAP + before
    block = parent_rows // row_count
    panel = parent_cols == 0
    place = block * (2 * 128) + parent_cols // col_count
    dest = jnp.arange(devices, dtype=jnp.int32)[:, None, None]
    part = jnp.arange(2 * CAP, dtype=jnp.int32)[None, :, None]
    in_main = (part < CAP) & (slot == dest * CAP + part) & ~panel
    in_panel = (part >= CAP) & panel & (row_of == dest // col_count) & (before == part - CAP)
    message = (
        jnp.sum(jnp.where(in_main, place + 1, 0) + jnp.where(in_panel, block + 1, 0), axis=2) - 1
    )
    panel_slot = (row_of ^ row_index) * CAP + before
    wanted = jnp.arange(row_count * CAP, dtype=jnp.int32)[:, None]
    chosen = panel & (panel_slot == wanted)
    panel_tiles = jnp.sum(jnp.where(chosen, order, 0), axis=1)
    return slot, panel_tiles, message


def pack_kernel(slot, panel_tiles, tiles, send, *rest):
    panels, (main_sem, panel_sem) = rest[:-2], rest[-2:]
    for k, panel in enumerate(panels):
        for s in range(CAP):
            pltpu.make_async_copy(
                tiles.at[panel_tiles[k * CAP + s]], panel.at[s], panel_sem.at[k]
            ).start()

    def start(k, carry):
        pltpu.make_async_copy(tiles.at[k], send.at[slot[k]], main_sem).start()
        return carry

    count = tiles.shape[0]
    lax.fori_loop(0, count, start, 0, unroll=8)
    for k, panel in enumerate(panels):
        pltpu.make_async_copy(tiles.at[pl.ds(0, CAP)], panel, panel_sem.at[k]).wait()
    pltpu.make_async_copy(tiles, send.at[pl.ds(0, count)], main_sem).wait()


def pack(slot, panel_tiles, tiles, slots, row_count):
    size = tiles.shape[1]
    out = [jax.ShapeDtypeStruct((slots, size, size), jnp.float32)]
    out += [jax.ShapeDtypeStruct((CAP, size, size), jnp.float32)] * row_count
    result = pl.pallas_call(
        pack_kernel,
        out_shape=out,
        in_specs=[
            pl.BlockSpec(memory_space=SMEM),
            pl.BlockSpec(memory_space=SMEM),
            pl.BlockSpec(memory_space=pl.ANY),
        ],
        out_specs=[pl.BlockSpec(memory_space=pl.ANY)] * len(out),
        scratch_shapes=[pltpu.SemaphoreType.DMA, pltpu.SemaphoreType.DMA((row_count,))],
        name="pack",
    )(slot, panel_tiles, tiles)
    return result[0], result[1:]


def column_kernel(shape, where, message, front, *refs):
    row_count, col_count, row_blocks, share = shape
    arrived = refs[:row_count]
    parts = refs[row_count : row_count + col_count]
    total = refs[-1]
    row_index, col_index = where[0], where[1]
    size = total.shape[1]

    @pl.when(col_index == 0)
    def _():
        def first(a, carry):
            total[a] = front[pl.ds(a * 2 * size, size, stride=2), :]
            return carry

        lax.fori_loop(0, row_blocks, first, 0)

    @pl.when(col_index != 0)
    def _():
        total[...] = jnp.zeros_like(total)

    for k in range(row_count):
        base = ((row_index ^ k) * col_count + col_index) * 2 * CAP + CAP
        for s in range(CAP):
            block = message[base + s]

            @pl.when(block >= 0)
            def _():
                total[block] += arrived[k][s]

    for k in range(col_count):
        parts[k][0] = total[0]
        parts[k][pl.ds(1, share)] = total[pl.ds((col_index ^ k) * share, share)]


def partial_column(where, message, front, arrived, row_count, col_count, row_blocks):
    size = front.shape[1]
    share = row_blocks // col_count
    out = [jax.ShapeDtypeStruct((share + 1, size, size), jnp.float32)] * col_count
    return pl.pallas_call(
        functools.partial(column_kernel, (row_count, col_count, row_blocks, share)),
        out_shape=out,
        in_specs=[pl.BlockSpec(memory_space=SMEM)] * 2
        + [pl.BlockSpec(memory_space=VMEM)] * (1 + row_count),
        out_specs=[pl.BlockSpec(memory_space=VMEM)] * col_count,
        scratch_shapes=[VMEM((row_blocks, size, size), jnp.float32)],
        compiler_params=pltpu.CompilerParams(vmem_limit_bytes=40 << 20),
        name="partial_column",
    )(where, message, front, *arrived)


def update_kernel(shape, where, front, inverse_t, window, *refs):
    row_blocks, share, col_count = shape
    shares = refs[:col_count]
    base, column, sems = refs[col_count:]
    row_index, col_index = where[0], where[1]
    size = inverse_t.shape[0]
    copies = [
        pltpu.make_async_copy(
            shares[k], column.at[pl.ds((col_index ^ k) * share, share)], sems.at[k]
        )
        for k in range(col_count)
    ]
    for copy in copies:
        copy.start()
    held = jnp.dot(
        window[...], inverse_t[...], precision=HIGH, preferred_element_type=jnp.float32
    )
    for copy in copies:
        copy.wait()
    contract = (((1,), (1,)), ((), ()))

    def block(a, carry):
        rows = jnp.dot(
            column[a], inverse_t[...], precision=HIGH, preferred_element_type=jnp.float32
        )
        update = lax.dot_general(
            rows, held, contract, precision=HIGH, preferred_element_type=jnp.float32
        )
        below = a * 16 + row_index > 0
        update = jnp.where(below, update, jnp.zeros_like(update))
        even = pl.ds(a * 2 * size, size, stride=2)
        odd = pl.ds(a * 2 * size + 1, size, stride=2)
        base[even, :] = jnp.where(col_index == 0, rows, front[even, :] - update[:, :size])
        base[odd, :] = front[odd, :] - update[:, size:]
        return carry

    lax.fori_loop(0, row_blocks, block, 0)


def update_front(where, front, inverse_t, window, shares, row_blocks):
    size = front.shape[1]
    col_count = len(shares)
    share = row_blocks // col_count
    return pl.pallas_call(
        functools.partial(update_kernel, (row_blocks, share, col_count)),
        out_shape=jax.ShapeDtypeStruct(front.shape, jnp.float32),
        in_specs=[pl.BlockSpec(memory_space=SMEM)]
        + [pl.BlockSpec(memory_space=VMEM)] * 3
        + [pl.BlockSpec(memory_space=pl.ANY)] * col_count,
        out_specs=pl.BlockSpec(memory_space=VMEM),
        scratch_shapes=[
            VMEM((row_blocks, size, size), jnp.float32),
            pltpu.SemaphoreType.DMA((col_count,)),
        ],
        compiler_params=pltpu.CompilerParams(vmem_limit_bytes=40 << 20),
        name="update_front",
    )(where, front, inverse_t, window, *shares)


def add_kernel(per_step, message, base, tiles, out, sem):
    step = pl.program_id(0)

    @pl.when(step == 0)
    def _():
        copy = pltpu.make_async_copy(base, out, sem)
        copy.start()
        copy.wait()

    size = tiles.shape[1]

    def add(j, carry):
        slot = step * per_step + j
        place = message[slot // CAP * 2 * CAP + slot % CAP]

        @pl.when(place >= 0)
        def _():
            rows = pl.ds(place, size, stride=2)
            out[rows, :] += tiles[j]

        return carry

    lax.fori_loop(0, per_step, add, 0)


def add_tiles(message, base, tiles):
    slots, size = tiles.shape[:2]
    per_step = 32
    return pl.pallas_call(
        functools.partial(add_kernel, per_step),
        out_shape=jax.ShapeDtypeStruct(base.shape, jnp.float32),
        grid=(slots // per_step,),
        in_specs=[
            pl.BlockSpec(memory_space=SMEM),
            pl.BlockSpec(memory_space=pl.ANY),
            pl.BlockSpec((per_step, size, size), lambda i: (i, 0, 0)),
        ],
        out_specs=pl.BlockSpec(base.shape, lambda i: (0, 0)),
        scratch_shapes=[pltpu.SemaphoreType.DMA],
        compiler_params=pltpu.CompilerParams(vmem_limit_bytes=40 << 20),
        name="add_tiles",
    )(message, base, tiles)


def exchange(parts, axis):
    count = len(parts)
    return [parts[0]] + [
        lax.ppermute(parts[k], axis, [(i, i ^ k) for i in range(count)]) for k in range(1, count)
    ]


def per_device(front, child_tiles, child_rows, child_cols):
    row_count = lax.axis_size("row")
    col_count = lax.axis_size("col")
    row_index = lax.axis_index("row")
    col_index = lax.axis_index("col")
    row_blocks, size, col_blocks = (front.shape[0], front.shape[2], front.shape[3])
    share = row_blocks // col_count
    flat_front = front.reshape(row_blocks * size * col_blocks, size)
    tiles = child_tiles.reshape(-1, size, size)
    slots = row_count * col_count * CAP
    where = jnp.stack([row_index, col_index]).astype(jnp.int32)

    slot, panel_tiles, message = tables(
        child_rows.reshape(-1), child_cols.reshape(-1), row_index, row_count, col_count
    )
    both = ("row", "col")
    message = lax.all_to_all(message, both, split_axis=0, concat_axis=0, tiled=True).reshape(-1)
    send, panel_send = pack(slot, panel_tiles, tiles, slots, row_count)
    arrived = lax.all_to_all(send, both, split_axis=0, concat_axis=0, tiled=True)

    panel_arrived = exchange(panel_send, "row")
    parts = partial_column(
        where, message, flat_front, panel_arrived, row_count, col_count, row_blocks
    )
    summed = functools.reduce(jnp.add, exchange(parts, "col"))
    own_share, own_window = summed[1:], summed[0]
    shares = exchange([own_share] * col_count, "col")
    windows = jnp.stack(exchange([own_window] * row_count, "row"))
    corner = lax.dynamic_index_in_dim(windows, row_index, axis=0, keepdims=False)
    held = [
        lax.dynamic_index_in_dim(
            windows, row_index ^ (m * col_count + col_index), axis=0, keepdims=False
        )
        for m in range(col_blocks)
    ]
    factor = jnp.linalg.cholesky(0.5 * (corner + corner.T))
    inverse = jax.scipy.linalg.solve_triangular(
        factor, jnp.eye(size, dtype=jnp.float32), lower=True
    )
    base = update_front(
        where, flat_front, inverse.T, jnp.concatenate(held, axis=0), shares, row_blocks
    )
    return add_tiles(message, base, arrived).reshape(front.shape)


def solution(mesh):
    in_specs = (
        P(None, "row", None, None, "col", None),
        P("row", "col", None, None, None),
        P("row", "col", None),
        P("row", "col", None),
    )
    out_specs = P(None, "row", None, None, "col", None)
    return jax.shard_map(
        per_device, mesh=mesh, in_specs=in_specs, out_specs=out_specs, check_vma=False
    )
```

time: 714 us -> 853 us (1.19)
  Pallas kernels: 0 us -> 364 us
  waiting for transfers between devices: 525 us -> 298 us
  starting transfers between devices: 22.2 us -> 139 us
  local copies, waits for them, and re-layouts: 77.5 us -> 21 us
  matrix products: 40.4 us -> 0.25 us
  between operations: 13.2 us -> 0.59 us
    pallas_call x0 -> x4, Pallas kernels: none -> 364 us  [the longest x1 320 us: pack(): pl.pallas_call(pack_kernel, out_shape=out, in_specs=[pl.BlockSpec(memory_...]
    ppermute x0 -> x44, waiting for transfers between devices: none -> 298 us  [exchange(): lax.ppermute(parts[k], axis, [(i, i ^ k) for i in range(count)])]
    psum x2 -> x0, waiting for transfers between devices: 272 us -> none  [broadcast(): return lax.psum(kept, axis)]
    all_to_all x2, waiting for transfers between devices: 210 us -> 0.01 us  [the longest x1 0.01 us: per_device(): lax.all_to_all(message, both, split_axis=0, concat_axis=0, tiled=True)]
    ppermute x0 -> x44, starting transfers between devices: none -> 118 us  [exchange(): lax.ppermute(parts[k], axis, [(i, i ^ k) for i in range(count)])]
    all_gather x1 -> x0, waiting for transfers between devices: 43.4 us -> none  [per_device(): lax.all_gather(panel_rows[:window_blocks][:, None], 'row', axis=1, tiled=...]
    dot_general x2 -> x0, matrix products: 32.6 us -> none  [the longest x1 22.8 us: per_device(): jnp.einsum('ams,spq->apmq', selector, arrived_tiles, precision=lax.Precis...]
    scatter x2 -> x0, local copies, waits for them, and re-layouts: 24.4 us -> none  [the longest x1 23.4 us: per_device(): jnp.zeros((slot_total, tile_size, tile_size), jnp.float32).at[send_slot]]
  transfers between devices with their start and end apart: 5 -> 46, of which waited for: 4 -> 25; matrix products, arithmetic and copies ran while one was open for 7% -> 4% of each run, Pallas kernels for 0% -> 41%
where the time goes in v1:
time: 853 us; the launch traced here: 852 us
  Pallas kernels  364 us (43%)
  waiting for transfers between devices  298 us (35%)
  starting transfers between devices  139 us (16%)
  other arithmetic  29.2 us (3%)
  local copies, waits for them, and re-layouts  21 us (2%)
    pallas_call x1, Pallas kernels, pack(): pl.pallas_call(pack_kernel, out_shape=out, in_specs=[pl.BlockSpec(memory_...  320 us
    ppermute x44, waiting for transfers between devices, exchange(): lax.ppermute(parts[k], axis, [(i, i ^ k) for i in range(count)])  298 us
    ppermute x44, starting transfers between devices, exchange(): lax.ppermute(parts[k], axis, [(i, i ^ k) for i in range(count)])  118 us
    pallas_call x1, Pallas kernels, update_front(): pl.pallas_call(functools.partial(update_kernel, (row_blocks, share, col_c...  29 us
    unnamed x52, local copies, waits for them, and re-layouts  17.2 us
  transfers between devices with their start and end apart: 46, of which 25 were waited for; matrix products, arithmetic and copies ran while one was open for 4% of the time, Pallas kernels for 41%

profile of v1, /device:TPU:0, one launch (start us, length us, event | category | flops | bytes accessed | tf_op | source)
XLA Modules:
  0.0 852.1 jit_solution(336797966679071111)
XLA Ops:
  4.2 11.2 %all-to-all-start = ((s32[128,1,4]{2,1,0:T(1,128)}), s32[128,1,4]{2,1,0:T(1,128)S(1)}, u32[]{:S(2)}, u32[]{:S(2)}) async-start(s32[128,1,4]{2,1,0:T(1,128)} %copy.14), calls=%async_computation | async-start | bytes 131072 | tf_op jit(solution)/shard_map/all_to_all | solution.py:256
  17.2 319.6 %pack.1 = (f32[256,128,128]{2,1,0:T(8,128)}, f32[2,128,128]{2,1,0:T(8,128)}, f32[2,128,128]{2,1,0:T(8,128)}, f32[2,128,128]{2,1,0:T(8,128)}, f32[2,128,128]{2,1,...) custom-call(s32[128]{0:T(128)} %multiply_add_fusion.1.slot, ...), custom_call_target="tpu_custom_call" | custom-call | tf_op jit(solution)/shard_map/pack/pallas_call | solution.py:65
  337.0 10.3 %all-to-all-start.1 = ((f32[256,128,128]{2,1,0:T(8,128)}), f32[256,128,128]{2,1,0:T(8,128)}, u32[]{:S(2)}, u32[]{:S(2)}) async-start(f32[256,128,128]{2,1,0:T(8,128)} %get-tuple-element.54), calls=%async_computation.1 | async-start | bytes 33554432 | tf_op jit(solution)/shard_map/all_to_all | solution.py:258
  356.3 131.3 %collective-permute-done.1.refs_2_ = f32[2,128,128]{2,1,0:T(8,128)S(1)} collective-permute-done((f32[2,128,128]{2,1,0:T(8,128)S(1)}, f32[2,128,128]{2,1,0:T(8,128)S(1)}, u32[]{:S(2)}, u32[]{:S(2)}) %collective-permute-start.1) | collective-permute-done | bytes 131104 | tf_op jit(solution)/shard_map/ppermute | solution.py:236
  487.5 10.0 %collective-permute-start.6 = (f32[2,128,128]{2,1,0:T(8,128)S(1)}, f32[2,128,128]{2,1,0:T(8,128)S(1)}, u32[]{:S(2)}, u32[]{:S(2)}) collective-permute-start(f32[2,128,128]{2,1,0:T(8,128)S(1)} %copy-done.12), channel_id=1, source_target_pairs={{0,56},{8,48},{16,40},{24,32},{32,24},{40,16},{48,8},{56,0},{64,12... | collective-permute-start | bytes 393224 | tf_op jit(solution)/shard_map/ppermute | solution.py:236
  497.5 38.7 %collective-permute-done.2.refs_3_ = f32[2,128,128]{2,1,0:T(8,128)S(1)} collective-permute-done((f32[2,128,128]{2,1,0:T(8,128)S(1)}, f32[2,128,128]{2,1,0:T(8,128)S(1)}, u32[]{:S(2)}, u32[]{:S(2)}) %collective-permute-start.2) | collective-permute-done | bytes 131104 | tf_op jit(solution)/shard_map/ppermute | solution.py:236
  536.2 10.5 %collective-permute-start.7 = (f32[2,128,128]{2,1,0:T(8,128)S(1)}, f32[2,128,128]{2,1,0:T(8,128)S(1)}, u32[]{:S(2)}, u32[]{:S(2)}) collective-permute-start(f32[2,128,128]{2,1,0:T(8,128)S(1)} %copy-done.11), channel_id=1, source_target_pairs={{0,64},{8,72},{16,80},{24,88},{32,96},{40,104},{48,112},{56,120},{... | collective-permute-start | bytes 393224 | tf_op jit(solution)/shard_map/ppermute | solution.py:236
  546.7 12.8 %collective-permute-done.3.refs_4_ = f32[2,128,128]{2,1,0:T(8,128)S(1)} collective-permute-done((f32[2,128,128]{2,1,0:T(8,128)S(1)}, f32[2,128,128]{2,1,0:T(8,128)S(1)}, u32[]{:S(2)}, u32[]{:S(2)}) %collective-permute-start.3) | collective-permute-done | bytes 131104 | tf_op jit(solution)/shard_map/ppermute | solution.py:236
  559.5 16.4 %collective-permute-start.8 = (f32[2,128,128]{2,1,0:T(8,128)S(1)}, f32[2,128,128]{2,1,0:T(8,128)S(1)}, u32[]{:S(2)}, u32[]{:S(2)}) collective-permute-start(f32[2,128,128]{2,1,0:T(8,128)S(1)} %copy-done.10), channel_id=1, source_target_pairs={{0,72},{8,64},{16,88},{24,80},{32,104},{40,96},{48,120},{56,112},{... | collective-permute-start | bytes 393224 | tf_op jit(solution)/shard_map/ppermute | solution.py:236
  576.1 7.8 collective-permute-start.10
  595.1 8.7 %collective-permute-done.13.refs_14_ = f32[2,128,128]{2,1,0:T(8,128)S(1)} collective-permute-done((f32[2,128,128]{2,1,0:T(8,128)S(1)}, f32[2,128,128]{2,1,0:T(8,128)S(1)}, u32[]{:S(2)}, u32[]{:S(2)}) %collective-permute-start.13) | collective-permute-done | bytes 131104 | tf_op jit(solution)/shard_map/ppermute | solution.py:236
  615.0 9.6 %collective-permute-start.18 = (f32[7,128,128]{2,1,0:T(8,128)S(1)}, f32[7,128,128]{2,1,0:T(8,128)S(1)}, u32[]{:S(2)}, u32[]{:S(2)}) collective-permute-start(f32[7,128,128]{2,1,0:T(8,128)S(1)} %get-tuple-element.50), channel_id=1, source_target_pairs={{0,4},{1,5},{2,6},{3,7},{4,0},{5,1},{6,2},{7,3},{8,12},{9,13},{10,... | collective-permute-start | bytes 1376264 | tf_op jit(solution)/shard_map/ppermute | solution.py:236
  628.8 5.7 collective-permute-start.21
  636.2 16.2 %collective-permute-done.18 = f32[7,128,128]{2,1,0:T(8,128)S(1)} collective-permute-done((f32[7,128,128]{2,1,0:T(8,128)S(1)}, f32[7,128,128]{2,1,0:T(8,128)S(1)}, u32[]{:S(2)}, u32[]{:S(2)}) %collective-permute-start.18) | collective-permute-done | bytes 458784 | tf_op jit(solution)/shard_map/ppermute | solution.py:236
  652.3 10.5 %collective-permute-done.19 = f32[7,128,128]{2,1,0:T(8,128)S(1)} collective-permute-done((f32[7,128,128]{2,1,0:T(8,128)S(1)}, f32[7,128,128]{2,1,0:T(8,128)S(1)}, u32[]{:S(2)}, u32[]{:S(2)}) %collective-permute-start.19) | collective-permute-done | bytes 458784 | tf_op jit(solution)/shard_map/ppermute | solution.py:236
  662.8 6.7 collective-permute-done.21
  679.0 7.1 collective-permute-start.23
  686.7 9.2 %collective-permute-done.23 = f32[128,128]{1,0:T(8,128)S(1)} collective-permute-done((f32[128,128]{1,0:T(8,128)S(1)}, f32[128,128]{1,0:T(8,128)S(1)}, u32[]{:S(2)}, u32[]{:S(2)}) %collective-permute-start.23) | collective-permute-done | bytes 65568 | tf_op jit(solution)/shard_map/ppermute | solution.py:236
  736.6 5.4 collective-permute-done.31
  743.9 5.6 collective-permute-done.32
  776.9 11.7 %cholesky.14 = f32[128,128]{1,0:T(8,128)S(1)} custom-call(f32[128,128]{1,0:T(8,128)S(1)} %fusion.3), custom_call_target="Cholesky" | custom-call | tf_op jit(solution)/shard_map/jit(cholesky)/cholesky | solution.py:275
  793.4 9.8 %custom-call.7 = f32[1,128,128]{1,2,0:T(8,128)S(1)} custom-call(f32[1,128,128]{2,1,0:T(8,128)S(1)} %fusion), custom_call_target="InvertDiagBlocksLowerTriangular" | custom-call | tf_op jit(solution)/shard_map/jit(_solve_triangular)/triangular_solve | solution.py:276
  803.6 29.0 %update_front.1.base = f32[12288,128]{1,0:T(8,128)S(1)} custom-call(s32[2]{0:T(128)S(1)} %pad_add_fusion.where, f32[12288,128]{1,0:T(8,128)} %bitcast.102, f32[128,128]{1,0:T(8,128)S(1)} %fusion.1.inverse_t, f32[256,128]{1,0:T(8,128)S(1)} %pad_maximum_fusion.window, f32[6,128,128]{2,1,0:T(8,128)S(1)} %slice.21.refs_0_, ...), custom_call_target="tpu_custom_call" | custom-call | tf_op jit(solution)/shard_map/update_front/pallas_call | solution.py:173
  838.1 13.8 %add_tiles.1 = f32[12288,128]{1,0:T(8,128)} custom-call(s32[512]{0:T(512)S(1)} %reshape.328.message, f32[12288,128]{1,0:T(8,128)S(1)} %copy-done.2, f32[256,128,128]{2,1,0:T(8,128)} %all-to-all-done.1.tiles), custom_call_target="tpu_custom_call" | custom-call | tf_op jit(solution)/shard_map/add_tiles/pallas_call | solution.py:217
  (164 shorter events, 134.1 us)
Async XLA Ops:
  4.2 332.6 %all-to-all-start = ((s32[128,1,4]{2,1,0:T(1,128)}), s32[128,1,4]{2,1,0:T(1,128)S(1)}, u32[]{:S(2)}, u32[]{:S(2)}) async-start(s32[128,1,4]{2,1,0:T(1,128)} %copy.14), calls=%async_computation | async-start | bytes 131072 | tf_op jit(solution)/shard_map/all_to_all | solution.py:256
  337.0 498.3 %all-to-all-start.1 = ((f32[256,128,128]{2,1,0:T(8,128)}), f32[256,128,128]{2,1,0:T(8,128)}, u32[]{:S(2)}, u32[]{:S(2)}) async-start(f32[256,128,128]{2,1,0:T(8,128)} %get-tuple-element.54), calls=%async_computation.1 | async-start | bytes 33554432 | tf_op jit(solution)/shard_map/all_to_all | solution.py:258
  347.4 140.1 %collective-permute-start.1 = (f32[2,128,128]{2,1,0:T(8,128)S(1)}, f32[2,128,128]{2,1,0:T(8,128)S(1)}, u32[]{:S(2)}, u32[]{:S(2)}) collective-permute-start(f32[2,128,128]{2,1,0:T(8,128)S(1)} %copy-done.17), channel_id=1, source_target_pairs={{0,16},{8,24},{16,0},{24,8},{32,48},{40,56},{48,32},{56,40},{64,80... | collective-permute-start | bytes 393224 | tf_op jit(solution)/shard_map/ppermute | solution.py:236
  350.3 185.9 %collective-permute-start.2 = (f32[2,128,128]{2,1,0:T(8,128)S(1)}, f32[2,128,128]{2,1,0:T(8,128)S(1)}, u32[]{:S(2)}, u32[]{:S(2)}) collective-permute-start(f32[2,128,128]{2,1,0:T(8,128)S(1)} %copy-done.16), channel_id=1, source_target_pairs={{0,24},{8,16},{16,8},{24,0},{32,56},{40,48},{48,40},{56,32},{64,88... | collective-permute-start | bytes 393224 | tf_op jit(solution)/shard_map/ppermute | solution.py:236
  350.8 208.7 %collective-permute-start.3 = (f32[2,128,128]{2,1,0:T(8,128)S(1)}, f32[2,128,128]{2,1,0:T(8,128)S(1)}, u32[]{:S(2)}, u32[]{:S(2)}) collective-permute-start(f32[2,128,128]{2,1,0:T(8,128)S(1)} %copy-done.15), channel_id=1, source_target_pairs={{0,32},{8,40},{16,48},{24,56},{32,0},{40,8},{48,16},{56,24},{64,96... | collective-permute-start | bytes 393224 | tf_op jit(solution)/shard_map/ppermute | solution.py:236
  351.9 224.0 %collective-permute-start.4 = (f32[2,128,128]{2,1,0:T(8,128)S(1)}, f32[2,128,128]{2,1,0:T(8,128)S(1)}, u32[]{:S(2)}, u32[]{:S(2)}) collective-permute-start(f32[2,128,128]{2,1,0:T(8,128)S(1)} %copy-done.14), channel_id=1, source_target_pairs={{0,40},{8,32},{16,56},{24,48},{32,8},{40,0},{48,24},{56,16},{64,10... | collective-permute-start | bytes 393224 | tf_op jit(solution)/shard_map/ppermute | solution.py:236
  352.5 223.6 %collective-permute-start.5 = (f32[2,128,128]{2,1,0:T(8,128)S(1)}, f32[2,128,128]{2,1,0:T(8,128)S(1)}, u32[]{:S(2)}, u32[]{:S(2)}) collective-permute-start(f32[2,128,128]{2,1,0:T(8,128)S(1)} %copy-done.13), channel_id=1, source_target_pairs={{0,48},{8,56},{16,32},{24,40},{32,16},{40,24},{48,0},{56,8},{64,11... | collective-permute-start | bytes 393224 | tf_op jit(solution)/shard_map/ppermute | solution.py:236
  487.5 96.4 %collective-permute-start.6 = (f32[2,128,128]{2,1,0:T(8,128)S(1)}, f32[2,128,128]{2,1,0:T(8,128)S(1)}, u32[]{:S(2)}, u32[]{:S(2)}) collective-permute-start(f32[2,128,128]{2,1,0:T(8,128)S(1)} %copy-done.12), channel_id=1, source_target_pairs={{0,56},{8,48},{16,40},{24,32},{32,24},{40,16},{48,8},{56,0},{64,12... | collective-permute-start | bytes 393224 | tf_op jit(solution)/shard_map/ppermute | solution.py:236
  536.2 48.4 %collective-permute-start.7 = (f32[2,128,128]{2,1,0:T(8,128)S(1)}, f32[2,128,128]{2,1,0:T(8,128)S(1)}, u32[]{:S(2)}, u32[]{:S(2)}) collective-permute-start(f32[2,128,128]{2,1,0:T(8,128)S(1)} %copy-done.11), channel_id=1, source_target_pairs={{0,64},{8,72},{16,80},{24,88},{32,96},{40,104},{48,112},{56,120},{... | collective-permute-start | bytes 393224 | tf_op jit(solution)/shard_map/ppermute | solution.py:236
  559.5 28.4 %collective-permute-start.8 = (f32[2,128,128]{2,1,0:T(8,128)S(1)}, f32[2,128,128]{2,1,0:T(8,128)S(1)}, u32[]{:S(2)}, u32[]{:S(2)}) collective-permute-start(f32[2,128,128]{2,1,0:T(8,128)S(1)} %copy-done.10), channel_id=1, source_target_pairs={{0,72},{8,64},{16,88},{24,80},{32,104},{40,96},{48,120},{56,112},{... | collective-permute-start | bytes 393224 | tf_op jit(solution)/shard_map/ppermute | solution.py:236
  575.9 17.3 %collective-permute-start.9 = (f32[2,128,128]{2,1,0:T(8,128)S(1)}, f32[2,128,128]{2,1,0:T(8,128)S(1)}, u32[]{:S(2)}, u32[]{:S(2)}) collective-permute-start(f32[2,128,128]{2,1,0:T(8,128)S(1)} %copy-done.9), channel_id=1, source_target_pairs={{0,80},{8,88},{16,64},{24,72},{32,112},{40,120},{48,96},{56,104},{... | collective-permute-start | bytes 393224 | tf_op jit(solution)/shard_map/ppermute | solution.py:236
  576.1 19.0 %collective-permute-start.10 = (f32[2,128,128]{2,1,0:T(8,128)S(1)}, f32[2,128,128]{2,1,0:T(8,128)S(1)}, u32[]{:S(2)}, u32[]{:S(2)}) collective-permute-start(f32[2,128,128]{2,1,0:T(8,128)S(1)} %copy-done.8), channel_id=1, source_target_pairs={{0,88},{8,80},{16,72},{24,64},{32,120},{40,112},{48,104},{56,96},{... | collective-permute-start | bytes 393224 | tf_op jit(solution)/shard_map/ppermute | solution.py:236
  587.8 16.0 %collective-permute-start.13 = (f32[2,128,128]{2,1,0:T(8,128)S(1)}, f32[2,128,128]{2,1,0:T(8,128)S(1)}, u32[]{:S(2)}, u32[]{:S(2)}) collective-permute-start(f32[2,128,128]{2,1,0:T(8,128)S(1)} %copy-done.5), channel_id=1, source_target_pairs={{0,112},{8,120},{16,96},{24,104},{32,80},{40,88},{48,64},{56,72},{... | collective-permute-start | bytes 393224 | tf_op jit(solution)/shard_map/ppermute | solution.py:236
  613.5 22.7 %collective-permute-start.17 = (f32[7,128,128]{2,1,0:T(8,128)S(1)}, f32[7,128,128]{2,1,0:T(8,128)S(1)}, u32[]{:S(2)}, u32[]{:S(2)}) collective-permute-start(f32[7,128,128]{2,1,0:T(8,128)S(1)} %get-tuple-element.49), channel_id=1, source_target_pairs={{0,3},{1,2},{2,1},{3,0},{4,7},{5,6},{6,5},{7,4},{8,11},{9,10},{10,... | collective-permute-start | bytes 1376264 | tf_op jit(solution)/shard_map/ppermute | solution.py:236
  615.0 37.3 %collective-permute-start.18 = (f32[7,128,128]{2,1,0:T(8,128)S(1)}, f32[7,128,128]{2,1,0:T(8,128)S(1)}, u32[]{:S(2)}, u32[]{:S(2)}) collective-permute-start(f32[7,128,128]{2,1,0:T(8,128)S(1)} %get-tuple-element.50), channel_id=1, source_target_pairs={{0,4},{1,5},{2,6},{3,7},{4,0},{5,1},{6,2},{7,3},{8,12},{9,13},{10,... | collective-permute-start | bytes 1376264 | tf_op jit(solution)/shard_map/ppermute | solution.py:236
  624.7 38.1 %collective-permute-start.19 = (f32[7,128,128]{2,1,0:T(8,128)S(1)}, f32[7,128,128]{2,1,0:T(8,128)S(1)}, u32[]{:S(2)}, u32[]{:S(2)}) collective-permute-start(f32[7,128,128]{2,1,0:T(8,128)S(1)} %get-tuple-element.51), channel_id=1, source_target_pairs={{0,5},{1,4},{2,7},{3,6},{4,1},{5,0},{6,3},{7,2},{8,13},{9,12},{10,... | collective-permute-start | bytes 1376264 | tf_op jit(solution)/shard_map/ppermute | solution.py:236
  624.7 38.1 %collective-permute-start.20 = (f32[7,128,128]{2,1,0:T(8,128)S(1)}, f32[7,128,128]{2,1,0:T(8,128)S(1)}, u32[]{:S(2)}, u32[]{:S(2)}) collective-permute-start(f32[7,128,128]{2,1,0:T(8,128)S(1)} %get-tuple-element.52), channel_id=1, source_target_pairs={{0,6},{1,7},{2,4},{3,5},{4,2},{5,3},{6,0},{7,1},{8,14},{9,15},{10,... | collective-permute-start | bytes 1376264 | tf_op jit(solution)/shard_map/ppermute | solution.py:236
  628.8 40.7 %collective-permute-start.21 = (f32[7,128,128]{2,1,0:T(8,128)S(1)}, f32[7,128,128]{2,1,0:T(8,128)S(1)}, u32[]{:S(2)}, u32[]{:S(2)}) collective-permute-start(f32[7,128,128]{2,1,0:T(8,128)S(1)} %get-tuple-element.53), channel_id=1, source_target_pairs={{0,7},{1,6},{2,5},{3,4},{4,3},{5,2},{6,1},{7,0},{8,15},{9,14},{10,... | collective-permute-start | bytes 1376264 | tf_op jit(solution)/shard_map/ppermute | solution.py:236
  670.4 118.9 %collective-permute-start.43 = (f32[6,128,128]{2,1,0:T(8,128)S(1)}, f32[6,128,128]{2,1,0:T(8,128)S(1)}, u32[]{:S(2)}, u32[]{:S(2)}) collective-permute-start(f32[6,128,128]{2,1,0:T(8,128)S(1)} %slice.21.refs_0_), channel_id=1, source_target_pairs={{0,7},{1,6},{2,5},{3,4},{4,3},{5,2},{6,1},{7,0},{8,15},{9,14},{10,... | collective-permute-start | bytes 1179656 | tf_op jit(solution)/shard_map/ppermute | solution.py:236
  673.5 117.8 %collective-permute-start.42 = (f32[6,128,128]{2,1,0:T(8,128)S(1)}, f32[6,128,128]{2,1,0:T(8,128)S(1)}, u32[]{:S(2)}, u32[]{:S(2)}) collective-permute-start(f32[6,128,128]{2,1,0:T(8,128)S(1)} %slice.21.refs_0_), channel_id=1, source_target_pairs={{0,6},{1,7},{2,4},{3,5},{4,2},{5,3},{6,0},{7,1},{8,14},{9,15},{10,... | collective-permute-start | bytes 1179656 | tf_op jit(solution)/shard_map/ppermute | solution.py:236
  673.8 129.8 %collective-permute-start.41 = (f32[6,128,128]{2,1,0:T(8,128)S(1)}, f32[6,128,128]{2,1,0:T(8,128)S(1)}, u32[]{:S(2)}, u32[]{:S(2)}) collective-permute-start(f32[6,128,128]{2,1,0:T(8,128)S(1)} %slice.21.refs_0_), channel_id=1, source_target_pairs={{0,5},{1,4},{2,7},{3,6},{4,1},{5,0},{6,3},{7,2},{8,13},{9,12},{10,... | collective-permute-start | bytes 1179656 | tf_op jit(solution)/shard_map/ppermute | solution.py:236
  679.0 124.6 %collective-permute-start.40 = (f32[6,128,128]{2,1,0:T(8,128)S(1)}, f32[6,128,128]{2,1,0:T(8,128)S(1)}, u32[]{:S(2)}, u32[]{:S(2)}) collective-permute-start(f32[6,128,128]{2,1,0:T(8,128)S(1)} %slice.21.refs_0_), channel_id=1, source_target_pairs={{0,4},{1,5},{2,6},{3,7},{4,0},{5,1},{6,2},{7,3},{8,12},{9,13},{10,... | collective-permute-start | bytes 1179656 | tf_op jit(solution)/shard_map/ppermute | solution.py:236
  679.0 16.9 %collective-permute-start.23 = (f32[128,128]{1,0:T(8,128)S(1)}, f32[128,128]{1,0:T(8,128)S(1)}, u32[]{:S(2)}, u32[]{:S(2)}) collective-permute-start(f32[128,128]{1,0:T(8,128)S(1)} %get-tuple-element.64), channel_id=1, source_target_pairs={{0,16},{8,24},{16,0},{24,8},{32,48},{40,56},{48,32},{56,40},{64,80... | collective-permute-start | bytes 196616 | tf_op jit(solution)/shard_map/ppermute | solution.py:236
  775.1 28.4 %collective-permute-start.39 = (f32[6,128,128]{2,1,0:T(8,128)S(1)}, f32[6,128,128]{2,1,0:T(8,128)S(1)}, u32[]{:S(2)}, u32[]{:S(2)}) collective-permute-start(f32[6,128,128]{2,1,0:T(8,128)S(1)} %slice.21.refs_0_), channel_id=1, source_target_pairs={{0,3},{1,2},{2,1},{3,0},{4,7},{5,6},{6,5},{7,4},{8,11},{9,10},{10,... | collective-permute-start | bytes 1179656 | tf_op jit(solution)/shard_map/ppermute | solution.py:236
  (41 other events, 2592.9 us)

commit v2 on v0

v2 whole, which is shorter than its diff:
```python
import functools

import jax
import jax.numpy as jnp
from jax import lax
from jax.experimental import pallas as pl
from jax.experimental.pallas import tpu as pltpu
from jax.sharding import PartitionSpec as P

CAP = 2
HIGH = lax.Precision.HIGHEST
SMEM = pltpu.SMEM
VMEM = pltpu.VMEM
ANY = pl.ANY
LIMIT = pltpu.CompilerParams(vmem_limit_bytes=58 << 20)


def send_tables(parent_rows, parent_cols, row_count, col_count, size):
    tiles = parent_rows.shape[0]
    order = jnp.arange(tiles, dtype=jnp.int32)
    row_of = parent_rows % row_count
    owners = row_of * col_count + parent_cols % col_count
    same = (owners[:, None] == owners[None, :]) & (order[None, :] < order[:, None])
    slot = owners * CAP + jnp.sum(same.astype(jnp.int32), axis=1)
    place = parent_rows // row_count * (2 * size) + parent_cols // col_count
    wanted = jnp.arange(row_count * CAP, dtype=jnp.int32)[:, None]
    chosen = (parent_cols == 0) & (
        slot == wanted // CAP * (col_count * CAP) + wanted % CAP
    )
    panel_tiles = jnp.sum(jnp.where(chosen, order, 0), axis=1)
    return slot, place, panel_tiles


def arrival_tables(slots, places, row_index, col_index, col_count, size):
    panel = (slots // CAP % col_count == 0) & (places % (2 * size) == 0)
    mine = (row_index * col_count + col_index) * CAP
    base = row_index * col_count * CAP

    def pick(hit, value):
        return jnp.sum(jnp.where(hit, value + 1, 0), axis=1) - 1

    main = [pick((slots == mine + s) & ~panel, places) for s in range(CAP)]
    part = [pick((slots == base + s) & panel, places // (2 * size)) for s in range(CAP)]
    return main, part


def pack_kernel(chunks, slot, panel_tiles, tiles, first, second, held, load_sem, main_sem, panel_sem):
    count = tiles.shape[0]
    step = count // chunks
    row_count, col_count = first.shape[:2]

    def load(i):
        part = pl.ds(i * step, step)
        return pltpu.make_async_copy(tiles.at[part], held.at[part], load_sem.at[i])

    for i in range(chunks):
        load(i).start()
    for i in range(chunks):
        load(i).wait()

        def send(k, carry):
            where = slot[k]
            owner = where // CAP

            @pl.when(where % CAP == 0)
            def _():
                pltpu.make_async_copy(
                    held.at[k],
                    first.at[owner // col_count, owner % col_count, pl.ds(CAP, held.shape[1])],
                    main_sem,
                ).start()

            @pl.when(where % CAP == 1)
            def _():
                pltpu.make_async_copy(held.at[k], second.at[owner], main_sem).start()

            return carry

        lax.fori_loop(i * step, (i + 1) * step, send, 0)
    for r in range(row_count):
        for s in range(CAP):
            pltpu.make_async_copy(
                held.at[panel_tiles[r * CAP + s]], first.at[r, :, s], panel_sem
            ).start()
    pltpu.make_async_copy(held, second, main_sem).wait()
    some = pl.ds(0, row_count * CAP)
    pltpu.make_async_copy(held.at[some], second.at[some], panel_sem).wait()


def pack(slot, panel_tiles, tiles, row_count, col_count):
    count, parts, rows, size = tiles.shape
    chunks = 8
    return pl.pallas_call(
        functools.partial(pack_kernel, chunks),
        out_shape=[
            jax.ShapeDtypeStruct((row_count, col_count, CAP + parts, rows, size), jnp.float32),
            jax.ShapeDtypeStruct((row_count * col_count, parts, rows, size), jnp.float32),
        ],
        in_specs=[
            pl.BlockSpec(memory_space=SMEM),
            pl.BlockSpec(memory_space=SMEM),
            pl.BlockSpec(memory_space=ANY),
        ],
        out_specs=[pl.BlockSpec(memory_space=ANY)] * 2,
        scratch_shapes=[
            VMEM(tiles.shape, jnp.float32),
            pltpu.SemaphoreType.DMA((chunks,)),
            pltpu.SemaphoreType.DMA,
            pltpu.SemaphoreType.DMA,
        ],
        compiler_params=LIMIT,
        name="pack",
    )(slot, panel_tiles, tiles)


def split_kernel(rows, front, *outs):
    col_count = len(outs)

    def block(a, carry):
        for q in range(col_count):
            start = (a * col_count + q) * rows * 2
            outs[q][a] = front[pl.ds(start, rows, stride=2), :]
        return carry

    lax.fori_loop(0, outs[0].shape[0], block, 0)


def split_front(front, row_blocks, col_count):
    size = front.shape[1]
    rows = size // col_count
    return pl.pallas_call(
        functools.partial(split_kernel, rows),
        out_shape=[jax.ShapeDtypeStruct((row_blocks, rows, size), jnp.float32)] * col_count,
        compiler_params=LIMIT,
        name="split_front",
    )(front)


def slices_kernel(col_count, where, part_0, part_1, arrived, *refs):
    own = refs[:col_count]
    windows, column, total, sem = refs[col_count:]
    col_index = where[1]
    for k in range(col_count):

        @pl.when(col_index == k)
        def _():
            copy = pltpu.make_async_copy(own[k], total, sem)
            copy.start()
            copy.wait()

    parts = (part_0, part_1)

    def source(d, carry):
        for s in range(CAP):
            block = parts[s][d]

            @pl.when(block >= 0)
            def _():
                total[block] += arrived[d, s]

        return carry

    lax.fori_loop(0, arrived.shape[0], source, 0, unroll=4)
    for k in range(col_count):
        column[k] = total[...]
    windows[...] = jnp.broadcast_to(total[0][None], windows.shape)


def sum_slices(where, parts, arrived, own, row_count, col_count):
    devices, _, rows, size = arrived.shape
    row_blocks = own[0].shape[0]
    outs = [
        jax.ShapeDtypeStruct((devices, rows, size), jnp.float32),
        jax.ShapeDtypeStruct((col_count, row_blocks, rows, size), jnp.float32),
    ]
    return pl.pallas_call(
        functools.partial(slices_kernel, col_count),
        out_shape=outs,
        grid=(1,),
        in_specs=[pl.BlockSpec(memory_space=SMEM)] * 3
        + [pl.BlockSpec((devices, CAP, rows, size), lambda i: (0, 0, 0, 0))]
        + [pl.BlockSpec(memory_space=ANY)] * col_count,
        out_specs=[
            pl.BlockSpec(outs[0].shape, lambda i: (0, 0, 0)),
            pl.BlockSpec(outs[1].shape, lambda i: (0, 0, 0, 0)),
        ],
        scratch_shapes=[
            VMEM((row_blocks, rows, size), jnp.float32),
            pltpu.SemaphoreType.DMA,
        ],
        compiler_params=LIMIT,
        name="sum_slices",
    )(where, *parts, arrived, *own)


def add_kernel(per_step, skip, places, base, tiles, out, sem):
    step = pl.program_id(0)

    @pl.when(step == 0)
    def _():
        copy = pltpu.make_async_copy(base, out, sem)
        copy.start()
        copy.wait()

    parts, rows, size = tiles.shape[1:]

    def add(j, carry):
        place = places[step * per_step + j]

        @pl.when(place >= 0)
        def _():
            tile = tiles[j, pl.ds(skip, parts - skip)].reshape(size, size)
            out[pl.ds(place, size, stride=2), :] += tile

        return carry

    lax.fori_loop(0, per_step, add, 0)


def add_tiles(places, base, tiles, skip):
    slots, parts, rows, size = tiles.shape
    per_step = 16
    return pl.pallas_call(
        functools.partial(add_kernel, per_step, skip),
        out_shape=jax.ShapeDtypeStruct(base.shape, jnp.float32),
        grid=(slots // per_step,),
        in_specs=[
            pl.BlockSpec(memory_space=SMEM),
            pl.BlockSpec(memory_space=ANY),
            pl.BlockSpec((per_step, parts, rows, size), lambda i: (i, 0, 0, 0)),
        ],
        out_specs=pl.BlockSpec(base.shape, lambda i: (0, 0)),
        scratch_shapes=[pltpu.SemaphoreType.DMA],
        compiler_params=LIMIT,
        name="add_tiles",
    )(places, base, tiles)


def update_kernel(row_count, where, front, inverse_t, window, column, base):
    row_index, col_index = where[0], where[1]
    size = inverse_t.shape[0]
    held = jnp.dot(
        window[...], inverse_t[...], precision=HIGH, preferred_element_type=jnp.float32
    )
    contract = (((1,), (1,)), ((), ()))

    def block(a, carry):
        rows = jnp.dot(
            column[:, a].reshape(size, size),
            inverse_t[...],
            precision=HIGH,
            preferred_element_type=jnp.float32,
        )
        update = lax.dot_general(
            rows, held, contract, precision=HIGH, preferred_element_type=jnp.float32
        )
        below = a * row_count + row_index > 0
        update = jnp.where(below, update, jnp.zeros_like(update))
        even = pl.ds(a * 2 * size, size, stride=2)
        odd = pl.ds(a * 2 * size + 1, size, stride=2)
        base[even, :] = jnp.where(col_index == 0, rows, front[even, :] - update[:, :size])
        base[odd, :] = front[odd, :] - update[:, size:]
        return carry

    lax.fori_loop(0, column.shape[1], block, 0)


def update_front(where, front, inverse_t, window, column, row_count):
    return pl.pallas_call(
        functools.partial(update_kernel, row_count),
        out_shape=jax.ShapeDtypeStruct(front.shape, jnp.float32),
        in_specs=[pl.BlockSpec(memory_space=SMEM)] + [pl.BlockSpec(memory_space=VMEM)] * 4,
        out_specs=pl.BlockSpec(memory_space=VMEM),
        compiler_params=LIMIT,
        name="update_front",
    )(where, front, inverse_t, window, column)


def after_kernel(value, other, out):
    pass


def after(value, other):
    return pl.pallas_call(
        after_kernel,
        out_shape=jax.ShapeDtypeStruct(value.shape, value.dtype),
        in_specs=[pl.BlockSpec(memory_space=ANY)] * 2,
        out_specs=pl.BlockSpec(memory_space=ANY),
        input_output_aliases={0: 0},
        name="after",
    )(value, other)


def per_device(front, child_tiles, child_rows, child_cols):
    row_count = lax.axis_size("row")
    col_count = lax.axis_size("col")
    row_index = lax.axis_index("row")
    col_index = lax.axis_index("col")
    both = ("row", "col")
    row_blocks, size, col_blocks = (front.shape[0], front.shape[2], front.shape[3])
    rows = size // col_count
    devices = row_count * col_count
    flat_front = front.reshape(row_blocks * size * col_blocks, size)
    tiles = child_tiles.reshape(-1, col_count, rows, size)
    where = jnp.stack([row_index, col_index]).astype(jnp.int32)

    own = split_front(flat_front, row_blocks, col_count)
    own = [own[0]] + [lax.ppermute(own[k], "col", [(0, k)]) for k in range(1, col_count)]
    slot, place, panel_tiles = send_tables(
        child_rows.reshape(-1), child_cols.reshape(-1), row_count, col_count, size
    )
    gathered = lax.all_gather(jnp.stack([slot, place])[None], both, axis=0, tiled=True)
    first, second = pack(slot, panel_tiles, tiles, row_count, col_count)
    first = first.reshape((devices,) + first.shape[2:])
    arrived = lax.all_to_all(first, both, split_axis=0, concat_axis=0, tiled=True)
    main, part = arrival_tables(
        gathered[:, 0], gathered[:, 1], row_index, col_index, col_count, size
    )
    windows, column = sum_slices(where, part, arrived, own, row_count, col_count)
    windows = lax.all_to_all(windows, both, split_axis=0, concat_axis=0, tiled=True)
    windows = windows.reshape(row_count, size, size)
    column = lax.all_to_all(column, "col", split_axis=0, concat_axis=0, tiled=True)
    second = lax.all_to_all(
        after(second, column), both, split_axis=0, concat_axis=0, tiled=True
    )
    corner = windows[0]
    window = jnp.concatenate(
        [
            lax.dynamic_index_in_dim(windows, m * col_count + col_index, axis=0, keepdims=False)
            for m in range(col_blocks)
        ],
        axis=0,
    )
    factor = jnp.linalg.cholesky(0.5 * (corner + corner.T))
    inverse = jax.scipy.linalg.solve_triangular(
        factor, jnp.eye(size, dtype=jnp.float32), lower=True
    )
    total = add_tiles(main[0], flat_front, arrived, CAP)
    base = update_front(where, total, inverse.T, window, column, row_count)
    return add_tiles(main[1], base, second, 0).reshape(front.shape)


def solution(mesh):
    in_specs = (
        P(None, "row", None, None, "col", None),
        P("row", "col", None, None, None),
        P("row", "col", None),
        P("row", "col", None),
    )
    out_specs = P(None, "row", None, None, "col", None)
    return jax.shard_map(
        per_device, mesh=mesh, in_specs=in_specs, out_specs=out_specs, check_vma=False
    )
```

time: 714 us -> 662 us (0.927)
  waiting for transfers between devices: 525 us -> 71.4 us
  blocking collectives: 0 us -> 450 us
  local copies, waits for them, and re-layouts: 77.5 us -> 1.04 us
  Pallas kernels: 0 us -> 75.9 us
  matrix products: 40.4 us -> 0.87 us
  between operations: 13.2 us -> 0.36 us
  starting transfers between devices: 22.2 us -> 33 us
    all_gather x0 -> x1, blocking collectives: none -> 421 us  [per_device(): lax.all_gather(jnp.stack([slot, place])[None], both, axis=0, tiled=True)]
    psum x2 -> x0, waiting for transfers between devices: 272 us -> none  [broadcast(): return lax.psum(kept, axis)]
    all_to_all x2 -> x3, waiting for transfers between devices: 210 us -> 58.2 us  [the longest x1 39.1 us: per_device(): lax.all_to_all(after(second, column), both, split_axis=0, concat_axis=0,...]
    pallas_call x0 -> x7, Pallas kernels: none -> 75.9 us  [the longest x1 31.2 us: update_front(): pl.pallas_call(functools.partial(update_kernel, row_count), out_shape=jax...]
    all_gather x1 -> x0, waiting for transfers between devices: 43.4 us -> none  [per_device(): lax.all_gather(panel_rows[:window_blocks][:, None], 'row', axis=1, tiled=...]
    dot_general x2 -> x0, matrix products: 32.6 us -> none  [the longest x1 22.8 us: per_device(): jnp.einsum('ams,spq->apmq', selector, arrived_tiles, precision=lax.Precis...]
    all_to_all x0 -> x1, blocking collectives: none -> 29.1 us  [per_device(): lax.all_to_all(column, 'col', split_axis=0, concat_axis=0, tiled=True)]
    scatter x2 -> x0, local copies, waits for them, and re-layouts: 24.4 us -> none  [the longest x1 23.4 us: per_device(): jnp.zeros((slot_total, tile_size, tile_size), jnp.float32).at[send_slot]]
  transfers between devices with their start and end apart: 5 -> 10, of which waited for: 4 -> 4; matrix products, arithmetic and copies ran while one was open for 7% -> 4% of each run, Pallas kernels for 0% -> 7%
where the time goes in v2:
time: 662 us; the launch traced here: 661 us
  blocking collectives  450 us (68%)
  Pallas kernels  75.9 us (11%)
  waiting for transfers between devices  71.4 us (11%)
  starting transfers between devices  33 us (5%)
  other arithmetic  28.4 us (4%)
    all_gather x1, blocking collectives, per_device(): lax.all_gather(jnp.stack([slot, place])[None], both, axis=0, tiled=True)  421 us
    all_to_all x1, waiting for transfers between devices, per_device(): lax.all_to_all(after(second, column), both, split_axis=0, concat_axis=0,...  39.1 us
    pallas_call x1, Pallas kernels, update_front(): pl.pallas_call(functools.partial(update_kernel, row_count), out_shape=jax...  31.2 us
    all_to_all x1, blocking collectives, per_device(): lax.all_to_all(column, 'col', split_axis=0, concat_axis=0, tiled=True)  29.1 us
    pallas_call x2, Pallas kernels, add_tiles(): pl.pallas_call(functools.partial(add_kernel, per_step, skip), out_shape=j...  24.9 us
    all_to_all x1, waiting for transfers between devices, per_device(): lax.all_to_all(windows, both, split_axis=0, concat_axis=0, tiled=True)  19.2 us
  transfers between devices with their start and end apart: 10, of which 4 were waited for; matrix products, arithmetic and copies ran while one was open for 4% of the time, Pallas kernels for 7%

profile of v2, /device:TPU:0, one launch (start us, length us, event | category | flops | bytes accessed | tf_op | source)
XLA Modules:
  0.0 661.4 jit_solution(2783439705531105473)
XLA Ops:
  2.2 7.8 %pack.1 = (f32[16,8,10,16,128]{4,3,2,1,0:T(8,128)}, f32[128,8,16,128]{3,2,1,0:T(8,128)}) custom-call(s32[128]{0:T(128)} %copy-done.7, s32[32]{0:T(128)} %select_reduce_fusion.5.panel_tiles, f32[128,8,16,128]{3,2,1,0:T(8,128)} %bitcast.78), custom_call_target="tpu_custom_call" | custom-call | tf_op jit(solution)/shard_map/pack/pallas_call | solution.py:93
  10.1 11.6 %all-to-all-start = ((f32[128,10,16,128]{3,2,1,0:T(8,128)}), f32[128,10,16,128]{3,2,1,0:T(8,128)}, u32[]{:S(2)}, u32[]{:S(2)}) async-start(f32[128,10,16,128]{3,2,1,0:T(8,128)} %bitcast.77), calls=%async_computation | async-start | bytes 20971520 | tf_op jit(solution)/shard_map/all_to_all | solution.py:315
  21.7 4.9 split_front.1
  26.6 2.9 collective-permute-start
  29.5 1.3 collective-permute-start.1
  30.9 1.3 collective-permute-start.2
  32.2 1.3 collective-permute-start.3
  33.5 1.3 collective-permute-start.4
  34.9 421.3 %all-gather.1 = s32[128,2,128]{2,1,0:T(2,128)S(1)} all-gather(s32[1,2,128]{2,1,0:T(2,128)S(1)} %add_bitcast_fusion), channel_id=2, replica_groups=mesh['row'=16,'col'=8] {'row','col'}, dimensions={0}, use_global_device_ids=true | all-gather | bytes 132096 | tf_op jit(solution)/shard_map/all_gather | solution.py:312
  456.4 1.3 collective-permute-start.5
  457.7 1.3 collective-permute-start.6
  460.5 2.7 collective-permute-done.5.refs_6_
  463.3 10.4 %collective-permute-done.6.refs_7_ = f32[48,16,128]{2,1,0:T(8,128)S(1)} collective-permute-done((f32[48,16,128]{2,1,0:T(8,128)}, f32[48,16,128]{2,1,0:T(8,128)S(1)}, u32[]{:S(2)}, u32[]{:S(2)}) %collective-permute-start.6) | collective-permute-done | bytes 393248 | tf_op jit(solution)/shard_map/ppermute | solution.py:308
  474.4 7.2 %sum_slices.1 = (f32[128,16,128]{2,1,0:T(8,128)}, f32[8,48,16,128]{3,2,1,0:T(8,128)}) custom-call(s32[2]{0:T(128)} %pad_add_fusion.where, s32[128]{0:T(128)} %get-tuple-element.40.part_0, s32[128]{0:T(128)} %get-tuple-element.39.part_1, f32[128,10,16,128]{3,2,1,0:T(8,128)} %all-to-all-done.tiles.arrived, f32[48,16,128]{2,1,0:T(8,128)} %get-tuple-element.18.refs_0_, ...), custom_call_target="tpu_custom_call" | custom-call | tf_op jit(solution)/shard_map/sum_slices/pallas_call | solution.py:176
  481.6 29.1 %all_to_all.20.column.other = f32[8,48,16,128]{3,2,1,0:T(8,128)} all-to-all(f32[8,48,16,128]{3,2,1,0:T(8,128)} %get-tuple-element.27), channel_id=1, replica_groups=mesh['row'=16,'col'=8] {'col'}, dimensions={0} | all-to-all | bytes 6291456 | tf_op jit(solution)/shard_map/all_to_all | solution.py:322
  510.7 4.6 all-to-all-start.1
  515.3 19.2 %all-to-all-done.1 = f32[128,16,128]{2,1,0:T(8,128)S(1)} async-done(((f32[128,16,128]{2,1,0:T(8,128)}), f32[128,16,128]{2,1,0:T(8,128)S(1)}, u32[]{:S(2)}, u32[]{:S(2)}) %all-to-all-start.1) | async-done | bytes 1048608 | tf_op jit(solution)/shard_map/all_to_all | solution.py:320
  534.5 5.9 all-to-all-start.3
  541.5 12.7 %add_tiles.2.front = f32[12288,128]{1,0:T(8,128)} custom-call(s32[128]{0:T(128)} %broadcast_add_fusion.2.places, f32[12288,128]{1,0:T(8,128)} %bitcast.76, f32[128,10,16,128]{3,2,1,0:T(8,128)} %all-to-all-done.tiles.arrived), custom_call_target="tpu_custom_call" | custom-call | tf_op jit(solution)/shard_map/add_tiles/pallas_call | solution.py:223
  554.5 11.7 %cholesky.14 = f32[128,128]{1,0:T(8,128)S(1)} custom-call(f32[128,128]{1,0:T(8,128)S(1)} %fusion.8), custom_call_target="Cholesky" | custom-call | tf_op jit(solution)/shard_map/jit(cholesky)/cholesky | solution.py:334
  567.6 9.8 %custom-call.7 = f32[1,128,128]{1,2,0:T(8,128)S(1)} custom-call(f32[1,128,128]{2,1,0:T(8,128)S(1)} %fusion), custom_call_target="InvertDiagBlocksLowerTriangular" | custom-call | tf_op jit(solution)/shard_map/jit(_solve_triangular)/triangular_solve | solution.py:335
  579.0 31.2 %update_front.1.base = f32[12288,128]{1,0:T(8,128)} custom-call(s32[2]{0:T(128)} %pad_add_fusion.where, f32[12288,128]{1,0:T(8,128)} %add_tiles.2.front, f32[128,128]{1,0:T(8,128)} %fusion.6.inverse_t, f32[256,128]{1,0:T(8,128)} %pad_maximum_fusion.window, f32[8,48,16,128]{3,2,1,0:T(8,128)} %all_to_all.20.column.other), custom_call_target="tpu_custom_call" | custom-call | tf_op jit(solution)/shard_map/update_front/pallas_call | solution.py:269
  610.1 39.1 %all-to-all-done.3.tiles = f32[128,8,16,128]{3,2,1,0:T(8,128)} async-done(((f32[128,8,16,128]{3,2,1,0:T(8,128)}), f32[128,8,16,128]{3,2,1,0:T(8,128)}, u32[]{:S(2)}, u32[]{:S(2)}) %all-to-all-start.3) | async-done | bytes 8388640 | tf_op jit(solution)/shard_map/all_to_all | solution.py:323
  649.2 12.2 %add_tiles.3 = f32[12288,128]{1,0:T(8,128)} custom-call(s32[128]{0:T(128)} %broadcast_add_fusion.3.places, f32[12288,128]{1,0:T(8,128)} %update_front.1.base, f32[128,8,16,128]{3,2,1,0:T(8,128)} %all-to-all-done.3.tiles), custom_call_target="tpu_custom_call" | custom-call | tf_op jit(solution)/shard_map/add_tiles/pallas_call | solution.py:223
  (52 shorter events, 8.8 us)
Async XLA Ops:
  1.5 0.7 copy-start.7
  10.0 24.8 %copy-start.8 = (s32[1,1,128]{2,1,0:T(1,128)S(1)}, s32[1,1,128]{2,1,0:T(1,128)}, u32[]{:S(2)}) copy-start(s32[1,1,128]{2,1,0:T(1,128)} %param.7) | copy-start | bytes 1540
  10.1 24.8 %copy-start.9 = (s32[1,1,128]{2,1,0:T(1,128)S(1)}, s32[1,1,128]{2,1,0:T(1,128)}, u32[]{:S(2)}) copy-start(s32[1,1,128]{2,1,0:T(1,128)} %param.6) | copy-start | bytes 1540
  10.1 463.6 %all-to-all-start = ((f32[128,10,16,128]{3,2,1,0:T(8,128)}), f32[128,10,16,128]{3,2,1,0:T(8,128)}, u32[]{:S(2)}, u32[]{:S(2)}) async-start(f32[128,10,16,128]{3,2,1,0:T(8,128)} %bitcast.77), calls=%async_computation | async-start | bytes 20971520 | tf_op jit(solution)/shard_map/all_to_all | solution.py:315
  26.6 429.7 %collective-permute-start = (f32[48,16,128]{2,1,0:T(8,128)}, f32[48,16,128]{2,1,0:T(8,128)S(1)}, u32[]{:S(2)}, u32[]{:S(2)}) collective-permute-start(f32[48,16,128]{2,1,0:T(8,128)} %get-tuple-element.19), channel_id=1, source_target_pairs={{0,1},{8,9},{16,17},{24,25},{32,33},{40,41},{48,49},{56,57},{64,65... | collective-permute-start | bytes 1179656 | tf_op jit(solution)/shard_map/ppermute | solution.py:308
  29.5 428.1 %collective-permute-start.1 = (f32[48,16,128]{2,1,0:T(8,128)}, f32[48,16,128]{2,1,0:T(8,128)S(1)}, u32[]{:S(2)}, u32[]{:S(2)}) collective-permute-start(f32[48,16,128]{2,1,0:T(8,128)} %get-tuple-element.20), channel_id=1, source_target_pairs={{0,2},{8,10},{16,18},{24,26},{32,34},{40,42},{48,50},{56,58},{64,6... | collective-permute-start | bytes 1179656 | tf_op jit(solution)/shard_map/ppermute | solution.py:308
  30.9 429.6 %collective-permute-start.2 = (f32[48,16,128]{2,1,0:T(8,128)}, f32[48,16,128]{2,1,0:T(8,128)S(1)}, u32[]{:S(2)}, u32[]{:S(2)}) collective-permute-start(f32[48,16,128]{2,1,0:T(8,128)} %get-tuple-element.21), channel_id=1, source_target_pairs={{0,3},{8,11},{16,19},{24,27},{32,35},{40,43},{48,51},{56,59},{64,6... | collective-permute-start | bytes 1179656 | tf_op jit(solution)/shard_map/ppermute | solution.py:308
  32.2 428.3 %collective-permute-start.3 = (f32[48,16,128]{2,1,0:T(8,128)}, f32[48,16,128]{2,1,0:T(8,128)S(1)}, u32[]{:S(2)}, u32[]{:S(2)}) collective-permute-start(f32[48,16,128]{2,1,0:T(8,128)} %get-tuple-element.22), channel_id=1, source_target_pairs={{0,4},{8,12},{16,20},{24,28},{32,36},{40,44},{48,52},{56,60},{64,6... | collective-permute-start | bytes 1179656 | tf_op jit(solution)/shard_map/ppermute | solution.py:308
  33.5 427.0 %collective-permute-start.4 = (f32[48,16,128]{2,1,0:T(8,128)}, f32[48,16,128]{2,1,0:T(8,128)S(1)}, u32[]{:S(2)}, u32[]{:S(2)}) collective-permute-start(f32[48,16,128]{2,1,0:T(8,128)} %get-tuple-element.23), channel_id=1, source_target_pairs={{0,5},{8,13},{16,21},{24,29},{32,37},{40,45},{48,53},{56,61},{64,6... | collective-permute-start | bytes 1179656 | tf_op jit(solution)/shard_map/ppermute | solution.py:308
  456.4 17.3 %copy-start = (f32[48,16,128]{2,1,0:T(8,128)}, f32[48,16,128]{2,1,0:T(8,128)S(1)}, u32[]{:S(2)}) copy-start(f32[48,16,128]{2,1,0:T(8,128)S(1)} %collective-permute-done.refs_1_) | copy-start | bytes 1179652
  456.4 6.9 %collective-permute-start.5 = (f32[48,16,128]{2,1,0:T(8,128)}, f32[48,16,128]{2,1,0:T(8,128)S(1)}, u32[]{:S(2)}, u32[]{:S(2)}) collective-permute-start(f32[48,16,128]{2,1,0:T(8,128)} %get-tuple-element.24), channel_id=1, source_target_pairs={{0,6},{8,14},{16,22},{24,30},{32,38},{40,46},{48,54},{56,62},{64,7... | collective-permute-start | bytes 1179656 | tf_op jit(solution)/shard_map/ppermute | solution.py:308
  457.7 15.9 %copy-start.1 = (f32[48,16,128]{2,1,0:T(8,128)}, f32[48,16,128]{2,1,0:T(8,128)S(1)}, u32[]{:S(2)}) copy-start(f32[48,16,128]{2,1,0:T(8,128)S(1)} %collective-permute-done.1.refs_2_) | copy-start | bytes 1179652
  457.7 15.9 %collective-permute-start.6 = (f32[48,16,128]{2,1,0:T(8,128)}, f32[48,16,128]{2,1,0:T(8,128)S(1)}, u32[]{:S(2)}, u32[]{:S(2)}) collective-permute-start(f32[48,16,128]{2,1,0:T(8,128)} %get-tuple-element.25), channel_id=1, source_target_pairs={{0,7},{8,15},{16,23},{24,31},{32,39},{40,47},{48,55},{56,63},{64,7... | collective-permute-start | bytes 1179656 | tf_op jit(solution)/shard_map/ppermute | solution.py:308
  460.5 13.2 %copy-start.2 = (f32[48,16,128]{2,1,0:T(8,128)}, f32[48,16,128]{2,1,0:T(8,128)S(1)}, u32[]{:S(2)}) copy-start(f32[48,16,128]{2,1,0:T(8,128)S(1)} %collective-permute-done.2.refs_3_) | copy-start | bytes 1179652
  460.5 13.2 %copy-start.3 = (f32[48,16,128]{2,1,0:T(8,128)}, f32[48,16,128]{2,1,0:T(8,128)S(1)}, u32[]{:S(2)}) copy-start(f32[48,16,128]{2,1,0:T(8,128)S(1)} %collective-permute-done.3.refs_4_) | copy-start | bytes 1179652
  460.5 13.2 %copy-start.4 = (f32[48,16,128]{2,1,0:T(8,128)}, f32[48,16,128]{2,1,0:T(8,128)S(1)}, u32[]{:S(2)}) copy-start(f32[48,16,128]{2,1,0:T(8,128)S(1)} %collective-permute-done.4.refs_5_) | copy-start | bytes 1179652
  463.3 10.4 %copy-start.5 = (f32[48,16,128]{2,1,0:T(8,128)}, f32[48,16,128]{2,1,0:T(8,128)S(1)}, u32[]{:S(2)}) copy-start(f32[48,16,128]{2,1,0:T(8,128)S(1)} %collective-permute-done.5.refs_6_) | copy-start | bytes 1179652
  473.6 0.7 copy-start.6
  510.7 23.8 %all-to-all-start.1 = ((f32[128,16,128]{2,1,0:T(8,128)}), f32[128,16,128]{2,1,0:T(8,128)S(1)}, u32[]{:S(2)}, u32[]{:S(2)}) async-start(f32[128,16,128]{2,1,0:T(8,128)} %get-tuple-element.26), calls=%async_computation.1 | async-start | bytes 2097152 | tf_op jit(solution)/shard_map/all_to_all | solution.py:320
  534.5 114.7 %all-to-all-start.3 = ((f32[128,8,16,128]{3,2,1,0:T(8,128)}), f32[128,8,16,128]{3,2,1,0:T(8,128)}, u32[]{:S(2)}, u32[]{:S(2)}) async-start(f32[128,8,16,128]{3,2,1,0:T(8,128)} %after.1), calls=%async_computation.3 | async-start | bytes 16777216 | tf_op jit(solution)/shard_map/all_to_all | solution.py:323

commit v3 on v2

--- a/solution.py
+++ b/solution.py
@@ -22,26 +22,19 @@
     owners = row_of * col_count + parent_cols % col_count
     same = (owners[:, None] == owners[None, :]) & (order[None, :] < order[:, None])
     slot = owners * CAP + jnp.sum(same.astype(jnp.int32), axis=1)
-    place = parent_rows // row_count * (2 * size) + parent_cols // col_count
+    block = parent_rows // row_count
+    place = block * (2 * size) + parent_cols // col_count
+    panel = parent_cols == 0
     wanted = jnp.arange(row_count * CAP, dtype=jnp.int32)[:, None]
-    chosen = (parent_cols == 0) & (
-        slot == wanted // CAP * (col_count * CAP) + wanted % CAP
-    )
+    chosen = panel & (slot == wanted // CAP * (col_count * CAP) + wanted % CAP)
     panel_tiles = jnp.sum(jnp.where(chosen, order, 0), axis=1)
-    return slot, place, panel_tiles
-
-
-def arrival_tables(slots, places, row_index, col_index, col_count, size):
-    panel = (slots // CAP % col_count == 0) & (places % (2 * size) == 0)
-    mine = (row_index * col_count + col_index) * CAP
-    base = row_index * col_count * CAP
-
-    def pick(hit, value):
-        return jnp.sum(jnp.where(hit, value + 1, 0), axis=1) - 1
-
-    main = [pick((slots == mine + s) & ~panel, places) for s in range(CAP)]
-    part = [pick((slots == base + s) & panel, places // (2 * size)) for s in range(CAP)]
-    return main, part
+    dest = jnp.arange(row_count * col_count, dtype=jnp.int32)[:, None, None]
+    part = jnp.arange(2 * CAP, dtype=jnp.int32)[None, :, None]
+    in_main = (part < CAP) & (slot == dest * CAP + part) & ~panel
+    first = dest // col_count * (col_count * CAP)
+    in_panel = (part >= CAP) & (slot == first + part - CAP) & panel
+    value = jnp.where(in_main, place + 1, 0) + jnp.where(in_panel, block + 1, 0)
+    return slot, panel_tiles, jnp.sum(value, axis=2) - 1
 
 
 def pack_kernel(chunks, slot, panel_tiles, tiles, first, second, held, load_sem, main_sem, panel_sem):
@@ -306,16 +299,14 @@
 
     own = split_front(flat_front, row_blocks, col_count)
     own = [own[0]] + [lax.ppermute(own[k], "col", [(0, k)]) for k in range(1, col_count)]
-    slot, place, panel_tiles = send_tables(
+    slot, panel_tiles, message = send_tables(
         child_rows.reshape(-1), child_cols.reshape(-1), row_count, col_count, size
     )
-    gathered = lax.all_gather(jnp.stack([slot, place])[None], both, axis=0, tiled=True)
+    message = lax.all_to_all(message, both, split_axis=0, concat_axis=0, tiled=True)
+    main, part = ([message[:, h * CAP + s] for s in range(CAP)] for h in range(2))
     first, second = pack(slot, panel_tiles, tiles, row_count, col_count)
     first = first.reshape((devices,) + first.shape[2:])
     arrived = lax.all_to_all(first, both, split_axis=0, concat_axis=0, tiled=True)
-    main, part = arrival_tables(
-        gathered[:, 0], gathered[:, 1], row_index, col_index, col_count, size
-    )
     windows, column = sum_slices(where, part, arrived, own, row_count, col_count)
     windows = lax.all_to_all(windows, both, split_axis=0, concat_axis=0, tiled=True)
     windows = windows.reshape(row_count, size, size)

time: 662 us -> 397 us (0.60)
  blocking collectives: 450 us -> 43 us
  waiting for transfers between devices: 71.4 us -> 198 us
  starting transfers between devices: 33 us -> 47.5 us
    all_gather x1 -> x0, blocking collectives: 421 us -> none  [per_device(): lax.all_gather(jnp.stack([slot, place])[None], both, axis=0, tiled=True)]
    ppermute x7, waiting for transfers between devices: 13.1 us -> 138 us  [per_device(): lax.ppermute(own[k], 'col', [(0, k)])]
    all_to_all x1, blocking collectives: 29.1 us -> 43 us  [per_device(): lax.all_to_all(column, 'col', split_axis=0, concat_axis=0, tiled=True)]
    all_to_all x0 -> x1, starting transfers between devices: none -> 11.1 us  [per_device(): lax.all_to_all(message, both, split_axis=0, concat_axis=0, tiled=True)]
  transfers between devices with their start and end apart: 10 -> 11, of which waited for: 4 -> 8; matrix products, arithmetic and copies ran while one was open for 4% -> 7% of each run, Pallas kernels for 7% -> 14%
where the time goes in v3:
time: 397 us; the launch traced here: 396 us
  waiting for transfers between devices  198 us (50%)
  Pallas kernels  75.9 us (19%)
  starting transfers between devices  47.5 us (12%)
  blocking collectives  43 us (11%)
  other arithmetic  28.1 us (7%)
    ppermute x7, waiting for transfers between devices, per_device(): lax.ppermute(own[k], 'col', [(0, k)])  138 us
    all_to_all x1, blocking collectives, per_device(): lax.all_to_all(column, 'col', split_axis=0, concat_axis=0, tiled=True)  43 us
    all_to_all x1, waiting for transfers between devices, per_device(): lax.all_to_all(after(second, column), both, split_axis=0, concat_axis=0,...  40.2 us
    pallas_call x1, Pallas kernels, update_front(): pl.pallas_call(functools.partial(update_kernel, row_count), out_shape=jax...  31.2 us
    pallas_call x2, Pallas kernels, add_tiles(): pl.pallas_call(functools.partial(add_kernel, per_step, skip), out_shape=j...  24.9 us
    all_to_all x1, waiting for transfers between devices, per_device(): lax.all_to_all(windows, both, split_axis=0, concat_axis=0, tiled=True)  19.2 us
    another operation x3, other arithmetic, per_device(): factor = jnp.linalg.cholesky(0.5 * (corner + corner.T))  12.4 us
    all_to_all x1, starting transfers between devices, per_device(): lax.all_to_all(message, both, split_axis=0, concat_axis=0, tiled=True)  11.1 us
  transfers between devices with their start and end apart: 11, of which 8 were waited for; matrix products, arithmetic and copies ran while one was open for 7% of the time, Pallas kernels for 14%

profile of v3, /device:TPU:0, one launch (start us, length us, event | category | flops | bytes accessed | tf_op | source)
XLA Modules:
  0.0 396.1 jit_solution(7687255827661939939)
XLA Ops:
  3.3 11.1 %all-to-all-start = ((s32[128,1,4]{2,1,0:T(1,128)}), s32[128,1,4]{2,1,0:T(1,128)S(1)}, u32[]{:S(2)}, u32[]{:S(2)}) async-start(s32[128,1,4]{2,1,0:T(1,128)} %copy.19), calls=%async_computation | async-start | bytes 131072 | tf_op jit(solution)/shard_map/all_to_all | solution.py:305
  15.9 7.8 %pack.1 = (f32[16,8,10,16,128]{4,3,2,1,0:T(8,128)}, f32[128,8,16,128]{3,2,1,0:T(8,128)}) custom-call(s32[128]{0:T(128)} %copy-done.7, s32[32]{0:T(128)} %select_reduce_fusion.1.panel_tiles, f32[128,8,16,128]{3,2,1,0:T(8,128)} %bitcast.78), custom_call_target="tpu_custom_call" | custom-call | tf_op jit(solution)/shard_map/pack/pallas_call | solution.py:86
  23.7 10.2 %all-to-all-start.1 = ((f32[128,10,16,128]{3,2,1,0:T(8,128)}), f32[128,10,16,128]{3,2,1,0:T(8,128)}, u32[]{:S(2)}, u32[]{:S(2)}) async-start(f32[128,10,16,128]{3,2,1,0:T(8,128)} %bitcast.77), calls=%async_computation.1 | async-start | bytes 20971520 | tf_op jit(solution)/shard_map/all_to_all | solution.py:309
  33.9 4.9 %split_front.1 = (f32[48,16,128]{2,1,0:T(8,128)}, f32[48,16,128]{2,1,0:T(8,128)}, f32[48,16,128]{2,1,0:T(8,128)}, f32[48,16,128]{2,1,0:T(8,128)}, f32[48,16,128]...) custom-call(f32[12288,128]{1,0:T(8,128)} %bitcast.75), custom_call_target="tpu_custom_call" | custom-call | tf_op jit(solution)/shard_map/split_front/pallas_call | solution.py:124
  38.8 2.9 collective-permute-start
  41.7 1.3 collective-permute-start.1
  44.4 1.3 collective-permute-start.3
  45.7 1.3 collective-permute-start.4
  47.1 110.0 %collective-permute-done.refs_1_ = f32[48,16,128]{2,1,0:T(8,128)S(1)} collective-permute-done((f32[48,16,128]{2,1,0:T(8,128)}, f32[48,16,128]{2,1,0:T(8,128)S(1)}, u32[]{:S(2)}, u32[]{:S(2)}) %collective-permute-start) | collective-permute-done | bytes 393248 | tf_op jit(solution)/shard_map/ppermute | solution.py:301
  158.3 7.1 %collective-permute-done.1.refs_2_ = f32[48,16,128]{2,1,0:T(8,128)S(1)} collective-permute-done((f32[48,16,128]{2,1,0:T(8,128)}, f32[48,16,128]{2,1,0:T(8,128)S(1)}, u32[]{:S(2)}, u32[]{:S(2)}) %collective-permute-start.1) | collective-permute-done | bytes 393248 | tf_op jit(solution)/shard_map/ppermute | solution.py:301
  168.2 5.6 %collective-permute-done.2.refs_3_ = f32[48,16,128]{2,1,0:T(8,128)S(1)} collective-permute-done((f32[48,16,128]{2,1,0:T(8,128)}, f32[48,16,128]{2,1,0:T(8,128)S(1)}, u32[]{:S(2)}, u32[]{:S(2)}) %collective-permute-start.2) | collective-permute-done | bytes 393248 | tf_op jit(solution)/shard_map/ppermute | solution.py:301
  173.8 8.4 %collective-permute-done.3.refs_4_ = f32[48,16,128]{2,1,0:T(8,128)S(1)} collective-permute-done((f32[48,16,128]{2,1,0:T(8,128)}, f32[48,16,128]{2,1,0:T(8,128)S(1)}, u32[]{:S(2)}, u32[]{:S(2)}) %collective-permute-start.3) | collective-permute-done | bytes 393248 | tf_op jit(solution)/shard_map/ppermute | solution.py:301
  182.3 7.2 %collective-permute-done.4.refs_5_ = f32[48,16,128]{2,1,0:T(8,128)S(1)} collective-permute-done((f32[48,16,128]{2,1,0:T(8,128)}, f32[48,16,128]{2,1,0:T(8,128)S(1)}, u32[]{:S(2)}, u32[]{:S(2)}) %collective-permute-start.4) | collective-permute-done | bytes 393248 | tf_op jit(solution)/shard_map/ppermute | solution.py:301
  190.5 7.2 %sum_slices.1 = (f32[128,16,128]{2,1,0:T(8,128)}, f32[8,48,16,128]{3,2,1,0:T(8,128)}) custom-call(s32[2]{0:T(128)} %pad_add_fusion.where, s32[128]{0:T(128)} %get-tuple-element.30.part_0, s32[128]{0:T(128)} %get-tuple-element.29.part_1, f32[128,10,16,128]{3,2,1,0:T(8,128)} %all-to-all-done.1.tiles.arrived, f32[48,16,128]{2,1,0:T(8,128)} %get-tuple-element.18.refs_0_, ...), custom_call_target="tpu_custom_call" | custom-call | tf_op jit(solution)/shard_map/sum_slices/pallas_call | solution.py:169
  197.7 43.0 %all_to_all.29.column.other = f32[8,48,16,128]{3,2,1,0:T(8,128)} all-to-all(f32[8,48,16,128]{3,2,1,0:T(8,128)} %get-tuple-element.27), channel_id=1, replica_groups=mesh['row'=16,'col'=8] {'col'}, dimensions={0} | all-to-all | bytes 6291456 | tf_op jit(solution)/shard_map/all_to_all | solution.py:313
  240.6 9.4 %all-to-all-start.2 = ((f32[128,16,128]{2,1,0:T(8,128)}), f32[128,16,128]{2,1,0:T(8,128)S(1)}, u32[]{:S(2)}, u32[]{:S(2)}) async-start(f32[128,16,128]{2,1,0:T(8,128)} %get-tuple-element.26), calls=%async_computation.2 | async-start | bytes 2097152 | tf_op jit(solution)/shard_map/all_to_all | solution.py:311
  250.1 19.2 %all-to-all-done.2 = f32[128,16,128]{2,1,0:T(8,128)S(1)} async-done(((f32[128,16,128]{2,1,0:T(8,128)}), f32[128,16,128]{2,1,0:T(8,128)S(1)}, u32[]{:S(2)}, u32[]{:S(2)}) %all-to-all-start.2) | async-done | bytes 1048608 | tf_op jit(solution)/shard_map/all_to_all | solution.py:311
  269.2 5.9 %all-to-all-start.4 = ((f32[128,8,16,128]{3,2,1,0:T(8,128)}), f32[128,8,16,128]{3,2,1,0:T(8,128)}, u32[]{:S(2)}, u32[]{:S(2)}) async-start(f32[128,8,16,128]{3,2,1,0:T(8,128)} %after.1), calls=%async_computation.4 | async-start | bytes 16777216 | tf_op jit(solution)/shard_map/all_to_all | solution.py:314
  275.2 12.7 %add_tiles.2.front = f32[12288,128]{1,0:T(8,128)} custom-call(s32[128]{0:T(128)} %get-tuple-element.31.places, f32[12288,128]{1,0:T(8,128)} %bitcast.76, f32[128,10,16,128]{3,2,1,0:T(8,128)} %all-to-all-done.1.tiles.arrived), custom_call_target="tpu_custom_call" | custom-call | tf_op jit(solution)/shard_map/add_tiles/pallas_call | solution.py:216
  288.2 11.7 %cholesky.14 = f32[128,128]{1,0:T(8,128)S(1)} custom-call(f32[128,128]{1,0:T(8,128)S(1)} %fusion.3), custom_call_target="Cholesky" | custom-call | tf_op jit(solution)/shard_map/jit(cholesky)/cholesky | solution.py:325
  301.2 9.8 %custom-call.7 = f32[1,128,128]{1,2,0:T(8,128)S(1)} custom-call(f32[1,128,128]{2,1,0:T(8,128)S(1)} %fusion), custom_call_target="InvertDiagBlocksLowerTriangular" | custom-call | tf_op jit(solution)/shard_map/jit(_solve_triangular)/triangular_solve | solution.py:326
  312.6 31.2 %update_front.1.base = f32[12288,128]{1,0:T(8,128)} custom-call(s32[2]{0:T(128)} %pad_add_fusion.where, f32[12288,128]{1,0:T(8,128)} %add_tiles.2.front, f32[128,128]{1,0:T(8,128)} %fusion.1.inverse_t, f32[256,128]{1,0:T(8,128)} %pad_maximum_fusion.window, f32[8,48,16,128]{3,2,1,0:T(8,128)} %all_to_all.29.column.other), custom_call_target="tpu_custom_call" | custom-call | tf_op jit(solution)/shard_map/update_front/pallas_call | solution.py:262
  343.8 40.2 %all-to-all-done.4.tiles = f32[128,8,16,128]{3,2,1,0:T(8,128)} async-done(((f32[128,8,16,128]{3,2,1,0:T(8,128)}), f32[128,8,16,128]{3,2,1,0:T(8,128)}, u32[]{:S(2)}, u32[]{:S(2)}) %all-to-all-start.4) | async-done | bytes 8388640 | tf_op jit(solution)/shard_map/all_to_all | solution.py:314
  384.0 12.2 %add_tiles.3 = f32[12288,128]{1,0:T(8,128)} custom-call(s32[128]{0:T(128)} %get-tuple-element.32.places, f32[12288,128]{1,0:T(8,128)} %update_front.1.base, f32[128,8,16,128]{3,2,1,0:T(8,128)} %all-to-all-done.4.tiles), custom_call_target="tpu_custom_call" | custom-call | tf_op jit(solution)/shard_map/add_tiles/pallas_call | solution.py:216
  (53 shorter events, 14.3 us)
Async XLA Ops:
  3.3 20.4 %all-to-all-start = ((s32[128,1,4]{2,1,0:T(1,128)}), s32[128,1,4]{2,1,0:T(1,128)S(1)}, u32[]{:S(2)}, u32[]{:S(2)}) async-start(s32[128,1,4]{2,1,0:T(1,128)} %copy.19), calls=%async_computation | async-start | bytes 131072 | tf_op jit(solution)/shard_map/all_to_all | solution.py:305
  14.5 1.4 copy-start.7
  23.7 165.8 %all-to-all-start.1 = ((f32[128,10,16,128]{3,2,1,0:T(8,128)}), f32[128,10,16,128]{3,2,1,0:T(8,128)}, u32[]{:S(2)}, u32[]{:S(2)}) async-start(f32[128,10,16,128]{3,2,1,0:T(8,128)} %bitcast.77), calls=%async_computation.1 | async-start | bytes 20971520 | tf_op jit(solution)/shard_map/all_to_all | solution.py:309
  38.8 118.2 %collective-permute-start = (f32[48,16,128]{2,1,0:T(8,128)}, f32[48,16,128]{2,1,0:T(8,128)S(1)}, u32[]{:S(2)}, u32[]{:S(2)}) collective-permute-start(f32[48,16,128]{2,1,0:T(8,128)} %get-tuple-element.19), channel_id=1, source_target_pairs={{0,1},{8,9},{16,17},{24,25},{32,33},{40,41},{48,49},{56,57},{64,65... | collective-permute-start | bytes 1179656 | tf_op jit(solution)/shard_map/ppermute | solution.py:301
  41.7 123.7 %collective-permute-start.1 = (f32[48,16,128]{2,1,0:T(8,128)}, f32[48,16,128]{2,1,0:T(8,128)S(1)}, u32[]{:S(2)}, u32[]{:S(2)}) collective-permute-start(f32[48,16,128]{2,1,0:T(8,128)} %get-tuple-element.20), channel_id=1, source_target_pairs={{0,2},{8,10},{16,18},{24,26},{32,34},{40,42},{48,50},{56,58},{64,6... | collective-permute-start | bytes 1179656 | tf_op jit(solution)/shard_map/ppermute | solution.py:301
  43.1 130.8 %collective-permute-start.2 = (f32[48,16,128]{2,1,0:T(8,128)}, f32[48,16,128]{2,1,0:T(8,128)S(1)}, u32[]{:S(2)}, u32[]{:S(2)}) collective-permute-start(f32[48,16,128]{2,1,0:T(8,128)} %get-tuple-element.21), channel_id=1, source_target_pairs={{0,3},{8,11},{16,19},{24,27},{32,35},{40,43},{48,51},{56,59},{64,6... | collective-permute-start | bytes 1179656 | tf_op jit(solution)/shard_map/ppermute | solution.py:301
  44.4 137.9 %collective-permute-start.3 = (f32[48,16,128]{2,1,0:T(8,128)}, f32[48,16,128]{2,1,0:T(8,128)S(1)}, u32[]{:S(2)}, u32[]{:S(2)}) collective-permute-start(f32[48,16,128]{2,1,0:T(8,128)} %get-tuple-element.22), channel_id=1, source_target_pairs={{0,4},{8,12},{16,20},{24,28},{32,36},{40,44},{48,52},{56,60},{64,6... | collective-permute-start | bytes 1179656 | tf_op jit(solution)/shard_map/ppermute | solution.py:301
  45.7 143.8 %collective-permute-start.4 = (f32[48,16,128]{2,1,0:T(8,128)}, f32[48,16,128]{2,1,0:T(8,128)S(1)}, u32[]{:S(2)}, u32[]{:S(2)}) collective-permute-start(f32[48,16,128]{2,1,0:T(8,128)} %get-tuple-element.23), channel_id=1, source_target_pairs={{0,5},{8,13},{16,21},{24,29},{32,37},{40,45},{48,53},{56,61},{64,6... | collective-permute-start | bytes 1179656 | tf_op jit(solution)/shard_map/ppermute | solution.py:301
  157.0 32.5 %copy-start = (f32[48,16,128]{2,1,0:T(8,128)}, f32[48,16,128]{2,1,0:T(8,128)S(1)}, u32[]{:S(2)}) copy-start(f32[48,16,128]{2,1,0:T(8,128)S(1)} %collective-permute-done.refs_1_) | copy-start | bytes 1179652
  157.0 32.4 %collective-permute-start.5 = (f32[48,16,128]{2,1,0:T(8,128)}, f32[48,16,128]{2,1,0:T(8,128)S(1)}, u32[]{:S(2)}, u32[]{:S(2)}) collective-permute-start(f32[48,16,128]{2,1,0:T(8,128)} %get-tuple-element.24), channel_id=1, source_target_pairs={{0,6},{8,14},{16,22},{24,30},{32,38},{40,46},{48,54},{56,62},{64,7... | collective-permute-start | bytes 1179656 | tf_op jit(solution)/shard_map/ppermute | solution.py:301
  165.4 24.1 %copy-start.1 = (f32[48,16,128]{2,1,0:T(8,128)}, f32[48,16,128]{2,1,0:T(8,128)S(1)}, u32[]{:S(2)}) copy-start(f32[48,16,128]{2,1,0:T(8,128)S(1)} %collective-permute-done.1.refs_2_) | copy-start | bytes 1179652
  165.4 24.1 %collective-permute-start.6 = (f32[48,16,128]{2,1,0:T(8,128)}, f32[48,16,128]{2,1,0:T(8,128)S(1)}, u32[]{:S(2)}, u32[]{:S(2)}) collective-permute-start(f32[48,16,128]{2,1,0:T(8,128)} %get-tuple-element.25), channel_id=1, source_target_pairs={{0,7},{8,15},{16,23},{24,31},{32,39},{40,47},{48,55},{56,63},{64,7... | collective-permute-start | bytes 1179656 | tf_op jit(solution)/shard_map/ppermute | solution.py:301
  173.8 15.7 %copy-start.2 = (f32[48,16,128]{2,1,0:T(8,128)}, f32[48,16,128]{2,1,0:T(8,128)S(1)}, u32[]{:S(2)}) copy-start(f32[48,16,128]{2,1,0:T(8,128)S(1)} %collective-permute-done.2.refs_3_) | copy-start | bytes 1179652
  182.3 7.3 %copy-start.3 = (f32[48,16,128]{2,1,0:T(8,128)}, f32[48,16,128]{2,1,0:T(8,128)S(1)}, u32[]{:S(2)}) copy-start(f32[48,16,128]{2,1,0:T(8,128)S(1)} %collective-permute-done.3.refs_4_) | copy-start | bytes 1179652
  189.5 0.8 copy-start.4
  189.5 0.9 copy-start.5
  189.5 1.0 copy-start.6
  240.6 28.6 %all-to-all-start.2 = ((f32[128,16,128]{2,1,0:T(8,128)}), f32[128,16,128]{2,1,0:T(8,128)S(1)}, u32[]{:S(2)}, u32[]{:S(2)}) async-start(f32[128,16,128]{2,1,0:T(8,128)} %get-tuple-element.26), calls=%async_computation.2 | async-start | bytes 2097152 | tf_op jit(solution)/shard_map/all_to_all | solution.py:311
  269.2 114.7 %all-to-all-start.4 = ((f32[128,8,16,128]{3,2,1,0:T(8,128)}), f32[128,8,16,128]{3,2,1,0:T(8,128)}, u32[]{:S(2)}, u32[]{:S(2)}) async-start(f32[128,8,16,128]{3,2,1,0:T(8,128)} %after.1), calls=%async_computation.4 | async-start | bytes 16777216 | tf_op jit(solution)/shard_map/all_to_all | solution.py:314

commit v4 on v3

--- a/solution.py
+++ b/solution.py
@@ -115,15 +115,20 @@
             outs[q][a] = front[pl.ds(start, rows, stride=2), :]
         return carry
 
-    lax.fori_loop(0, outs[0].shape[0], block, 0)
+    lax.fori_loop(0, outs[0].shape[0], block, 0, unroll=True)
 
 
 def split_front(front, row_blocks, col_count):
     size = front.shape[1]
     rows = size // col_count
+    steps = 6
     return pl.pallas_call(
         functools.partial(split_kernel, rows),
         out_shape=[jax.ShapeDtypeStruct((row_blocks, rows, size), jnp.float32)] * col_count,
+        grid=(steps,),
+        in_specs=[pl.BlockSpec((front.shape[0] // steps, size), lambda i: (i, 0))],
+        out_specs=[pl.BlockSpec((row_blocks // steps, rows, size), lambda i: (i, 0, 0))]
+        * col_count,
         compiler_params=LIMIT,
         name="split_front",
     )(front)
@@ -132,12 +137,14 @@
 def slices_kernel(col_count, where, part_0, part_1, arrived, *refs):
     own = refs[:col_count]
     windows, column, total, sem = refs[col_count:]
+    row_blocks = own[0].shape[0]
+    blocks = pl.ds(0, row_blocks)
     col_index = where[1]
     for k in range(col_count):
 
         @pl.when(col_index == k)
         def _():
-            copy = pltpu.make_async_copy(own[k], total, sem)
+            copy = pltpu.make_async_copy(own[k], total.at[blocks], sem)
             copy.start()
             copy.wait()
 
@@ -146,25 +153,21 @@
     def source(d, carry):
         for s in range(CAP):
             block = parts[s][d]
-
-            @pl.when(block >= 0)
-            def _():
-                total[block] += arrived[d, s]
-
+            total[jnp.where(block < 0, row_blocks, block)] += arrived[d, s]
         return carry
 
-    lax.fori_loop(0, arrived.shape[0], source, 0, unroll=4)
+    lax.fori_loop(0, arrived.shape[0], source, 0, unroll=8)
     for k in range(col_count):
-        column[k] = total[...]
+        column[k, blocks] = total[blocks]
     windows[...] = jnp.broadcast_to(total[0][None], windows.shape)
 
 
-def sum_slices(where, parts, arrived, own, row_count, col_count):
+def sum_slices(where, parts, arrived, own, row_count, col_count, extra):
     devices, _, rows, size = arrived.shape
     row_blocks = own[0].shape[0]
     outs = [
-        jax.ShapeDtypeStruct((devices, rows, size), jnp.float32),
-        jax.ShapeDtypeStruct((col_count, row_blocks, rows, size), jnp.float32),
+        jax.ShapeDtypeStruct((row_count, rows, size), jnp.float32),
+        jax.ShapeDtypeStruct((col_count, row_blocks + extra, rows, size), jnp.float32),
     ]
     return pl.pallas_call(
         functools.partial(slices_kernel, col_count),
@@ -178,7 +181,7 @@
             pl.BlockSpec(outs[1].shape, lambda i: (0, 0, 0, 0)),
         ],
         scratch_shapes=[
-            VMEM((row_blocks, rows, size), jnp.float32),
+            VMEM((row_blocks + 1, rows, size), jnp.float32),
             pltpu.SemaphoreType.DMA,
         ],
         compiler_params=LIMIT,
@@ -186,50 +189,92 @@
     )(where, *parts, arrived, *own)
 
 
-def add_kernel(per_step, skip, places, base, tiles, out, sem):
-    step = pl.program_id(0)
-
-    @pl.when(step == 0)
-    def _():
-        copy = pltpu.make_async_copy(base, out, sem)
+def windows_kernel(row_blocks, windows, column, out, sem):
+    col_count = column.shape[0]
+    copies = []
+    for k in range(col_count):
+        for i, j in enumerate((0, *range(k, windows.shape[0], col_count))):
+            copies.append(
+                pltpu.make_async_copy(
+                    windows.at[j], out.at[k, row_blocks + i], sem.at[len(copies)]
+                )
+            )
+    for copy in copies:
         copy.start()
+    for copy in copies:
         copy.wait()
 
-    parts, rows, size = tiles.shape[1:]
+
+def add_windows(windows, column, row_blocks):
+    count = column.shape[0] * (column.shape[1] - row_blocks)
+    return pl.pallas_call(
+        functools.partial(windows_kernel, row_blocks),
+        out_shape=jax.ShapeDtypeStruct(column.shape, column.dtype),
+        in_specs=[pl.BlockSpec(memory_space=VMEM), pl.BlockSpec(memory_space=ANY)],
+        out_specs=pl.BlockSpec(memory_space=ANY),
+        input_output_aliases={1: 0},
+        scratch_shapes=[pltpu.SemaphoreType.DMA((count,))],
+        compiler_params=LIMIT,
+        name="add_windows",
+    )(windows, column)
+
+
+def add_kernel(chunks, places, base, tiles, out, total, held, base_sem, tile_sem):
+    slots, parts, rows, size = held.shape
+    step = slots // chunks
+    last = base.shape[0]
+    whole = pl.ds(0, last)
+    load_base = pltpu.make_async_copy(base, total.at[whole], base_sem)
+    load_base.start()
+
+    def load(i):
+        some = pl.ds(i * step, step)
+        skip = pl.ds(tiles.shape[1] - parts, parts)
+        return pltpu.make_async_copy(tiles.at[some, skip], held.at[some], tile_sem.at[i])
+
+    for i in range(chunks):
+        load(i).start()
+    load_base.wait()
 
     def add(j, carry):
-        place = places[step * per_step + j]
-
-        @pl.when(place >= 0)
-        def _():
-            tile = tiles[j, pl.ds(skip, parts - skip)].reshape(size, size)
-            out[pl.ds(place, size, stride=2), :] += tile
-
+        place = places[j]
+        start = jnp.where(place < 0, last, place)
+        total[pl.ds(start, size, stride=2), :] += held[j].reshape(size, size)
         return carry
 
-    lax.fori_loop(0, per_step, add, 0)
+    for i in range(chunks):
+        load(i).wait()
+        lax.fori_loop(i * step, (i + 1) * step, add, 0, unroll=4)
+    store = pltpu.make_async_copy(total.at[whole], out, base_sem)
+    store.start()
+    store.wait()
 
 
 def add_tiles(places, base, tiles, skip):
     slots, parts, rows, size = tiles.shape
-    per_step = 16
-    return pl.pallas_call(
-        functools.partial(add_kernel, per_step, skip),
+    chunks = 8
+    return pl.pallas_call(
+        functools.partial(add_kernel, chunks),
         out_shape=jax.ShapeDtypeStruct(base.shape, jnp.float32),
-        grid=(slots // per_step,),
         in_specs=[
             pl.BlockSpec(memory_space=SMEM),
             pl.BlockSpec(memory_space=ANY),
-            pl.BlockSpec((per_step, parts, rows, size), lambda i: (i, 0, 0, 0)),
-        ],
-        out_specs=pl.BlockSpec(base.shape, lambda i: (0, 0)),
-        scratch_shapes=[pltpu.SemaphoreType.DMA],
+            pl.BlockSpec(memory_space=ANY),
+        ],
+        out_specs=pl.BlockSpec(memory_space=ANY),
+        scratch_shapes=[
+            VMEM((base.shape[0] + 2 * size, size), jnp.float32),
+            VMEM((slots, parts - skip, rows, size), jnp.float32),
+            pltpu.SemaphoreType.DMA,
+            pltpu.SemaphoreType.DMA((chunks,)),
+        ],
         compiler_params=LIMIT,
         name="add_tiles",
     )(places, base, tiles)
 
 
-def update_kernel(row_count, where, front, inverse_t, window, column, base):
+def update_kernel(shape, where, front, inverse_t, window, column, base):
+    row_count, row_blocks = shape
     row_index, col_index = where[0], where[1]
     size = inverse_t.shape[0]
     held = jnp.dot(
@@ -255,12 +300,12 @@
         base[odd, :] = front[odd, :] - update[:, size:]
         return carry
 
-    lax.fori_loop(0, column.shape[1], block, 0)
-
-
-def update_front(where, front, inverse_t, window, column, row_count):
-    return pl.pallas_call(
-        functools.partial(update_kernel, row_count),
+    lax.fori_loop(0, row_blocks, block, 0)
+
+
+def update_front(where, front, inverse_t, window, column, row_count, row_blocks):
+    return pl.pallas_call(
+        functools.partial(update_kernel, (row_count, row_blocks)),
         out_shape=jax.ShapeDtypeStruct(front.shape, jnp.float32),
         in_specs=[pl.BlockSpec(memory_space=SMEM)] + [pl.BlockSpec(memory_space=VMEM)] * 4,
         out_specs=pl.BlockSpec(memory_space=VMEM),
@@ -269,19 +314,19 @@
     )(where, front, inverse_t, window, column)
 
 
-def after_kernel(value, other, out):
+def after_kernel(*refs):
     pass
 
 
-def after(value, other):
+def after(value, *others):
     return pl.pallas_call(
         after_kernel,
         out_shape=jax.ShapeDtypeStruct(value.shape, value.dtype),
-        in_specs=[pl.BlockSpec(memory_space=ANY)] * 2,
+        in_specs=[pl.BlockSpec(memory_space=ANY)] * (1 + len(others)),
         out_specs=pl.BlockSpec(memory_space=ANY),
         input_output_aliases={0: 0},
         name="after",
-    )(value, other)
+    )(value, *others)
 
 
 def per_device(front, child_tiles, child_rows, child_cols):
@@ -306,28 +351,25 @@
     main, part = ([message[:, h * CAP + s] for s in range(CAP)] for h in range(2))
     first, second = pack(slot, panel_tiles, tiles, row_count, col_count)
     first = first.reshape((devices,) + first.shape[2:])
+    first = after(first, *own[1:])
     arrived = lax.all_to_all(first, both, split_axis=0, concat_axis=0, tiled=True)
-    windows, column = sum_slices(where, part, arrived, own, row_count, col_count)
-    windows = lax.all_to_all(windows, both, split_axis=0, concat_axis=0, tiled=True)
-    windows = windows.reshape(row_count, size, size)
+    windows, column = sum_slices(
+        where, part, arrived, own, row_count, col_count, 1 + col_blocks
+    )
+    windows = lax.all_to_all(windows, "row", split_axis=0, concat_axis=0, tiled=True)
+    column = add_windows(windows, column, row_blocks)
     column = lax.all_to_all(column, "col", split_axis=0, concat_axis=0, tiled=True)
     second = lax.all_to_all(
         after(second, column), both, split_axis=0, concat_axis=0, tiled=True
     )
-    corner = windows[0]
-    window = jnp.concatenate(
-        [
-            lax.dynamic_index_in_dim(windows, m * col_count + col_index, axis=0, keepdims=False)
-            for m in range(col_blocks)
-        ],
-        axis=0,
-    )
+    corner = column[:, row_blocks].reshape(size, size)
+    window = jnp.swapaxes(column[:, row_blocks + 1 :], 0, 1).reshape(-1, size)
     factor = jnp.linalg.cholesky(0.5 * (corner + corner.T))
     inverse = jax.scipy.linalg.solve_triangular(
         factor, jnp.eye(size, dtype=jnp.float32), lower=True
     )
     total = add_tiles(main[0], flat_front, arrived, CAP)
-    base = update_front(where, total, inverse.T, window, column, row_count)
+    base = update_front(where, total, inverse.T, window, column, row_count, row_blocks)
     return add_tiles(main[1], base, second, 0).reshape(front.shape)
 
 

time: 397 us -> 386 us (0.972)
  waiting for transfers between devices: 198 us -> 180 us
  blocking collectives: 43 us -> 60.4 us
  starting transfers between devices: 47.5 us -> 41.1 us
    all_to_all x1, waiting for transfers between devices: 0.01 us -> 135 us  [per_device(): lax.all_to_all(first, both, split_axis=0, concat_axis=0, tiled=True)]
    ppermute x7, waiting for transfers between devices: 138 us -> 6.88 us  [per_device(): lax.ppermute(own[k], 'col', [(0, k)])]
    all_to_all x1 -> x0, waiting for transfers between devices: 19.2 us -> none  [per_device(): lax.all_to_all(windows, both, split_axis=0, concat_axis=0, tiled=True)]
    all_to_all x0 -> x1, blocking collectives: none -> 12.5 us  [per_device(): lax.all_to_all(windows, 'row', split_axis=0, concat_axis=0, tiled=True)]
    all_to_all x1 -> x0, starting transfers between devices: 9.43 us -> none  [per_device(): lax.all_to_all(windows, both, split_axis=0, concat_axis=0, tiled=True)]
    all_to_all x1, blocking collectives: 43 us -> 47.9 us  [per_device(): lax.all_to_all(column, 'col', split_axis=0, concat_axis=0, tiled=True)]
    ppermute x7, starting transfers between devices: 10.8 us -> 15.3 us  [per_device(): lax.ppermute(own[k], 'col', [(0, k)])]
    pallas_call x3 -> x4, Pallas kernels: 56.1 us -> 52.5 us  [the longest x1 31.2 us: update_front(): pl.pallas_call(functools.partial(update_kernel, (row_count, row_blocks)),...]
  transfers between devices with their start and end apart: 11 -> 10, of which waited for: 8 -> 4; matrix products, arithmetic and copies ran while one was open for 7% -> 8% of each run, Pallas kernels for 14% -> 13%
where the time goes in v4:
time: 386 us; the launch traced here: 385 us
  waiting for transfers between devices  180 us (47%)
  Pallas kernels  72.2 us (19%)
  blocking collectives  60.4 us (16%)
  starting transfers between devices  41.1 us (11%)
  other arithmetic  24.7 us (6%)
  local copies, waits for them, and re-layouts  4.92 us (1%)
    all_to_all x1, waiting for transfers between devices, per_device(): lax.all_to_all(first, both, split_axis=0, concat_axis=0, tiled=True)  135 us
    all_to_all x1, blocking collectives, per_device(): lax.all_to_all(column, 'col', split_axis=0, concat_axis=0, tiled=True)  47.9 us
    all_to_all x1, waiting for transfers between devices, per_device(): lax.all_to_all(after(second, column), both, split_axis=0, concat_axis=0,...  38.6 us
    pallas_call x1, Pallas kernels, update_front(): pl.pallas_call(functools.partial(update_kernel, (row_count, row_blocks)),...  31.2 us
    pallas_call x2, Pallas kernels, add_tiles(): pl.pallas_call(functools.partial(add_kernel, chunks), out_shape=jax.Shape...  19.5 us
    ppermute x7, starting transfers between devices, per_device(): lax.ppermute(own[k], 'col', [(0, k)])  15.3 us
    all_to_all x1, blocking collectives, per_device(): lax.all_to_all(windows, 'row', split_axis=0, concat_axis=0, tiled=True)  12.5 us
    another operation x3, other arithmetic, per_device(): factor = jnp.linalg.cholesky(0.5 * (corner + corner.T))  12.4 us
  transfers between devices with their start and end apart: 10, of which 4 were waited for; matrix products, arithmetic and copies ran while one was open for 8% of the time, Pallas kernels for 13%

profile of v4, /device:TPU:0, one launch (start us, length us, event | category | flops | bytes accessed | tf_op | source)
XLA Modules:
  0.0 385.1 jit_solution(12722072323989639670)
XLA Ops:
  0.0 5.9 %split_front.1 = (f32[48,16,128]{2,1,0:T(8,128)}, f32[48,16,128]{2,1,0:T(8,128)}, f32[48,16,128]{2,1,0:T(8,128)}, f32[48,16,128]{2,1,0:T(8,128)}, f32[48,16,128]...) custom-call(f32[12288,128]{1,0:T(8,128)} %bitcast.74), custom_call_target="tpu_custom_call" | custom-call | tf_op jit(solution)/shard_map/split_front/pallas_call | solution.py:125
  5.9 3.9 %collective-permute-start = (f32[48,16,128]{2,1,0:T(8,128)}, f32[48,16,128]{2,1,0:T(8,128)S(1)}, u32[]{:S(2)}, u32[]{:S(2)}) collective-permute-start(f32[48,16,128]{2,1,0:T(8,128)} %get-tuple-element.18), channel_id=1, source_target_pairs={{0,1},{8,9},{16,17},{24,25},{32,33},{40,41},{48,49},{56,57},{64,65... | collective-permute-start | bytes 1179656 | tf_op jit(solution)/shard_map/ppermute | solution.py:346
  9.8 1.3 collective-permute-start.1
  11.1 1.3 collective-permute-start.2
  12.4 1.3 collective-permute-start.3
  13.8 1.4 collective-permute-start.4
  16.6 8.0 %all-to-all-start = ((s32[128,1,4]{2,1,0:T(1,128)}), s32[128,1,4]{2,1,0:T(1,128)S(1)}, u32[]{:S(2)}, u32[]{:S(2)}) async-start(s32[128,1,4]{2,1,0:T(1,128)} %copy.23), calls=%async_computation | async-start | bytes 131072 | tf_op jit(solution)/shard_map/all_to_all | solution.py:350
  24.6 4.2 %collective-permute-start.5 = (f32[48,16,128]{2,1,0:T(8,128)}, f32[48,16,128]{2,1,0:T(8,128)S(1)}, u32[]{:S(2)}, u32[]{:S(2)}) collective-permute-start(f32[48,16,128]{2,1,0:T(8,128)} %get-tuple-element.23), channel_id=1, source_target_pairs={{0,6},{8,14},{16,22},{24,30},{32,38},{40,46},{48,54},{56,62},{64,7... | collective-permute-start | bytes 1179656 | tf_op jit(solution)/shard_map/ppermute | solution.py:346
  28.8 1.9 collective-permute-start.6
  31.4 7.9 %pack.1 = (f32[16,8,10,16,128]{4,3,2,1,0:T(8,128)}, f32[128,8,16,128]{3,2,1,0:T(8,128)}) custom-call(s32[128]{0:T(128)} %copy-done.7, s32[32]{0:T(128)} %select_reduce_fusion.1.panel_tiles, f32[128,8,16,128]{3,2,1,0:T(8,128)} %bitcast.76), custom_call_target="tpu_custom_call" | custom-call | tf_op jit(solution)/shard_map/pack/pallas_call | solution.py:86
  39.3 6.4 %collective-permute-done.4.refs_5_ = f32[48,16,128]{2,1,0:T(8,128)S(1)} collective-permute-done((f32[48,16,128]{2,1,0:T(8,128)}, f32[48,16,128]{2,1,0:T(8,128)S(1)}, u32[]{:S(2)}, u32[]{:S(2)}) %collective-permute-start.4) | collective-permute-done | bytes 393248 | tf_op jit(solution)/shard_map/ppermute | solution.py:346
  46.9 11.7 %all-to-all-start.1 = ((f32[128,10,16,128]{3,2,1,0:T(8,128)}), f32[128,10,16,128]{3,2,1,0:T(8,128)}, u32[]{:S(2)}, u32[]{:S(2)}) async-start(f32[128,10,16,128]{3,2,1,0:T(8,128)} %after.2), calls=%async_computation.1 | async-start | bytes 20971520 | tf_op jit(solution)/shard_map/all_to_all | solution.py:355
  60.0 134.9 %all-to-all-done.1.tiles.arrived = f32[128,10,16,128]{3,2,1,0:T(8,128)} async-done(((f32[128,10,16,128]{3,2,1,0:T(8,128)}), f32[128,10,16,128]{3,2,1,0:T(8,128)}, u32[]{:S(2)}, u32[]{:S(2)}) %all-to-all-start.1) | async-done | bytes 10485792 | tf_op jit(solution)/shard_map/all_to_all | solution.py:355
  195.0 5.9 %sum_slices.1 = (f32[16,16,128]{2,1,0:T(8,128)}, f32[8,51,16,128]{3,2,1,0:T(8,128)}) custom-call(s32[2]{0:T(128)} %pad_add_fusion.where, s32[128]{0:T(128)} %get-tuple-element.30.part_0, s32[128]{0:T(128)} %get-tuple-element.29.part_1, f32[128,10,16,128]{3,2,1,0:T(8,128)} %all-to-all-done.1.tiles.arrived, f32[48,16,128]{2,1,0:T(8,128)} %get-tuple-element.25.refs_0_, ...), custom_call_target="tpu_custom_call" | custom-call | tf_op jit(solution)/shard_map/sum_slices/pallas_call | solution.py:172
  200.9 12.5 %all_to_all.29.windows = f32[16,16,128]{2,1,0:T(8,128)} all-to-all(f32[16,16,128]{2,1,0:T(8,128)} %get-tuple-element.26), channel_id=1, replica_groups=mesh['row'=16,'col'=8] {'row'}, dimensions={0} | all-to-all | bytes 262144 | tf_op jit(solution)/shard_map/all_to_all | solution.py:359
  213.4 1.8 add_windows.1
  215.2 47.9 %all_to_all.30.column.refs_1_ = f32[8,51,16,128]{3,2,1,0:T(8,128)} all-to-all(f32[8,51,16,128]{3,2,1,0:T(8,128)} %add_windows.1), channel_id=1, replica_groups=mesh['row'=16,'col'=8] {'col'}, dimensions={0} | all-to-all | bytes 6684672 | tf_op jit(solution)/shard_map/all_to_all | solution.py:361
  263.1 6.1 %all-to-all-start.4 = ((f32[128,8,16,128]{3,2,1,0:T(8,128)}), f32[128,8,16,128]{3,2,1,0:T(8,128)}, u32[]{:S(2)}, u32[]{:S(2)}) async-start(f32[128,8,16,128]{3,2,1,0:T(8,128)} %after.3), calls=%async_computation.4 | async-start | bytes 16777216 | tf_op jit(solution)/shard_map/all_to_all | solution.py:362
  269.2 9.7 %add_tiles.2.front = f32[12288,128]{1,0:T(8,128)} custom-call(s32[128]{0:T(128)} %get-tuple-element.31.places, f32[12288,128]{1,0:T(8,128)} %bitcast.75, f32[128,10,16,128]{3,2,1,0:T(8,128)} %all-to-all-done.1.tiles.arrived), custom_call_target="tpu_custom_call" | custom-call | tf_op jit(solution)/shard_map/add_tiles/pallas_call | solution.py:256
  280.0 11.7 %cholesky.14 = f32[128,128]{1,0:T(8,128)S(1)} custom-call(f32[128,128]{1,0:T(8,128)S(1)} %fusion.3), custom_call_target="Cholesky" | custom-call | tf_op jit(solution)/shard_map/jit(cholesky)/cholesky | solution.py:367
  293.1 9.8 %custom-call.7 = f32[1,128,128]{1,2,0:T(8,128)S(1)} custom-call(f32[1,128,128]{2,1,0:T(8,128)S(1)} %fusion), custom_call_target="InvertDiagBlocksLowerTriangular" | custom-call | tf_op jit(solution)/shard_map/jit(_solve_triangular)/triangular_solve | solution.py:368
  305.4 31.2 %update_front.1.base = f32[12288,128]{1,0:T(8,128)} custom-call(s32[2]{0:T(128)} %pad_add_fusion.where, f32[12288,128]{1,0:T(8,128)} %add_tiles.2.front, f32[128,128]{1,0:T(8,128)} %fusion.1.inverse_t, f32[256,128]{1,0:T(8,128)} %bitcast.79, f32[8,51,16,128]{3,2,1,0:T(8,128)} %all_to_all.30.column.refs_1_), custom_call_target="tpu_custom_call" | custom-call | tf_op jit(solution)/shard_map/update_front/pallas_call | solution.py:307
  336.6 38.6 %all-to-all-done.4.tiles = f32[128,8,16,128]{3,2,1,0:T(8,128)} async-done(((f32[128,8,16,128]{3,2,1,0:T(8,128)}), f32[128,8,16,128]{3,2,1,0:T(8,128)}, u32[]{:S(2)}, u32[]{:S(2)}) %all-to-all-start.4) | async-done | bytes 8388640 | tf_op jit(solution)/shard_map/all_to_all | solution.py:362
  375.2 9.7 %add_tiles.3 = f32[12288,128]{1,0:T(8,128)} custom-call(s32[128]{0:T(128)} %get-tuple-element.32.places, f32[12288,128]{1,0:T(8,128)} %update_front.1.base, f32[128,8,16,128]{3,2,1,0:T(8,128)} %all-to-all-done.4.tiles), custom_call_target="tpu_custom_call" | custom-call | tf_op jit(solution)/shard_map/add_tiles/pallas_call | solution.py:256
  (57 shorter events, 9.5 us)
Async XLA Ops:
  0.0 15.2 %copy-start.9 = (s32[1,1,128]{2,1,0:T(1,128)S(1)}, s32[1,1,128]{2,1,0:T(1,128)}, u32[]{:S(2)}) copy-start(s32[1,1,128]{2,1,0:T(1,128)} %param.7) | copy-start | bytes 1540
  0.0 15.2 %copy-start.8 = (s32[1,1,128]{2,1,0:T(1,128)S(1)}, s32[1,1,128]{2,1,0:T(1,128)}, u32[]{:S(2)}) copy-start(s32[1,1,128]{2,1,0:T(1,128)} %param.6) | copy-start | bytes 1540
  5.9 18.7 %collective-permute-start = (f32[48,16,128]{2,1,0:T(8,128)}, f32[48,16,128]{2,1,0:T(8,128)S(1)}, u32[]{:S(2)}, u32[]{:S(2)}) collective-permute-start(f32[48,16,128]{2,1,0:T(8,128)} %get-tuple-element.18), channel_id=1, source_target_pairs={{0,1},{8,9},{16,17},{24,25},{32,33},{40,41},{48,49},{56,57},{64,65... | collective-permute-start | bytes 1179656 | tf_op jit(solution)/shard_map/ppermute | solution.py:346
  9.8 19.0 %collective-permute-start.1 = (f32[48,16,128]{2,1,0:T(8,128)}, f32[48,16,128]{2,1,0:T(8,128)S(1)}, u32[]{:S(2)}, u32[]{:S(2)}) collective-permute-start(f32[48,16,128]{2,1,0:T(8,128)} %get-tuple-element.19), channel_id=1, source_target_pairs={{0,2},{8,10},{16,18},{24,26},{32,34},{40,42},{48,50},{56,58},{64,6... | collective-permute-start | bytes 1179656 | tf_op jit(solution)/shard_map/ppermute | solution.py:346
  11.1 28.1 %collective-permute-start.2 = (f32[48,16,128]{2,1,0:T(8,128)}, f32[48,16,128]{2,1,0:T(8,128)S(1)}, u32[]{:S(2)}, u32[]{:S(2)}) collective-permute-start(f32[48,16,128]{2,1,0:T(8,128)} %get-tuple-element.20), channel_id=1, source_target_pairs={{0,3},{8,11},{16,19},{24,27},{32,35},{40,43},{48,51},{56,59},{64,6... | collective-permute-start | bytes 1179656 | tf_op jit(solution)/shard_map/ppermute | solution.py:346
  12.4 26.8 %collective-permute-start.3 = (f32[48,16,128]{2,1,0:T(8,128)}, f32[48,16,128]{2,1,0:T(8,128)S(1)}, u32[]{:S(2)}, u32[]{:S(2)}) collective-permute-start(f32[48,16,128]{2,1,0:T(8,128)} %get-tuple-element.21), channel_id=1, source_target_pairs={{0,4},{8,12},{16,20},{24,28},{32,36},{40,44},{48,52},{56,60},{64,6... | collective-permute-start | bytes 1179656 | tf_op jit(solution)/shard_map/ppermute | solution.py:346
  13.8 31.9 %collective-permute-start.4 = (f32[48,16,128]{2,1,0:T(8,128)}, f32[48,16,128]{2,1,0:T(8,128)S(1)}, u32[]{:S(2)}, u32[]{:S(2)}) collective-permute-start(f32[48,16,128]{2,1,0:T(8,128)} %get-tuple-element.22), channel_id=1, source_target_pairs={{0,5},{8,13},{16,21},{24,29},{32,37},{40,45},{48,53},{56,61},{64,6... | collective-permute-start | bytes 1179656 | tf_op jit(solution)/shard_map/ppermute | solution.py:346
  15.5 15.9 %copy-start.7 = (s32[128]{0:T(128)}, s32[128]{0:T(128)S(1)}, u32[]{:S(2)}) copy-start(s32[128]{0:T(128)S(1)} %get-tuple-element.38.slot) | copy-start | bytes 1540
  16.6 30.3 %all-to-all-start = ((s32[128,1,4]{2,1,0:T(1,128)}), s32[128,1,4]{2,1,0:T(1,128)S(1)}, u32[]{:S(2)}, u32[]{:S(2)}) async-start(s32[128,1,4]{2,1,0:T(1,128)} %copy.23), calls=%async_computation | async-start | bytes 131072 | tf_op jit(solution)/shard_map/all_to_all | solution.py:350
  24.6 21.6 %copy-start = (f32[48,16,128]{2,1,0:T(8,128)}, f32[48,16,128]{2,1,0:T(8,128)S(1)}, u32[]{:S(2)}) copy-start(f32[48,16,128]{2,1,0:T(8,128)S(1)} %collective-permute-done.refs_1_) | copy-start | bytes 1179652
  24.6 21.1 %collective-permute-start.5 = (f32[48,16,128]{2,1,0:T(8,128)}, f32[48,16,128]{2,1,0:T(8,128)S(1)}, u32[]{:S(2)}, u32[]{:S(2)}) collective-permute-start(f32[48,16,128]{2,1,0:T(8,128)} %get-tuple-element.23), channel_id=1, source_target_pairs={{0,6},{8,14},{16,22},{24,30},{32,38},{40,46},{48,54},{56,62},{64,7... | collective-permute-start | bytes 1179656 | tf_op jit(solution)/shard_map/ppermute | solution.py:346
  28.8 17.4 %copy-start.1 = (f32[48,16,128]{2,1,0:T(8,128)}, f32[48,16,128]{2,1,0:T(8,128)S(1)}, u32[]{:S(2)}) copy-start(f32[48,16,128]{2,1,0:T(8,128)S(1)} %collective-permute-done.1.refs_2_) | copy-start | bytes 1179652
  28.8 17.4 %collective-permute-start.6 = (f32[48,16,128]{2,1,0:T(8,128)}, f32[48,16,128]{2,1,0:T(8,128)S(1)}, u32[]{:S(2)}, u32[]{:S(2)}) collective-permute-start(f32[48,16,128]{2,1,0:T(8,128)} %get-tuple-element.24), channel_id=1, source_target_pairs={{0,7},{8,15},{16,23},{24,31},{32,39},{40,47},{48,55},{56,63},{64,7... | collective-permute-start | bytes 1179656 | tf_op jit(solution)/shard_map/ppermute | solution.py:346
  39.2 6.9 %copy-start.2 = (f32[48,16,128]{2,1,0:T(8,128)}, f32[48,16,128]{2,1,0:T(8,128)S(1)}, u32[]{:S(2)}) copy-start(f32[48,16,128]{2,1,0:T(8,128)S(1)} %collective-permute-done.2.refs_3_) | copy-start | bytes 1179652
  39.3 6.9 %copy-start.3 = (f32[48,16,128]{2,1,0:T(8,128)}, f32[48,16,128]{2,1,0:T(8,128)S(1)}, u32[]{:S(2)}) copy-start(f32[48,16,128]{2,1,0:T(8,128)S(1)} %collective-permute-done.3.refs_4_) | copy-start | bytes 1179652
  45.7 0.8 copy-start.4
  45.7 0.9 copy-start.5
  46.2 0.7 copy-start.6
  46.9 148.1 %all-to-all-start.1 = ((f32[128,10,16,128]{3,2,1,0:T(8,128)}), f32[128,10,16,128]{3,2,1,0:T(8,128)}, u32[]{:S(2)}, u32[]{:S(2)}) async-start(f32[128,10,16,128]{3,2,1,0:T(8,128)} %after.2), calls=%async_computation.1 | async-start | bytes 20971520 | tf_op jit(solution)/shard_map/all_to_all | solution.py:355
  263.1 112.1 %all-to-all-start.4 = ((f32[128,8,16,128]{3,2,1,0:T(8,128)}), f32[128,8,16,128]{3,2,1,0:T(8,128)}, u32[]{:S(2)}, u32[]{:S(2)}) async-start(f32[128,8,16,128]{3,2,1,0:T(8,128)} %after.3), calls=%async_computation.4 | async-start | bytes 16777216 | tf_op jit(solution)/shard_map/all_to_all | solution.py:362

commit v5 on v4

--- a/solution.py
+++ b/solution.py
@@ -15,7 +15,7 @@
 LIMIT = pltpu.CompilerParams(vmem_limit_bytes=58 << 20)
 
 
-def send_tables(parent_rows, parent_cols, row_count, col_count, size):
+def send_tables(parent_rows, parent_cols, row_index, col_index, row_count, col_count, size):
     tiles = parent_rows.shape[0]
     order = jnp.arange(tiles, dtype=jnp.int32)
     row_of = parent_rows % row_count
@@ -31,23 +31,35 @@
     dest = jnp.arange(row_count * col_count, dtype=jnp.int32)[:, None, None]
     part = jnp.arange(2 * CAP, dtype=jnp.int32)[None, :, None]
     in_main = (part < CAP) & (slot == dest * CAP + part) & ~panel
-    first = dest // col_count * (col_count * CAP)
-    in_panel = (part >= CAP) & (slot == first + part - CAP) & panel
-    value = jnp.where(in_main, place + 1, 0) + jnp.where(in_panel, block + 1, 0)
-    return slot, panel_tiles, jnp.sum(value, axis=2) - 1
-
-
-def pack_kernel(chunks, slot, panel_tiles, tiles, first, second, held, load_sem, main_sem, panel_sem):
-    count = tiles.shape[0]
+    dest_row = dest // col_count
+    local = (dest_row == row_index) & (col_index == 0)
+    in_panel = (part >= CAP) & (slot == dest_row * (col_count * CAP) + part - CAP) & panel
+    value = jnp.where(in_main, place + 1, 0) + jnp.where(in_panel & ~local, block + 1, 0)
+    message = jnp.sum(value, axis=2) - 1
+    message = jnp.where(local[..., 0] & (part[..., 0] == CAP), 0, message)
+    mine = jnp.arange(CAP, dtype=jnp.int32)[:, None]
+    stays = panel & (col_index == 0) & (slot == row_index * (col_count * CAP) + mine)
+    stay_tiles = jnp.sum(jnp.where(stays, order, 0), axis=1)
+    stay_blocks = jnp.sum(jnp.where(stays, block + 1, 0), axis=1) - 1
+    where = jnp.stack([row_index, col_index]).astype(jnp.int32)
+    return slot, panel_tiles, message, jnp.concatenate([where, stay_tiles, stay_blocks])
+
+
+def pack_kernel(chunks, slot, panel_tiles, local, tiles, front, first, second, *scratch):
+    held, corner, block, load_sem, main_sem, panel_sem, corner_sem = scratch
+    count, parts, rows, size = tiles.shape
     step = count // chunks
     row_count, col_count = first.shape[:2]
+    row_index, col_index = local[0], local[1]
 
     def load(i):
         part = pl.ds(i * step, step)
         return pltpu.make_async_copy(tiles.at[part], held.at[part], load_sem.at[i])
 
+    load_corner = pltpu.make_async_copy(front.at[pl.ds(0, 2 * parts * rows)], corner, corner_sem)
     for i in range(chunks):
         load(i).start()
+    load_corner.start()
     for i in range(chunks):
         load(i).wait()
 
@@ -59,7 +71,7 @@
             def _():
                 pltpu.make_async_copy(
                     held.at[k],
-                    first.at[owner // col_count, owner % col_count, pl.ds(CAP, held.shape[1])],
+                    first.at[owner // col_count, owner % col_count, pl.ds(CAP, parts)],
                     main_sem,
                 ).start()
 
@@ -70,17 +82,34 @@
             return carry
 
         lax.fori_loop(i * step, (i + 1) * step, send, 0)
+    load_corner.wait()
+    block[...] = corner[pl.ds(0, parts * rows, stride=2), :].reshape(block.shape)
+    for s in range(CAP):
+
+        @pl.when(local[2 + CAP + s] == 0)
+        def _():
+            block[...] += held[local[2 + s]]
+
     for r in range(row_count):
         for s in range(CAP):
-            pltpu.make_async_copy(
-                held.at[panel_tiles[r * CAP + s]], first.at[r, :, s], panel_sem
-            ).start()
+            own = (row_index == r) & (col_index == 0) & (s == 0)
+
+            @pl.when(own)
+            def _():
+                pltpu.make_async_copy(block, first.at[r, :, s], panel_sem).start()
+
+            @pl.when(jnp.logical_not(own))
+            def _():
+                pltpu.make_async_copy(
+                    held.at[panel_tiles[r * CAP + s]], first.at[r, :, s], panel_sem
+                ).start()
+
     pltpu.make_async_copy(held, second, main_sem).wait()
     some = pl.ds(0, row_count * CAP)
     pltpu.make_async_copy(held.at[some], second.at[some], panel_sem).wait()
 
 
-def pack(slot, panel_tiles, tiles, row_count, col_count):
+def pack(slot, panel_tiles, local, tiles, front, row_count, col_count):
     count, parts, rows, size = tiles.shape
     chunks = 8
     return pl.pallas_call(
@@ -89,25 +118,29 @@
             jax.ShapeDtypeStruct((row_count, col_count, CAP + parts, rows, size), jnp.float32),
             jax.ShapeDtypeStruct((row_count * col_count, parts, rows, size), jnp.float32),
         ],
-        in_specs=[
-            pl.BlockSpec(memory_space=SMEM),
-            pl.BlockSpec(memory_space=SMEM),
-            pl.BlockSpec(memory_space=ANY),
-        ],
+        in_specs=[pl.BlockSpec(memory_space=SMEM)] * 3 + [pl.BlockSpec(memory_space=ANY)] * 2,
         out_specs=[pl.BlockSpec(memory_space=ANY)] * 2,
         scratch_shapes=[
             VMEM(tiles.shape, jnp.float32),
+            VMEM((2 * parts * rows, size), jnp.float32),
+            VMEM((parts, rows, size), jnp.float32),
             pltpu.SemaphoreType.DMA((chunks,)),
             pltpu.SemaphoreType.DMA,
             pltpu.SemaphoreType.DMA,
+            pltpu.SemaphoreType.DMA,
         ],
         compiler_params=LIMIT,
         name="pack",
-    )(slot, panel_tiles, tiles)
-
-
-def split_kernel(rows, front, *outs):
+    )(slot, panel_tiles, local, tiles, front)
+
+
+def split_kernel(rows, local, front, tiles, *refs):
+    outs, (held, sem) = refs[:-2], refs[-2:]
     col_count = len(outs)
+    for s in range(CAP):
+        copy = pltpu.make_async_copy(tiles.at[local[2 + s]], held.at[s], sem.at[s])
+        copy.start()
+        copy.wait()
 
     def block(a, carry):
         for q in range(col_count):
@@ -115,39 +148,41 @@
             outs[q][a] = front[pl.ds(start, rows, stride=2), :]
         return carry
 
-    lax.fori_loop(0, outs[0].shape[0], block, 0, unroll=True)
-
-
-def split_front(front, row_blocks, col_count):
-    size = front.shape[1]
-    rows = size // col_count
-    steps = 6
+    lax.fori_loop(0, outs[0].shape[0], block, 0, unroll=4)
+    for s in range(CAP):
+        place = local[2 + CAP + s]
+
+        @pl.when(place >= 0)
+        def _():
+            for q in range(col_count):
+                outs[q][place] += held[s, q]
+
+    for q in range(col_count):
+        outs[q][0] = jnp.zeros_like(outs[q][0])
+
+
+def split_front(local, front, tiles, row_blocks):
+    col_count, rows, size = tiles.shape[1:]
     return pl.pallas_call(
         functools.partial(split_kernel, rows),
         out_shape=[jax.ShapeDtypeStruct((row_blocks, rows, size), jnp.float32)] * col_count,
-        grid=(steps,),
-        in_specs=[pl.BlockSpec((front.shape[0] // steps, size), lambda i: (i, 0))],
-        out_specs=[pl.BlockSpec((row_blocks // steps, rows, size), lambda i: (i, 0, 0))]
-        * col_count,
+        in_specs=[
+            pl.BlockSpec(memory_space=SMEM),
+            pl.BlockSpec(memory_space=VMEM),
+            pl.BlockSpec(memory_space=ANY),
+        ],
+        out_specs=[pl.BlockSpec(memory_space=VMEM)] * col_count,
+        scratch_shapes=[
+            VMEM((CAP, col_count, rows, size), jnp.float32),
+            pltpu.SemaphoreType.DMA((CAP,)),
+        ],
         compiler_params=LIMIT,
         name="split_front",
-    )(front)
-
-
-def slices_kernel(col_count, where, part_0, part_1, arrived, *refs):
-    own = refs[:col_count]
-    windows, column, total, sem = refs[col_count:]
-    row_blocks = own[0].shape[0]
-    blocks = pl.ds(0, row_blocks)
-    col_index = where[1]
-    for k in range(col_count):
-
-        @pl.when(col_index == k)
-        def _():
-            copy = pltpu.make_async_copy(own[k], total.at[blocks], sem)
-            copy.start()
-            copy.wait()
-
+    )(local, front, tiles)
+
+
+def slices_kernel(row_blocks, part_0, part_1, arrived, windows, column, total):
+    total[...] = jnp.zeros_like(total)
     parts = (part_0, part_1)
 
     def source(d, carry):
@@ -157,66 +192,63 @@
         return carry
 
     lax.fori_loop(0, arrived.shape[0], source, 0, unroll=8)
-    for k in range(col_count):
-        column[k, blocks] = total[blocks]
+    column[...] = total[pl.ds(0, row_blocks)]
     windows[...] = jnp.broadcast_to(total[0][None], windows.shape)
 
 
-def sum_slices(where, parts, arrived, own, row_count, col_count, extra):
+def sum_slices(parts, arrived, row_count, row_blocks):
     devices, _, rows, size = arrived.shape
-    row_blocks = own[0].shape[0]
     outs = [
         jax.ShapeDtypeStruct((row_count, rows, size), jnp.float32),
-        jax.ShapeDtypeStruct((col_count, row_blocks + extra, rows, size), jnp.float32),
+        jax.ShapeDtypeStruct((row_blocks, rows, size), jnp.float32),
     ]
     return pl.pallas_call(
-        functools.partial(slices_kernel, col_count),
+        functools.partial(slices_kernel, row_blocks),
         out_shape=outs,
         grid=(1,),
-        in_specs=[pl.BlockSpec(memory_space=SMEM)] * 3
-        + [pl.BlockSpec((devices, CAP, rows, size), lambda i: (0, 0, 0, 0))]
-        + [pl.BlockSpec(memory_space=ANY)] * col_count,
-        out_specs=[
-            pl.BlockSpec(outs[0].shape, lambda i: (0, 0, 0)),
-            pl.BlockSpec(outs[1].shape, lambda i: (0, 0, 0, 0)),
-        ],
-        scratch_shapes=[
-            VMEM((row_blocks + 1, rows, size), jnp.float32),
-            pltpu.SemaphoreType.DMA,
-        ],
+        in_specs=[pl.BlockSpec(memory_space=SMEM)] * 2
+        + [pl.BlockSpec((devices, CAP, rows, size), lambda i: (0, 0, 0, 0))],
+        out_specs=[pl.BlockSpec(out.shape, lambda i: (0, 0, 0)) for out in outs],
+        scratch_shapes=[VMEM((row_blocks + 1, rows, size), jnp.float32)],
         compiler_params=LIMIT,
         name="sum_slices",
-    )(where, *parts, arrived, *own)
-
-
-def windows_kernel(row_blocks, windows, column, out, sem):
-    col_count = column.shape[0]
-    copies = []
+    )(*parts, arrived)
+
+
+def spread_kernel(local, windows, column, *refs):
+    col_count = len(refs) - 3
+    own, (out, held, sem) = refs[:col_count], refs[col_count:]
+    row_blocks = column.shape[0]
     for k in range(col_count):
+
+        @pl.when(local[1] == k)
+        def _():
+            copy = pltpu.make_async_copy(own[k], held, sem)
+            copy.start()
+            copy.wait()
+
+    total = column[...] + held[...]
+    for k in range(col_count):
+        out[k, pl.ds(0, row_blocks)] = total
         for i, j in enumerate((0, *range(k, windows.shape[0], col_count))):
-            copies.append(
-                pltpu.make_async_copy(
-                    windows.at[j], out.at[k, row_blocks + i], sem.at[len(copies)]
-                )
-            )
-    for copy in copies:
-        copy.start()
-    for copy in copies:
-        copy.wait()
-
-
-def add_windows(windows, column, row_blocks):
-    count = column.shape[0] * (column.shape[1] - row_blocks)
-    return pl.pallas_call(
-        functools.partial(windows_kernel, row_blocks),
-        out_shape=jax.ShapeDtypeStruct(column.shape, column.dtype),
-        in_specs=[pl.BlockSpec(memory_space=VMEM), pl.BlockSpec(memory_space=ANY)],
-        out_specs=pl.BlockSpec(memory_space=ANY),
-        input_output_aliases={1: 0},
-        scratch_shapes=[pltpu.SemaphoreType.DMA((count,))],
-        compiler_params=LIMIT,
-        name="add_windows",
-    )(windows, column)
+            out[k, row_blocks + i] = windows[j]
+
+
+def spread(local, windows, column, own):
+    row_blocks, rows, size = column.shape
+    extra = 1 + windows.shape[0] // len(own)
+    out = jax.ShapeDtypeStruct((len(own), row_blocks + extra, rows, size), jnp.float32)
+    return pl.pallas_call(
+        spread_kernel,
+        out_shape=out,
+        in_specs=[pl.BlockSpec(memory_space=SMEM)]
+        + [pl.BlockSpec(memory_space=VMEM)] * 2
+        + [pl.BlockSpec(memory_space=ANY)] * len(own),
+        out_specs=pl.BlockSpec(memory_space=VMEM),
+        scratch_shapes=[VMEM(column.shape, jnp.float32), pltpu.SemaphoreType.DMA],
+        compiler_params=LIMIT,
+        name="spread",
+    )(local, windows, column, *own)
 
 
 def add_kernel(chunks, places, base, tiles, out, total, held, base_sem, tile_sem):
@@ -340,24 +372,26 @@
     devices = row_count * col_count
     flat_front = front.reshape(row_blocks * size * col_blocks, size)
     tiles = child_tiles.reshape(-1, col_count, rows, size)
-    where = jnp.stack([row_index, col_index]).astype(jnp.int32)
-
-    own = split_front(flat_front, row_blocks, col_count)
-    own = [own[0]] + [lax.ppermute(own[k], "col", [(0, k)]) for k in range(1, col_count)]
-    slot, panel_tiles, message = send_tables(
-        child_rows.reshape(-1), child_cols.reshape(-1), row_count, col_count, size
+    slot, panel_tiles, message, local = send_tables(
+        child_rows.reshape(-1),
+        child_cols.reshape(-1),
+        row_index,
+        col_index,
+        row_count,
+        col_count,
+        size,
     )
     message = lax.all_to_all(message, both, split_axis=0, concat_axis=0, tiled=True)
     main, part = ([message[:, h * CAP + s] for s in range(CAP)] for h in range(2))
-    first, second = pack(slot, panel_tiles, tiles, row_count, col_count)
+    first, second = pack(slot, panel_tiles, local, tiles, flat_front, row_count, col_count)
     first = first.reshape((devices,) + first.shape[2:])
-    first = after(first, *own[1:])
+    own = list(split_front(local, flat_front, tiles, row_blocks))
+    for k in (7, 2, 4, 5, 3, 1, 6):
+        own[k] = lax.ppermute(own[k], "col", [(0, k)])
     arrived = lax.all_to_all(first, both, split_axis=0, concat_axis=0, tiled=True)
-    windows, column = sum_slices(
-        where, part, arrived, own, row_count, col_count, 1 + col_blocks
-    )
+    windows, column = sum_slices(part, arrived, row_count, row_blocks)
     windows = lax.all_to_all(windows, "row", split_axis=0, concat_axis=0, tiled=True)
-    column = add_windows(windows, column, row_blocks)
+    column = spread(local, windows, column, own)
     column = lax.all_to_all(column, "col", split_axis=0, concat_axis=0, tiled=True)
     second = lax.all_to_all(
         after(second, column), both, split_axis=0, concat_axis=0, tiled=True
@@ -369,7 +403,7 @@
         factor, jnp.eye(size, dtype=jnp.float32), lower=True
     )
     total = add_tiles(main[0], flat_front, arrived, CAP)
-    base = update_front(where, total, inverse.T, window, column, row_count, row_blocks)
+    base = update_front(local, total, inverse.T, window, column, row_count, row_blocks)
     return add_tiles(main[1], base, second, 0).reshape(front.shape)
 
 

time: 386 us -> 368 us (0.953)
  blocking collectives: 60.4 us -> 45.3 us
  waiting for transfers between devices: 180 us -> 168 us
  starting transfers between devices: 41.1 us -> 46.7 us
    all_to_all x1, waiting for transfers between devices: 135 us -> 2.66 us  [per_device(): lax.all_to_all(first, both, split_axis=0, concat_axis=0, tiled=True)]
    ppermute x7, waiting for transfers between devices: 6.88 us -> 127 us  [per_device(): own[k] = lax.ppermute(own[k], 'col', [(0, k)])]
    all_to_all x1 -> x0, blocking collectives: 12.5 us -> none  [per_device(): lax.all_to_all(windows, 'row', split_axis=0, concat_axis=0, tiled=True)]
    ppermute x7, starting transfers between devices: 15.3 us -> 10.8 us  [per_device(): own[k] = lax.ppermute(own[k], 'col', [(0, k)])]
    all_to_all x0 -> x1, starting transfers between devices: none -> 4.22 us  [per_device(): lax.all_to_all(windows, 'row', split_axis=0, concat_axis=0, tiled=True)]
    all_to_all x1, starting transfers between devices: 6.11 us -> 10.2 us  [per_device(): lax.all_to_all(after(second, column), both, split_axis=0, concat_axis=0,...]
  transfers between devices with their start and end apart: 10 -> 11, of which waited for: 4 -> 6; matrix products, arithmetic and copies ran while one was open for 8% -> 8% of each run, Pallas kernels for 13% -> 16%
where the time goes in v5:
time: 368 us; the launch traced here: 367 us
  waiting for transfers between devices  168 us (46%)
  Pallas kernels  72.9 us (20%)
  starting transfers between devices  46.7 us (13%)
  blocking collectives  45.3 us (12%)
  other arithmetic  27.8 us (8%)
  local copies, waits for them, and re-layouts  5.2 us (1%)
    ppermute x7, waiting for transfers between devices, per_device(): own[k] = lax.ppermute(own[k], 'col', [(0, k)])  127 us
    all_to_all x1, blocking collectives, per_device(): lax.all_to_all(column, 'col', split_axis=0, concat_axis=0, tiled=True)  45.3 us
    all_to_all x1, waiting for transfers between devices, per_device(): lax.all_to_all(after(second, column), both, split_axis=0, concat_axis=0,...  38.6 us
    pallas_call x1, Pallas kernels, update_front(): pl.pallas_call(functools.partial(update_kernel, (row_count, row_blocks)),...  31.3 us
    pallas_call x2, Pallas kernels, add_tiles(): pl.pallas_call(functools.partial(add_kernel, chunks), out_shape=jax.Shape...  19.4 us
    another operation x3, other arithmetic, per_device(): factor = jnp.linalg.cholesky(0.5 * (corner + corner.T))  12.4 us
    all_to_all x1, starting transfers between devices, per_device(): lax.all_to_all(message, both, split_axis=0, concat_axis=0, tiled=True)  11.2 us
    ppermute x7, starting transfers between devices, per_device(): own[k] = lax.ppermute(own[k], 'col', [(0, k)])  10.8 us
  transfers between devices with their start and end apart: 11, of which 6 were waited for; matrix products, arithmetic and copies ran while one was open for 8% of the time, Pallas kernels for 16%

profile of v5, /device:TPU:0, one launch (start us, length us, event | category | flops | bytes accessed | tf_op | source)
XLA Modules:
  0.0 367.1 jit_solution(2567943366815270338)
XLA Ops:
  4.1 11.2 %all-to-all-start = ((s32[128,1,4]{2,1,0:T(1,128)}), s32[128,1,4]{2,1,0:T(1,128)S(1)}, u32[]{:S(2)}, u32[]{:S(2)}) async-start(s32[128,1,4]{2,1,0:T(1,128)} %copy.21), calls=%async_computation | async-start | bytes 131072 | tf_op jit(solution)/shard_map/all_to_all | solution.py:384
  16.9 7.9 %pack.1 = (f32[16,8,10,16,128]{4,3,2,1,0:T(8,128)}, f32[128,8,16,128]{3,2,1,0:T(8,128)}) custom-call(s32[128]{0:T(128)} %copy-done.8, s32[32]{0:T(128)} %select_reduce_fusion.1.panel_tiles, s32[6]{0:T(128)} %pad_add_fusion.local.where, f32[128,8,16,128]{3,2,1,0:T(8,128)} %bitcast.78, f32[12288,128]{1,0:T(8,128)} %bitcast.75), custom_call_target="tpu_custom_call" | custom-call | tf_op jit(solution)/shard_map/pack/pallas_call | solution.py:115
  24.7 10.2 %all-to-all-start.1 = ((f32[128,10,16,128]{3,2,1,0:T(8,128)}), f32[128,10,16,128]{3,2,1,0:T(8,128)}, u32[]{:S(2)}, u32[]{:S(2)}) async-start(f32[128,10,16,128]{3,2,1,0:T(8,128)} %bitcast.80), calls=%async_computation.1 | async-start | bytes 20971520 | tf_op jit(solution)/shard_map/all_to_all | solution.py:391
  35.0 6.4 %split_front.1 = (f32[48,16,128]{2,1,0:T(8,128)}, f32[48,16,128]{2,1,0:T(8,128)}, f32[48,16,128]{2,1,0:T(8,128)}, f32[48,16,128]{2,1,0:T(8,128)}, f32[48,16,128]...) custom-call(s32[6]{0:T(128)} %pad_add_fusion.local.where, ...), custom_call_target="tpu_custom_call" | custom-call | tf_op jit(solution)/shard_map/split_front/pallas_call | solution.py:166
  41.4 2.9 collective-permute-start
  44.4 1.3 collective-permute-start.1
  45.7 1.3 collective-permute-start.2
  48.3 1.3 collective-permute-start.4
  49.7 108.5 %collective-permute-done.refs_1_ = f32[48,16,128]{2,1,0:T(8,128)S(1)} collective-permute-done((f32[48,16,128]{2,1,0:T(8,128)}, f32[48,16,128]{2,1,0:T(8,128)S(1)}, u32[]{:S(2)}, u32[]{:S(2)}) %collective-permute-start) | collective-permute-done | bytes 393248 | tf_op jit(solution)/shard_map/ppermute | solution.py:390
  159.4 7.1 %collective-permute-done.1.refs_2_ = f32[48,16,128]{2,1,0:T(8,128)S(1)} collective-permute-done((f32[48,16,128]{2,1,0:T(8,128)}, f32[48,16,128]{2,1,0:T(8,128)S(1)}, u32[]{:S(2)}, u32[]{:S(2)}) %collective-permute-start.1) | collective-permute-done | bytes 393248 | tf_op jit(solution)/shard_map/ppermute | solution.py:390
  168.6 2.7 all-to-all-done.1.tiles.arrived
  171.3 3.9 %sum_slices.1 = (f32[16,16,128]{2,1,0:T(8,128)}, f32[48,16,128]{2,1,0:T(8,128)}) custom-call(s32[128]{0:T(128)} %get-tuple-element.30.part_0, s32[128]{0:T(128)} %get-tuple-element.29.part_1, f32[128,10,16,128]{3,2,1,0:T(8,128)} %all-to-all-done.1.tiles.arrived), custom_call_target="tpu_custom_call" | custom-call | tf_op jit(solution)/shard_map/sum_slices/pallas_call | solution.py:205
  175.2 4.2 %all-to-all-start.2 = ((f32[16,16,128]{2,1,0:T(8,128)}), f32[16,16,128]{2,1,0:T(8,128)S(1)}, u32[]{:S(2)}, u32[]{:S(2)}) async-start(f32[16,16,128]{2,1,0:T(8,128)} %get-tuple-element.18), calls=%async_computation.2 | async-start | bytes 262144 | tf_op jit(solution)/shard_map/all_to_all | solution.py:393
  179.4 3.9 %collective-permute-done.3.refs_4_ = f32[48,16,128]{2,1,0:T(8,128)S(1)} collective-permute-done((f32[48,16,128]{2,1,0:T(8,128)}, f32[48,16,128]{2,1,0:T(8,128)S(1)}, u32[]{:S(2)}, u32[]{:S(2)}) %collective-permute-start.3) | collective-permute-done | bytes 393248 | tf_op jit(solution)/shard_map/ppermute | solution.py:390
  183.3 7.2 %collective-permute-done.4.refs_5_ = f32[48,16,128]{2,1,0:T(8,128)S(1)} collective-permute-done((f32[48,16,128]{2,1,0:T(8,128)}, f32[48,16,128]{2,1,0:T(8,128)S(1)}, u32[]{:S(2)}, u32[]{:S(2)}) %collective-permute-start.4) | collective-permute-done | bytes 393248 | tf_op jit(solution)/shard_map/ppermute | solution.py:390
  191.6 4.0 %spread.1 = f32[8,51,16,128]{3,2,1,0:T(8,128)} custom-call(s32[6]{0:T(128)} %pad_add_fusion.local.where, f32[16,16,128]{2,1,0:T(8,128)} %copy-done, f32[48,16,128]{2,1,0:T(8,128)} %get-tuple-element.19.column, f32[48,16,128]{2,1,0:T(8,128)} %get-tuple-element.20.refs_0_, f32[48,16,128]{2,1,0:T(8,128)} %copy-done.1, f32[48,16,128]{2,1,0:T(8,128)} %copy-done.2, ...), custom_call_target="tpu_custom_call" | custom-call | tf_op jit(solution)/shard_map/spread/pallas_call | solution.py:241
  195.7 45.3 %all_to_all.29.column.refs_1_ = f32[8,51,16,128]{3,2,1,0:T(8,128)} all-to-all(f32[8,51,16,128]{3,2,1,0:T(8,128)} %spread.1), channel_id=1, replica_groups=mesh['row'=16,'col'=8] {'col'}, dimensions={0} | all-to-all | bytes 6684672 | tf_op jit(solution)/shard_map/all_to_all | solution.py:395
  240.9 10.2 %all-to-all-start.4 = ((f32[128,8,16,128]{3,2,1,0:T(8,128)}), f32[128,8,16,128]{3,2,1,0:T(8,128)}, u32[]{:S(2)}, u32[]{:S(2)}) async-start(f32[128,8,16,128]{3,2,1,0:T(8,128)} %after.1), calls=%async_computation.4 | async-start | bytes 16777216 | tf_op jit(solution)/shard_map/all_to_all | solution.py:396
  251.2 9.7 %add_tiles.2.front = f32[12288,128]{1,0:T(8,128)} custom-call(s32[128]{0:T(128)} %get-tuple-element.31.places, f32[12288,128]{1,0:T(8,128)} %bitcast.77, f32[128,10,16,128]{3,2,1,0:T(8,128)} %all-to-all-done.1.tiles.arrived), custom_call_target="tpu_custom_call" | custom-call | tf_op jit(solution)/shard_map/add_tiles/pallas_call | solution.py:288
  262.0 11.7 %cholesky.14 = f32[128,128]{1,0:T(8,128)S(1)} custom-call(f32[128,128]{1,0:T(8,128)S(1)} %fusion.3), custom_call_target="Cholesky" | custom-call | tf_op jit(solution)/shard_map/jit(cholesky)/cholesky | solution.py:401
  275.0 9.8 %custom-call.7 = f32[1,128,128]{1,2,0:T(8,128)S(1)} custom-call(f32[1,128,128]{2,1,0:T(8,128)S(1)} %fusion), custom_call_target="InvertDiagBlocksLowerTriangular" | custom-call | tf_op jit(solution)/shard_map/jit(_solve_triangular)/triangular_solve | solution.py:402
  287.3 31.3 %update_front.1.base = f32[12288,128]{1,0:T(8,128)} custom-call(s32[6]{0:T(128)} %pad_add_fusion.local.where, f32[12288,128]{1,0:T(8,128)} %add_tiles.2.front, f32[128,128]{1,0:T(8,128)} %fusion.1.inverse_t, f32[256,128]{1,0:T(8,128)} %bitcast.83, f32[8,51,16,128]{3,2,1,0:T(8,128)} %all_to_all.29.column.refs_1_), custom_call_target="tpu_custom_call" | custom-call | tf_op jit(solution)/shard_map/update_front/pallas_call | solution.py:339
  318.6 38.6 %all-to-all-done.4.tiles = f32[128,8,16,128]{3,2,1,0:T(8,128)} async-done(((f32[128,8,16,128]{3,2,1,0:T(8,128)}), f32[128,8,16,128]{3,2,1,0:T(8,128)}, u32[]{:S(2)}, u32[]{:S(2)}) %all-to-all-start.4) | async-done | bytes 8388640 | tf_op jit(solution)/shard_map/all_to_all | solution.py:396
  357.2 9.7 %add_tiles.3 = f32[12288,128]{1,0:T(8,128)} custom-call(s32[128]{0:T(128)} %get-tuple-element.32.places, f32[12288,128]{1,0:T(8,128)} %update_front.1.base, f32[128,8,16,128]{3,2,1,0:T(8,128)} %all-to-all-done.4.tiles), custom_call_target="tpu_custom_call" | custom-call | tf_op jit(solution)/shard_map/add_tiles/pallas_call | solution.py:288
  (59 shorter events, 16.3 us)
Async XLA Ops:
  2.2 14.6 %copy-start.8 = (s32[128]{0:T(128)}, s32[128]{0:T(128)S(1)}, u32[]{:S(2)}) copy-start(s32[128]{0:T(128)S(1)} %get-tuple-element.44.slot) | copy-start | bytes 1540
  4.1 20.6 %all-to-all-start = ((s32[128,1,4]{2,1,0:T(1,128)}), s32[128,1,4]{2,1,0:T(1,128)S(1)}, u32[]{:S(2)}, u32[]{:S(2)}) async-start(s32[128,1,4]{2,1,0:T(1,128)} %copy.21), calls=%async_computation | async-start | bytes 131072 | tf_op jit(solution)/shard_map/all_to_all | solution.py:384
  24.7 146.5 %all-to-all-start.1 = ((f32[128,10,16,128]{3,2,1,0:T(8,128)}), f32[128,10,16,128]{3,2,1,0:T(8,128)}, u32[]{:S(2)}, u32[]{:S(2)}) async-start(f32[128,10,16,128]{3,2,1,0:T(8,128)} %bitcast.80), calls=%async_computation.1 | async-start | bytes 20971520 | tf_op jit(solution)/shard_map/all_to_all | solution.py:391
  41.4 116.7 %collective-permute-start = (f32[48,16,128]{2,1,0:T(8,128)}, f32[48,16,128]{2,1,0:T(8,128)S(1)}, u32[]{:S(2)}, u32[]{:S(2)}) collective-permute-start(f32[48,16,128]{2,1,0:T(8,128)} %get-tuple-element.21), channel_id=1, source_target_pairs={{0,1},{8,9},{16,17},{24,25},{32,33},{40,41},{48,49},{56,57},{64,65... | collective-permute-start | bytes 1179656 | tf_op jit(solution)/shard_map/ppermute | solution.py:390
  44.4 122.1 %collective-permute-start.1 = (f32[48,16,128]{2,1,0:T(8,128)}, f32[48,16,128]{2,1,0:T(8,128)S(1)}, u32[]{:S(2)}, u32[]{:S(2)}) collective-permute-start(f32[48,16,128]{2,1,0:T(8,128)} %get-tuple-element.22), channel_id=1, source_target_pairs={{0,2},{8,10},{16,18},{24,26},{32,34},{40,42},{48,50},{56,58},{64,6... | collective-permute-start | bytes 1179656 | tf_op jit(solution)/shard_map/ppermute | solution.py:390
  45.7 133.7 %collective-permute-start.2 = (f32[48,16,128]{2,1,0:T(8,128)}, f32[48,16,128]{2,1,0:T(8,128)S(1)}, u32[]{:S(2)}, u32[]{:S(2)}) collective-permute-start(f32[48,16,128]{2,1,0:T(8,128)} %get-tuple-element.23), channel_id=1, source_target_pairs={{0,3},{8,11},{16,19},{24,27},{32,35},{40,43},{48,51},{56,59},{64,6... | collective-permute-start | bytes 1179656 | tf_op jit(solution)/shard_map/ppermute | solution.py:390
  47.0 136.3 %collective-permute-start.3 = (f32[48,16,128]{2,1,0:T(8,128)}, f32[48,16,128]{2,1,0:T(8,128)S(1)}, u32[]{:S(2)}, u32[]{:S(2)}) collective-permute-start(f32[48,16,128]{2,1,0:T(8,128)} %get-tuple-element.24), channel_id=1, source_target_pairs={{0,4},{8,12},{16,20},{24,28},{32,36},{40,44},{48,52},{56,60},{64,6... | collective-permute-start | bytes 1179656 | tf_op jit(solution)/shard_map/ppermute | solution.py:390
  48.3 142.2 %collective-permute-start.4 = (f32[48,16,128]{2,1,0:T(8,128)}, f32[48,16,128]{2,1,0:T(8,128)S(1)}, u32[]{:S(2)}, u32[]{:S(2)}) collective-permute-start(f32[48,16,128]{2,1,0:T(8,128)} %get-tuple-element.25), channel_id=1, source_target_pairs={{0,5},{8,13},{16,21},{24,29},{32,37},{40,45},{48,53},{56,61},{64,6... | collective-permute-start | bytes 1179656 | tf_op jit(solution)/shard_map/ppermute | solution.py:390
  158.1 32.5 %copy-start.1 = (f32[48,16,128]{2,1,0:T(8,128)}, f32[48,16,128]{2,1,0:T(8,128)S(1)}, u32[]{:S(2)}) copy-start(f32[48,16,128]{2,1,0:T(8,128)S(1)} %collective-permute-done.refs_1_) | copy-start | bytes 1179652
  158.1 32.4 %collective-permute-start.5 = (f32[48,16,128]{2,1,0:T(8,128)}, f32[48,16,128]{2,1,0:T(8,128)S(1)}, u32[]{:S(2)}, u32[]{:S(2)}) collective-permute-start(f32[48,16,128]{2,1,0:T(8,128)} %get-tuple-element.26), channel_id=1, source_target_pairs={{0,6},{8,14},{16,22},{24,30},{32,38},{40,46},{48,54},{56,62},{64,7... | collective-permute-start | bytes 1179656 | tf_op jit(solution)/shard_map/ppermute | solution.py:390
  166.5 24.1 %copy-start.2 = (f32[48,16,128]{2,1,0:T(8,128)}, f32[48,16,128]{2,1,0:T(8,128)S(1)}, u32[]{:S(2)}) copy-start(f32[48,16,128]{2,1,0:T(8,128)S(1)} %collective-permute-done.1.refs_2_) | copy-start | bytes 1179652
  166.5 24.1 %collective-permute-start.6 = (f32[48,16,128]{2,1,0:T(8,128)}, f32[48,16,128]{2,1,0:T(8,128)S(1)}, u32[]{:S(2)}, u32[]{:S(2)}) collective-permute-start(f32[48,16,128]{2,1,0:T(8,128)} %get-tuple-element.27), channel_id=1, source_target_pairs={{0,7},{8,15},{16,23},{24,31},{32,39},{40,47},{48,55},{56,63},{64,7... | collective-permute-start | bytes 1179656 | tf_op jit(solution)/shard_map/ppermute | solution.py:390
  175.2 15.4 %all-to-all-start.2 = ((f32[16,16,128]{2,1,0:T(8,128)}), f32[16,16,128]{2,1,0:T(8,128)S(1)}, u32[]{:S(2)}, u32[]{:S(2)}) async-start(f32[16,16,128]{2,1,0:T(8,128)} %get-tuple-element.18), calls=%async_computation.2 | async-start | bytes 262144 | tf_op jit(solution)/shard_map/all_to_all | solution.py:393
  179.4 11.2 %copy-start.3 = (f32[48,16,128]{2,1,0:T(8,128)}, f32[48,16,128]{2,1,0:T(8,128)S(1)}, u32[]{:S(2)}) copy-start(f32[48,16,128]{2,1,0:T(8,128)S(1)} %collective-permute-done.2.refs_3_) | copy-start | bytes 1179652
  183.3 7.3 %copy-start.4 = (f32[48,16,128]{2,1,0:T(8,128)}, f32[48,16,128]{2,1,0:T(8,128)S(1)}, u32[]{:S(2)}) copy-start(f32[48,16,128]{2,1,0:T(8,128)S(1)} %collective-permute-done.3.refs_4_) | copy-start | bytes 1179652
  190.6 0.8 copy-start.5
  190.6 0.9 copy-start.6
  190.6 1.0 copy-start.7
  190.6 1.1 copy-start
  240.9 116.3 %all-to-all-start.4 = ((f32[128,8,16,128]{3,2,1,0:T(8,128)}), f32[128,8,16,128]{3,2,1,0:T(8,128)}, u32[]{:S(2)}, u32[]{:S(2)}) async-start(f32[128,8,16,128]{3,2,1,0:T(8,128)} %after.1), calls=%async_computation.4 | async-start | bytes 16777216 | tf_op jit(solution)/shard_map/all_to_all | solution.py:396

commit v6 on v5

--- a/solution.py
+++ b/solution.py
@@ -45,21 +45,72 @@
     return slot, panel_tiles, message, jnp.concatenate([where, stay_tiles, stay_blocks])
 
 
-def pack_kernel(chunks, slot, panel_tiles, local, tiles, front, first, second, *scratch):
-    held, corner, block, load_sem, main_sem, panel_sem, corner_sem = scratch
+def pack_panel_kernel(panel_tiles, local, tiles, front, out, held, corner, block, load_sem, corner_sem, sem):
+    parts, rows, size = block.shape
+    slots = held.shape[0]
+    row_count = out.shape[0]
+    load_corner = pltpu.make_async_copy(front.at[pl.ds(0, 2 * parts * rows)], corner, corner_sem)
+    load_corner.start()
+    loads = [
+        pltpu.make_async_copy(tiles.at[panel_tiles[i]], held.at[i], load_sem.at[i])
+        for i in range(slots)
+    ]
+    for load in loads:
+        load.start()
+    load_corner.wait()
+    block[...] = corner[pl.ds(0, parts * rows, stride=2), :].reshape(block.shape)
+    for r in range(row_count):
+        mine = (local[0] == r) & (local[1] == 0)
+        for s in range(CAP):
+            loads[r * CAP + s].wait()
+
+        @pl.when(mine)
+        def _():
+            for s in range(CAP):
+
+                @pl.when(local[2 + CAP + s] == 0)
+                def _():
+                    block[...] += held[r * CAP + s]
+
+            held[r * CAP] = block[...]
+
+        for s in range(CAP):
+            pltpu.make_async_copy(held.at[r * CAP + s], out.at[r, :, s], sem).start()
+    whole = pltpu.make_async_copy(out, out, sem)
+    whole.wait()
+
+
+def pack_panel(panel_tiles, local, tiles, front, row_count):
     count, parts, rows, size = tiles.shape
+    slots = row_count * CAP
+    return pl.pallas_call(
+        pack_panel_kernel,
+        out_shape=jax.ShapeDtypeStruct((row_count, parts, CAP, rows, size), jnp.float32),
+        in_specs=[pl.BlockSpec(memory_space=SMEM)] * 2 + [pl.BlockSpec(memory_space=ANY)] * 2,
+        out_specs=pl.BlockSpec(memory_space=ANY),
+        scratch_shapes=[
+            VMEM((slots, parts, rows, size), jnp.float32),
+            VMEM((2 * parts * rows, size), jnp.float32),
+            VMEM((parts, rows, size), jnp.float32),
+            pltpu.SemaphoreType.DMA((slots,)),
+            pltpu.SemaphoreType.DMA,
+            pltpu.SemaphoreType.DMA,
+        ],
+        compiler_params=LIMIT,
+        name="pack_panel",
+    )(panel_tiles, local, tiles, front)
+
+
+def pack_kernel(chunks, slot, tiles, first, second, held, load_sem, main_sem):
+    count = tiles.shape[0]
     step = count // chunks
-    row_count, col_count = first.shape[:2]
-    row_index, col_index = local[0], local[1]
 
     def load(i):
         part = pl.ds(i * step, step)
         return pltpu.make_async_copy(tiles.at[part], held.at[part], load_sem.at[i])
 
-    load_corner = pltpu.make_async_copy(front.at[pl.ds(0, 2 * parts * rows)], corner, corner_sem)
     for i in range(chunks):
         load(i).start()
-    load_corner.start()
     for i in range(chunks):
         load(i).wait()
 
@@ -69,11 +120,7 @@
 
             @pl.when(where % CAP == 0)
             def _():
-                pltpu.make_async_copy(
-                    held.at[k],
-                    first.at[owner // col_count, owner % col_count, pl.ds(CAP, parts)],
-                    main_sem,
-                ).start()
+                pltpu.make_async_copy(held.at[k], first.at[owner], main_sem).start()
 
             @pl.when(where % CAP == 1)
             def _():
@@ -82,56 +129,25 @@
             return carry
 
         lax.fori_loop(i * step, (i + 1) * step, send, 0)
-    load_corner.wait()
-    block[...] = corner[pl.ds(0, parts * rows, stride=2), :].reshape(block.shape)
-    for s in range(CAP):
-
-        @pl.when(local[2 + CAP + s] == 0)
-        def _():
-            block[...] += held[local[2 + s]]
-
-    for r in range(row_count):
-        for s in range(CAP):
-            own = (row_index == r) & (col_index == 0) & (s == 0)
-
-            @pl.when(own)
-            def _():
-                pltpu.make_async_copy(block, first.at[r, :, s], panel_sem).start()
-
-            @pl.when(jnp.logical_not(own))
-            def _():
-                pltpu.make_async_copy(
-                    held.at[panel_tiles[r * CAP + s]], first.at[r, :, s], panel_sem
-                ).start()
-
     pltpu.make_async_copy(held, second, main_sem).wait()
-    some = pl.ds(0, row_count * CAP)
-    pltpu.make_async_copy(held.at[some], second.at[some], panel_sem).wait()
-
-
-def pack(slot, panel_tiles, local, tiles, front, row_count, col_count):
-    count, parts, rows, size = tiles.shape
+
+
+def pack(slot, tiles, devices):
     chunks = 8
+    out = jax.ShapeDtypeStruct((devices,) + tiles.shape[1:], jnp.float32)
     return pl.pallas_call(
         functools.partial(pack_kernel, chunks),
-        out_shape=[
-            jax.ShapeDtypeStruct((row_count, col_count, CAP + parts, rows, size), jnp.float32),
-            jax.ShapeDtypeStruct((row_count * col_count, parts, rows, size), jnp.float32),
-        ],
-        in_specs=[pl.BlockSpec(memory_space=SMEM)] * 3 + [pl.BlockSpec(memory_space=ANY)] * 2,
+        out_shape=[out, out],
+        in_specs=[pl.BlockSpec(memory_space=SMEM), pl.BlockSpec(memory_space=ANY)],
         out_specs=[pl.BlockSpec(memory_space=ANY)] * 2,
         scratch_shapes=[
             VMEM(tiles.shape, jnp.float32),
-            VMEM((2 * parts * rows, size), jnp.float32),
-            VMEM((parts, rows, size), jnp.float32),
             pltpu.SemaphoreType.DMA((chunks,)),
             pltpu.SemaphoreType.DMA,
-            pltpu.SemaphoreType.DMA,
-            pltpu.SemaphoreType.DMA,
         ],
         compiler_params=LIMIT,
         name="pack",
-    )(slot, panel_tiles, local, tiles, front)
+    )(slot, tiles)
 
 
 def split_kernel(rows, local, front, tiles, *refs):
@@ -261,8 +277,7 @@
 
     def load(i):
         some = pl.ds(i * step, step)
-        skip = pl.ds(tiles.shape[1] - parts, parts)
-        return pltpu.make_async_copy(tiles.at[some, skip], held.at[some], tile_sem.at[i])
+        return pltpu.make_async_copy(tiles.at[some], held.at[some], tile_sem.at[i])
 
     for i in range(chunks):
         load(i).start()
@@ -282,7 +297,7 @@
     store.wait()
 
 
-def add_tiles(places, base, tiles, skip):
+def add_tiles(places, base, tiles):
     slots, parts, rows, size = tiles.shape
     chunks = 8
     return pl.pallas_call(
@@ -296,7 +311,7 @@
         out_specs=pl.BlockSpec(memory_space=ANY),
         scratch_shapes=[
             VMEM((base.shape[0] + 2 * size, size), jnp.float32),
-            VMEM((slots, parts - skip, rows, size), jnp.float32),
+            VMEM(tiles.shape, jnp.float32),
             pltpu.SemaphoreType.DMA,
             pltpu.SemaphoreType.DMA((chunks,)),
         ],
@@ -383,15 +398,19 @@
     )
     message = lax.all_to_all(message, both, split_axis=0, concat_axis=0, tiled=True)
     main, part = ([message[:, h * CAP + s] for s in range(CAP)] for h in range(2))
-    first, second = pack(slot, panel_tiles, local, tiles, flat_front, row_count, col_count)
-    first = first.reshape((devices,) + first.shape[2:])
+    sliced = pack_panel(panel_tiles, local, tiles, flat_front, row_count)
+    sliced = sliced.reshape((devices,) + sliced.shape[2:])
+    sliced = lax.all_to_all(sliced, both, split_axis=0, concat_axis=0, tiled=True)
+    first, second = pack(slot, tiles, devices)
     own = list(split_front(local, flat_front, tiles, row_blocks))
-    for k in (7, 2, 4, 5, 3, 1, 6):
+    order = (1, 7, 4, 5, 2, 3, 6)
+    for k in order:
         own[k] = lax.ppermute(own[k], "col", [(0, k)])
-    arrived = lax.all_to_all(first, both, split_axis=0, concat_axis=0, tiled=True)
-    windows, column = sum_slices(part, arrived, row_count, row_blocks)
+    windows, column = sum_slices(part, sliced, row_count, row_blocks)
     windows = lax.all_to_all(windows, "row", split_axis=0, concat_axis=0, tiled=True)
-    column = spread(local, windows, column, own)
+    first = after(first, windows, *(own[k] for k in order))
+    first = lax.all_to_all(first, both, split_axis=0, concat_axis=0, tiled=True)
+    column = after(spread(local, windows, column, own), first)
     column = lax.all_to_all(column, "col", split_axis=0, concat_axis=0, tiled=True)
     second = lax.all_to_all(
         after(second, column), both, split_axis=0, concat_axis=0, tiled=True
@@ -402,9 +421,9 @@
     inverse = jax.scipy.linalg.solve_triangular(
         factor, jnp.eye(size, dtype=jnp.float32), lower=True
     )
-    total = add_tiles(main[0], flat_front, arrived, CAP)
+    total = add_tiles(main[0], flat_front, first)
     base = update_front(local, total, inverse.T, window, column, row_count, row_blocks)
-    return add_tiles(main[1], base, second, 0).reshape(front.shape)
+    return add_tiles(main[1], base, second).reshape(front.shape)
 
 
 def solution(mesh):

time: 368 us -> 377 us (1.024)
  starting transfers between devices: 46.7 us -> 60.4 us
  waiting for transfers between devices: 168 us -> 161 us
    ppermute x7, waiting for transfers between devices: 127 us -> 13.9 us  [per_device(): own[k] = lax.ppermute(own[k], 'col', [(0, k)])]
    all_to_all x1 -> x2, waiting for transfers between devices: 2.66 us -> 105 us  [the longest x1 105 us: per_device(): first = lax.all_to_all(first, both, split_axis=0, concat_axis=0, tiled=True)]
    all_to_all x1 -> x2, starting transfers between devices: 10.2 us -> 20.3 us  [the longest x1 13.4 us: per_device(): first = lax.all_to_all(first, both, split_axis=0, concat_axis=0, tiled=True)]
    ppermute x7, starting transfers between devices: 10.8 us -> 15.5 us  [per_device(): own[k] = lax.ppermute(own[k], 'col', [(0, k)])]
    all_to_all x1, starting transfers between devices: 10.2 us -> 6.11 us  [per_device(): lax.all_to_all(after(second, column), both, split_axis=0, concat_axis=0,...]
    pallas_call x1 -> x2, Pallas kernels: 7.86 us -> 11.7 us  [the longest x1 7.01 us: pack(): pl.pallas_call(functools.partial(pack_kernel, chunks), out_shape=[out, ou...]
  transfers between devices with their start and end apart: 11 -> 12, of which waited for: 6 -> 5; matrix products, arithmetic and copies ran while one was open for 8% -> 8% of each run, Pallas kernels for 16% -> 18%
where the time goes in v6:
time: 377 us; the launch traced here: 376 us
  waiting for transfers between devices  161 us (43%)
  Pallas kernels  76.2 us (20%)
  starting transfers between devices  60.4 us (16%)
  blocking collectives  42.9 us (11%)
  other arithmetic  27.8 us (7%)
  local copies, waits for them, and re-layouts  6.13 us (2%)
    all_to_all x1, waiting for transfers between devices, per_device(): first = lax.all_to_all(first, both, split_axis=0, concat_axis=0, tiled=True)  105 us
    all_to_all x1, blocking collectives, per_device(): lax.all_to_all(column, 'col', split_axis=0, concat_axis=0, tiled=True)  42.9 us
    all_to_all x1, waiting for transfers between devices, per_device(): lax.all_to_all(after(second, column), both, split_axis=0, concat_axis=0,...  38.6 us
    pallas_call x1, Pallas kernels, update_front(): pl.pallas_call(functools.partial(update_kernel, (row_count, row_blocks)),...  31.3 us
    pallas_call x2, Pallas kernels, add_tiles(): pl.pallas_call(functools.partial(add_kernel, chunks), out_shape=jax.Shape...  19.3 us
    ppermute x7, starting transfers between devices, per_device(): own[k] = lax.ppermute(own[k], 'col', [(0, k)])  15.5 us
    ppermute x7, waiting for transfers between devices, per_device(): own[k] = lax.ppermute(own[k], 'col', [(0, k)])  13.9 us
    all_to_all x1, starting transfers between devices, per_device(): first = lax.all_to_all(first, both, split_axis=0, concat_axis=0, tiled=True)  13.4 us
  transfers between devices with their start and end apart: 12, of which 5 were waited for; matrix products, arithmetic and copies ran while one was open for 8% of the time, Pallas kernels for 18%

profile of v6, /device:TPU:0, one launch (start us, length us, event | category | flops | bytes accessed | tf_op | source)
XLA Modules:
  0.0 375.9 jit_solution(733099646358953315)
XLA Ops:
  4.1 11.2 %all-to-all-start = ((s32[128,1,4]{2,1,0:T(1,128)}), s32[128,1,4]{2,1,0:T(1,128)S(1)}, u32[]{:S(2)}, u32[]{:S(2)}) async-start(s32[128,1,4]{2,1,0:T(1,128)} %copy.23), calls=%async_computation | async-start | bytes 131072 | tf_op jit(solution)/shard_map/all_to_all | solution.py:399
  16.8 4.7 %pack_panel.1 = f32[16,8,2,16,128]{4,3,2,1,0:T(8,128)} custom-call(s32[32]{0:T(128)} %select_reduce_fusion.1.panel_tiles, s32[6]{0:T(128)} %pad_add_fusion.local.where, f32[128,8,16,128]{3,2,1,0:T(8,128)} %bitcast.75, f32[12288,128]{1,0:T(8,128)} %bitcast.78), custom_call_target="tpu_custom_call" | custom-call | tf_op jit(solution)/shard_map/pack_panel/pallas_call | solution.py:86
  21.4 3.1 all-to-all-done
  24.6 6.8 %all-to-all-start.1 = ((f32[128,2,16,128]{3,2,1,0:T(8,128)}), f32[128,2,16,128]{3,2,1,0:T(8,128)S(1)}, u32[]{:S(2)}, u32[]{:S(2)}) async-start(f32[128,2,16,128]{3,2,1,0:T(8,128)} %bitcast.81), calls=%async_computation.1 | async-start | bytes 4194304 | tf_op jit(solution)/shard_map/all_to_all | solution.py:403
  31.4 6.5 %split_front.1 = (f32[48,16,128]{2,1,0:T(8,128)}, f32[48,16,128]{2,1,0:T(8,128)}, f32[48,16,128]{2,1,0:T(8,128)}, f32[48,16,128]{2,1,0:T(8,128)}, f32[48,16,128]...) custom-call(s32[6]{0:T(128)} %pad_add_fusion.local.where, ...), custom_call_target="tpu_custom_call" | custom-call | tf_op jit(solution)/shard_map/split_front/pallas_call | solution.py:182
  37.9 3.0 collective-permute-start
  40.9 3.0 collective-permute-start.1
  45.2 2.1 collective-permute-start.3
  47.3 2.1 collective-permute-start.4
  49.4 13.8 %collective-permute-done.refs_2_.refs_1_ = f32[48,16,128]{2,1,0:T(8,128)S(1)} collective-permute-done((f32[48,16,128]{2,1,0:T(8,128)}, f32[48,16,128]{2,1,0:T(8,128)S(1)}, u32[]{:S(2)}, u32[]{:S(2)}) %collective-permute-start) | collective-permute-done | bytes 393248 | tf_op jit(solution)/shard_map/ppermute | solution.py:408
  69.5 3.4 sum_slices.1
  72.9 7.4 %all-to-all-start.2 = ((f32[16,16,128]{2,1,0:T(8,128)}), f32[16,16,128]{2,1,0:T(8,128)S(1)}, u32[]{:S(2)}, u32[]{:S(2)}) async-start(f32[16,16,128]{2,1,0:T(8,128)} %get-tuple-element.18), calls=%async_computation.2 | async-start | bytes 262144 | tf_op jit(solution)/shard_map/all_to_all | solution.py:410
  80.2 7.0 %pack.1 = (f32[128,8,16,128]{3,2,1,0:T(8,128)}, f32[128,8,16,128]{3,2,1,0:T(8,128)}) custom-call(s32[128]{0:T(128)} %copy-done.5, f32[128,8,16,128]{3,2,1,0:T(8,128)} %bitcast.77), custom_call_target="tpu_custom_call" | custom-call | tf_op jit(solution)/shard_map/pack/pallas_call | solution.py:138
  88.8 13.4 %all-to-all-start.3 = ((f32[128,8,16,128]{3,2,1,0:T(8,128)}), f32[128,8,16,128]{3,2,1,0:T(8,128)}, u32[]{:S(2)}, u32[]{:S(2)}) async-start(f32[128,8,16,128]{3,2,1,0:T(8,128)} %after.3), calls=%async_computation.3 | async-start | bytes 16777216 | tf_op jit(solution)/shard_map/all_to_all | solution.py:412
  102.3 4.0 %spread.1.refs_0_ = f32[8,51,16,128]{3,2,1,0:T(8,128)} custom-call(s32[6]{0:T(128)} %pad_add_fusion.local.where, f32[16,16,128]{2,1,0:T(8,128)} %copy-done.4, f32[48,16,128]{2,1,0:T(8,128)} %get-tuple-element.26.column, f32[48,16,128]{2,1,0:T(8,128)} %get-tuple-element.27.refs_0_, f32[48,16,128]{2,1,0:T(8,128)} %copy-done.1, ...), custom_call_target="tpu_custom_call" | custom-call | tf_op jit(solution)/shard_map/spread/pallas_call | solution.py:257
  106.3 104.8 %all-to-all-done.3.tiles.refs_1_ = f32[128,8,16,128]{3,2,1,0:T(8,128)} async-done(((f32[128,8,16,128]{3,2,1,0:T(8,128)}), f32[128,8,16,128]{3,2,1,0:T(8,128)}, u32[]{:S(2)}, u32[]{:S(2)}) %all-to-all-start.3) | async-done | bytes 8388640 | tf_op jit(solution)/shard_map/all_to_all | solution.py:412
  211.1 42.9 %all_to_all.34.column.refs_1_ = f32[8,51,16,128]{3,2,1,0:T(8,128)} all-to-all(f32[8,51,16,128]{3,2,1,0:T(8,128)} %after.4), channel_id=1, replica_groups=mesh['row'=16,'col'=8] {'col'}, dimensions={0} | all-to-all | bytes 6684672 | tf_op jit(solution)/shard_map/all_to_all | solution.py:414
  254.0 6.1 %all-to-all-start.5 = ((f32[128,8,16,128]{3,2,1,0:T(8,128)}), f32[128,8,16,128]{3,2,1,0:T(8,128)}, u32[]{:S(2)}, u32[]{:S(2)}) async-start(f32[128,8,16,128]{3,2,1,0:T(8,128)} %after.5), calls=%async_computation.5 | async-start | bytes 16777216 | tf_op jit(solution)/shard_map/all_to_all | solution.py:415
  260.1 9.7 %add_tiles.2.front = f32[12288,128]{1,0:T(8,128)} custom-call(s32[128]{0:T(128)} %get-tuple-element.31.places, f32[12288,128]{1,0:T(8,128)} %bitcast.80, f32[128,8,16,128]{3,2,1,0:T(8,128)} %all-to-all-done.3.tiles.refs_1_), custom_call_target="tpu_custom_call" | custom-call | tf_op jit(solution)/shard_map/add_tiles/pallas_call | solution.py:303
  270.8 11.7 %cholesky.14 = f32[128,128]{1,0:T(8,128)S(1)} custom-call(f32[128,128]{1,0:T(8,128)S(1)} %fusion.3), custom_call_target="Cholesky" | custom-call | tf_op jit(solution)/shard_map/jit(cholesky)/cholesky | solution.py:420
  284.0 9.8 %custom-call.7 = f32[1,128,128]{1,2,0:T(8,128)S(1)} custom-call(f32[1,128,128]{2,1,0:T(8,128)S(1)} %fusion), custom_call_target="InvertDiagBlocksLowerTriangular" | custom-call | tf_op jit(solution)/shard_map/jit(_solve_triangular)/triangular_solve | solution.py:421
  296.2 31.3 %update_front.1.base = f32[12288,128]{1,0:T(8,128)} custom-call(s32[6]{0:T(128)} %pad_add_fusion.local.where, f32[12288,128]{1,0:T(8,128)} %add_tiles.2.front, f32[128,128]{1,0:T(8,128)} %fusion.1.inverse_t, f32[256,128]{1,0:T(8,128)} %bitcast.84, f32[8,51,16,128]{3,2,1,0:T(8,128)} %all_to_all.34.column.refs_1_), custom_call_target="tpu_custom_call" | custom-call | tf_op jit(solution)/shard_map/update_front/pallas_call | solution.py:354
  327.5 38.6 %all-to-all-done.5.tiles = f32[128,8,16,128]{3,2,1,0:T(8,128)} async-done(((f32[128,8,16,128]{3,2,1,0:T(8,128)}), f32[128,8,16,128]{3,2,1,0:T(8,128)}, u32[]{:S(2)}, u32[]{:S(2)}) %all-to-all-start.5) | async-done | bytes 8388640 | tf_op jit(solution)/shard_map/all_to_all | solution.py:415
  366.1 9.7 %add_tiles.3 = f32[12288,128]{1,0:T(8,128)} custom-call(s32[128]{0:T(128)} %get-tuple-element.32.places, f32[12288,128]{1,0:T(8,128)} %update_front.1.base, f32[128,8,16,128]{3,2,1,0:T(8,128)} %all-to-all-done.5.tiles), custom_call_target="tpu_custom_call" | custom-call | tf_op jit(solution)/shard_map/add_tiles/pallas_call | solution.py:303
  (58 shorter events, 19.5 us)
Async XLA Ops:
  2.2 19.2 %copy-start.5 = (s32[128]{0:T(128)}, s32[128]{0:T(128)S(1)}, u32[]{:S(2)}) copy-start(s32[128]{0:T(128)S(1)} %get-tuple-element.44.slot) | copy-start | bytes 1540
  4.1 20.5 %all-to-all-start = ((s32[128,1,4]{2,1,0:T(1,128)}), s32[128,1,4]{2,1,0:T(1,128)S(1)}, u32[]{:S(2)}, u32[]{:S(2)}) async-start(s32[128,1,4]{2,1,0:T(1,128)} %copy.23), calls=%async_computation | async-start | bytes 131072 | tf_op jit(solution)/shard_map/all_to_all | solution.py:399
  24.6 43.6 %all-to-all-start.1 = ((f32[128,2,16,128]{3,2,1,0:T(8,128)}), f32[128,2,16,128]{3,2,1,0:T(8,128)S(1)}, u32[]{:S(2)}, u32[]{:S(2)}) async-start(f32[128,2,16,128]{3,2,1,0:T(8,128)} %bitcast.81), calls=%async_computation.1 | async-start | bytes 4194304 | tf_op jit(solution)/shard_map/all_to_all | solution.py:403
  37.9 25.3 %collective-permute-start = (f32[48,16,128]{2,1,0:T(8,128)}, f32[48,16,128]{2,1,0:T(8,128)S(1)}, u32[]{:S(2)}, u32[]{:S(2)}) collective-permute-start(f32[48,16,128]{2,1,0:T(8,128)} %get-tuple-element.19), channel_id=1, source_target_pairs={{0,1},{8,9},{16,17},{24,25},{32,33},{40,41},{48,49},{56,57},{64,65... | collective-permute-start | bytes 1179656 | tf_op jit(solution)/shard_map/ppermute | solution.py:408
  40.9 24.4 %collective-permute-start.1 = (f32[48,16,128]{2,1,0:T(8,128)}, f32[48,16,128]{2,1,0:T(8,128)S(1)}, u32[]{:S(2)}, u32[]{:S(2)}) collective-permute-start(f32[48,16,128]{2,1,0:T(8,128)} %get-tuple-element.20), channel_id=1, source_target_pairs={{0,7},{8,15},{16,23},{24,31},{32,39},{40,47},{48,55},{56,63},{64,7... | collective-permute-start | bytes 1179656 | tf_op jit(solution)/shard_map/ppermute | solution.py:408
  43.9 43.4 %collective-permute-start.2 = (f32[48,16,128]{2,1,0:T(8,128)}, f32[48,16,128]{2,1,0:T(8,128)S(1)}, u32[]{:S(2)}, u32[]{:S(2)}) collective-permute-start(f32[48,16,128]{2,1,0:T(8,128)} %get-tuple-element.21), channel_id=1, source_target_pairs={{0,4},{8,12},{16,20},{24,28},{32,36},{40,44},{48,52},{56,60},{64,6... | collective-permute-start | bytes 1179656 | tf_op jit(solution)/shard_map/ppermute | solution.py:408
  45.2 42.1 %collective-permute-start.3 = (f32[48,16,128]{2,1,0:T(8,128)}, f32[48,16,128]{2,1,0:T(8,128)}, u32[]{:S(2)}, u32[]{:S(2)}) collective-permute-start(f32[48,16,128]{2,1,0:T(8,128)} %get-tuple-element.22), channel_id=1, source_target_pairs={{0,5},{8,13},{16,21},{24,29},{32,37},{40,45},{48,53},{56,61},{64,6... | collective-permute-start | bytes 1179656 | tf_op jit(solution)/shard_map/ppermute | solution.py:408
  47.3 40.0 %collective-permute-start.4 = (f32[48,16,128]{2,1,0:T(8,128)}, f32[48,16,128]{2,1,0:T(8,128)}, u32[]{:S(2)}, u32[]{:S(2)}) collective-permute-start(f32[48,16,128]{2,1,0:T(8,128)} %get-tuple-element.23), channel_id=1, source_target_pairs={{0,2},{8,10},{16,18},{24,26},{32,34},{40,42},{48,50},{56,58},{64,6... | collective-permute-start | bytes 1179656 | tf_op jit(solution)/shard_map/ppermute | solution.py:408
  63.2 25.0 %copy-start.1 = (f32[48,16,128]{2,1,0:T(8,128)}, f32[48,16,128]{2,1,0:T(8,128)S(1)}, u32[]{:S(2)}) copy-start(f32[48,16,128]{2,1,0:T(8,128)S(1)} %collective-permute-done.refs_2_.refs_1_) | copy-start | bytes 1179652
  63.2 24.1 %collective-permute-start.5 = (f32[48,16,128]{2,1,0:T(8,128)}, f32[48,16,128]{2,1,0:T(8,128)}, u32[]{:S(2)}, u32[]{:S(2)}) collective-permute-start(f32[48,16,128]{2,1,0:T(8,128)} %get-tuple-element.24), channel_id=1, source_target_pairs={{0,3},{8,11},{16,19},{24,27},{32,35},{40,43},{48,51},{56,59},{64,6... | collective-permute-start | bytes 1179656 | tf_op jit(solution)/shard_map/ppermute | solution.py:408
  65.3 23.0 %copy-start.2 = (f32[48,16,128]{2,1,0:T(8,128)}, f32[48,16,128]{2,1,0:T(8,128)S(1)}, u32[]{:S(2)}) copy-start(f32[48,16,128]{2,1,0:T(8,128)S(1)} %collective-permute-done.1.refs_3_.refs_7_) | copy-start | bytes 1179652
  65.3 22.1 %collective-permute-start.6 = (f32[48,16,128]{2,1,0:T(8,128)}, f32[48,16,128]{2,1,0:T(8,128)}, u32[]{:S(2)}, u32[]{:S(2)}) collective-permute-start(f32[48,16,128]{2,1,0:T(8,128)} %get-tuple-element.25), channel_id=1, source_target_pairs={{0,6},{8,14},{16,22},{24,30},{32,38},{40,46},{48,54},{56,62},{64,7... | collective-permute-start | bytes 1179656 | tf_op jit(solution)/shard_map/ppermute | solution.py:408
  68.1 1.3 copy-start
  72.9 15.3 %all-to-all-start.2 = ((f32[16,16,128]{2,1,0:T(8,128)}), f32[16,16,128]{2,1,0:T(8,128)S(1)}, u32[]{:S(2)}, u32[]{:S(2)}) async-start(f32[16,16,128]{2,1,0:T(8,128)} %get-tuple-element.18), calls=%async_computation.2 | async-start | bytes 262144 | tf_op jit(solution)/shard_map/all_to_all | solution.py:410
  87.3 0.9 copy-start.3
  88.2 0.6 copy-start.4
  88.8 122.2 %all-to-all-start.3 = ((f32[128,8,16,128]{3,2,1,0:T(8,128)}), f32[128,8,16,128]{3,2,1,0:T(8,128)}, u32[]{:S(2)}, u32[]{:S(2)}) async-start(f32[128,8,16,128]{3,2,1,0:T(8,128)} %after.3), calls=%async_computation.3 | async-start | bytes 16777216 | tf_op jit(solution)/shard_map/all_to_all | solution.py:412
  254.0 112.1 %all-to-all-start.5 = ((f32[128,8,16,128]{3,2,1,0:T(8,128)}), f32[128,8,16,128]{3,2,1,0:T(8,128)}, u32[]{:S(2)}, u32[]{:S(2)}) async-start(f32[128,8,16,128]{3,2,1,0:T(8,128)} %after.5), calls=%async_computation.5 | async-start | bytes 16777216 | tf_op jit(solution)/shard_map/all_to_all | solution.py:415

commit v7 on v6

--- a/solution.py
+++ b/solution.py
@@ -231,11 +231,10 @@
     )(*parts, arrived)
 
 
-def spread_kernel(local, windows, column, *refs):
-    col_count = len(refs) - 3
-    own, (out, held, sem) = refs[:col_count], refs[col_count:]
+def join_kernel(local, windows, column, *refs):
+    own, (out, held, sem) = refs[:-3], refs[-3:]
     row_blocks = column.shape[0]
-    for k in range(col_count):
+    for k in range(len(own)):
 
         @pl.when(local[1] == k)
         def _():
@@ -243,19 +242,15 @@
             copy.start()
             copy.wait()
 
-    total = column[...] + held[...]
-    for k in range(col_count):
-        out[k, pl.ds(0, row_blocks)] = total
-        for i, j in enumerate((0, *range(k, windows.shape[0], col_count))):
-            out[k, row_blocks + i] = windows[j]
-
-
-def spread(local, windows, column, own):
+    out[pl.ds(0, row_blocks)] = column[...] + held[...]
+    out[pl.ds(row_blocks, windows.shape[0])] = windows[...]
+
+
+def join(local, windows, column, own):
     row_blocks, rows, size = column.shape
-    extra = 1 + windows.shape[0] // len(own)
-    out = jax.ShapeDtypeStruct((len(own), row_blocks + extra, rows, size), jnp.float32)
-    return pl.pallas_call(
-        spread_kernel,
+    out = jax.ShapeDtypeStruct((row_blocks + windows.shape[0], rows, size), jnp.float32)
+    return pl.pallas_call(
+        join_kernel,
         out_shape=out,
         in_specs=[pl.BlockSpec(memory_space=SMEM)]
         + [pl.BlockSpec(memory_space=VMEM)] * 2
@@ -263,7 +258,7 @@
         out_specs=pl.BlockSpec(memory_space=VMEM),
         scratch_shapes=[VMEM(column.shape, jnp.float32), pltpu.SemaphoreType.DMA],
         compiler_params=LIMIT,
-        name="spread",
+        name="join",
     )(local, windows, column, *own)
 
 
@@ -405,18 +400,26 @@
     own = list(split_front(local, flat_front, tiles, row_blocks))
     order = (1, 7, 4, 5, 2, 3, 6)
     for k in order:
-        own[k] = lax.ppermute(own[k], "col", [(0, k)])
+        late = order.index(k) >= 5
+        own[k] = lax.ppermute(after(own[k], sliced) if late else own[k], "col", [(0, k)])
+    sliced = after(sliced, first)
     windows, column = sum_slices(part, sliced, row_count, row_blocks)
     windows = lax.all_to_all(windows, "row", split_axis=0, concat_axis=0, tiled=True)
-    first = after(first, windows, *(own[k] for k in order))
+    column = join(local, windows, column, own)
+    first = after(first, column)
+    column = lax.all_gather(column, "col", axis=0)
     first = lax.all_to_all(first, both, split_axis=0, concat_axis=0, tiled=True)
-    column = after(spread(local, windows, column, own), first)
-    column = lax.all_to_all(column, "col", split_axis=0, concat_axis=0, tiled=True)
-    second = lax.all_to_all(
-        after(second, column), both, split_axis=0, concat_axis=0, tiled=True
-    )
-    corner = column[:, row_blocks].reshape(size, size)
-    window = jnp.swapaxes(column[:, row_blocks + 1 :], 0, 1).reshape(-1, size)
+    second = after(second, first)
+    second = lax.all_to_all(second, both, split_axis=0, concat_axis=0, tiled=True)
+
+    def block_of(j):
+        found = lax.dynamic_index_in_dim(column, row_blocks + j, axis=1, keepdims=False)
+        return found.reshape(size, size)
+
+    corner = block_of(0)
+    window = jnp.concatenate(
+        [block_of(m * col_count + col_index) for m in range(col_blocks)], axis=0
+    )
     factor = jnp.linalg.cholesky(0.5 * (corner + corner.T))
     inverse = jax.scipy.linalg.solve_triangular(
         factor, jnp.eye(size, dtype=jnp.float32), lower=True

time: 377 us -> 466 us (1.24)
  waiting for transfers between devices: 161 us -> 276 us
  blocking collectives: 42.9 us -> 0 us
  between operations: 0.45 us -> 13.8 us
    all_gather x0 -> x1, waiting for transfers between devices: none -> 139 us  [per_device(): column = lax.all_gather(column, 'col', axis=0)]
    all_to_all x1 -> x0, blocking collectives: 42.9 us -> none  [per_device(): lax.all_to_all(column, 'col', split_axis=0, concat_axis=0, tiled=True)]
    all_to_all x1, waiting for transfers between devices: 38.6 us -> 0.01 us  [per_device(): lax.all_to_all(second, both, split_axis=0, concat_axis=0, tiled=True)]
    ppermute x7, waiting for transfers between devices: 13.9 us -> 0.08 us  [per_device(): lax.ppermute(after(own[k], sliced) if late else own[k], 'col', [(0, k)])]
    all_to_all x1, waiting for transfers between devices: 0.01 us -> 13.1 us  [per_device(): lax.all_to_all(sliced, both, split_axis=0, concat_axis=0, tiled=True)]
    all_to_all x1, starting transfers between devices: 6.11 us -> 16.9 us  [per_device(): lax.all_to_all(second, both, split_axis=0, concat_axis=0, tiled=True)]
    all_to_all x1, waiting for transfers between devices: 0.88 us -> 7.92 us  [per_device(): lax.all_to_all(windows, 'row', split_axis=0, concat_axis=0, tiled=True)]
    all_to_all x1, starting transfers between devices: 13.4 us -> 7.28 us  [per_device(): first = lax.all_to_all(first, both, split_axis=0, concat_axis=0, tiled=True)]
  transfers between devices with their start and end apart: 12 -> 13, of which waited for: 5 -> 6; matrix products, arithmetic and copies ran while one was open for 8% -> 6% of each run, Pallas kernels for 18% -> 13%
where the time goes in v7:
time: 466 us; the launch traced here: 461 us
  waiting for transfers between devices  276 us (59%)
  Pallas kernels  76.1 us (16%)
  starting transfers between devices  63.1 us (14%)
  other arithmetic  27 us (6%)
  between operations  13.8 us (3%)
  local copies, waits for them, and re-layouts  4.9 us (1%)
    all_gather x1, waiting for transfers between devices, per_device(): column = lax.all_gather(column, 'col', axis=0)  139 us
    all_to_all x1, waiting for transfers between devices, per_device(): first = lax.all_to_all(first, both, split_axis=0, concat_axis=0, tiled=True)  109 us
    pallas_call x1, Pallas kernels, update_front(): pl.pallas_call(functools.partial(update_kernel, (row_count, row_blocks)),...  31.5 us
    pallas_call x2, Pallas kernels, add_tiles(): pl.pallas_call(functools.partial(add_kernel, chunks), out_shape=jax.Shape...  19.4 us
    all_to_all x1, starting transfers between devices, per_device(): lax.all_to_all(second, both, split_axis=0, concat_axis=0, tiled=True)  16.9 us
    ppermute x7, starting transfers between devices, per_device(): lax.ppermute(after(own[k], sliced) if late else own[k], 'col', [(0, k)])  13.8 us
    all_to_all x1, waiting for transfers between devices, per_device(): lax.all_to_all(sliced, both, split_axis=0, concat_axis=0, tiled=True)  13.1 us
    another operation x3, other arithmetic, per_device(): factor = jnp.linalg.cholesky(0.5 * (corner + corner.T))  12.4 us
  transfers between devices with their start and end apart: 13, of which 6 were waited for; matrix products, arithmetic and copies ran while one was open for 6% of the time, Pallas kernels for 13%

profile of v7, /device:TPU:0, one launch (start us, length us, event | category | flops | bytes accessed | tf_op | source)
XLA Modules:
  0.0 461.4 jit_solution(5099570209562062128)
XLA Ops:
  9.6 4.9 %pack_panel.1 = f32[16,8,2,16,128]{4,3,2,1,0:T(8,128)} custom-call(s32[32]{0:T(128)} %select_reduce_fusion.1.panel_tiles, s32[6]{0:T(128)} %pad_add_fusion.local.where, f32[128,8,16,128]{3,2,1,0:T(8,128)} %bitcast.75, f32[12288,128]{1,0:T(8,128)} %bitcast.78), custom_call_target="tpu_custom_call" | custom-call | tf_op jit(solution)/shard_map/pack_panel/pallas_call | solution.py:86
  14.5 11.1 %all-to-all-start.1 = ((f32[128,2,16,128]{3,2,1,0:T(8,128)}), f32[128,2,16,128]{3,2,1,0:T(8,128)S(1)}, u32[]{:S(2)}, u32[]{:S(2)}) async-start(f32[128,2,16,128]{3,2,1,0:T(8,128)} %bitcast.81), calls=%async_computation.1 | async-start | bytes 4194304 | tf_op jit(solution)/shard_map/all_to_all | solution.py:398
  25.6 6.4 %split_front.1 = (f32[48,16,128]{2,1,0:T(8,128)}, f32[48,16,128]{2,1,0:T(8,128)}, f32[48,16,128]{2,1,0:T(8,128)}, f32[48,16,128]{2,1,0:T(8,128)}, f32[48,16,128]...) custom-call(s32[6]{0:T(128)} %pad_add_fusion.local.where, ...), custom_call_target="tpu_custom_call" | custom-call | tf_op jit(solution)/shard_map/split_front/pallas_call | solution.py:182
  32.0 3.0 collective-permute-start
  37.8 2.6 collective-permute-start.4
  40.4 2.0 collective-permute-start.6
  42.9 13.1 %all-to-all-done.1.refs_0_.refs_1_ = f32[128,2,16,128]{3,2,1,0:T(8,128)S(1)} async-done(((f32[128,2,16,128]{3,2,1,0:T(8,128)}), f32[128,2,16,128]{3,2,1,0:T(8,128)S(1)}, u32[]{:S(2)}, u32[]{:S(2)}) %all-to-all-start.1) | async-done | bytes 2097184 | tf_op jit(solution)/shard_map/all_to_all | solution.py:398
  57.4 1.7 collective-permute-start.2
  61.7 6.5 %all-to-all-start = ((s32[128,1,4]{2,1,0:T(1,128)}), s32[128,1,4]{2,1,0:T(1,128)S(1)}, u32[]{:S(2)}, u32[]{:S(2)}) async-start(s32[128,1,4]{2,1,0:T(1,128)} %copy.19), calls=%async_computation | async-start | bytes 131072 | tf_op jit(solution)/shard_map/all_to_all | solution.py:394
  68.2 7.0 %pack.1 = (f32[128,8,16,128]{3,2,1,0:T(8,128)}, f32[128,8,16,128]{3,2,1,0:T(8,128)}) custom-call(s32[128]{0:T(128)} %copy-done.7, f32[128,8,16,128]{3,2,1,0:T(8,128)} %bitcast.77), custom_call_target="tpu_custom_call" | custom-call | tf_op jit(solution)/shard_map/pack/pallas_call | solution.py:138
  75.2 6.4 %all-to-all-done = s32[128,1,4]{2,1,0:T(1,128)S(1)} async-done(((s32[128,1,4]{2,1,0:T(1,128)}), s32[128,1,4]{2,1,0:T(1,128)S(1)}, u32[]{:S(2)}, u32[]{:S(2)}) %all-to-all-start) | async-done | bytes 2080 | tf_op jit(solution)/shard_map/all_to_all | solution.py:394
  82.5 3.9 sum_slices.1
  86.5 7.4 %all-to-all-start.2 = ((f32[16,16,128]{2,1,0:T(8,128)}), f32[16,16,128]{2,1,0:T(8,128)S(1)}, u32[]{:S(2)}, u32[]{:S(2)}) async-start(f32[16,16,128]{2,1,0:T(8,128)} %get-tuple-element.18), calls=%async_computation.2 | async-start | bytes 262144 | tf_op jit(solution)/shard_map/all_to_all | solution.py:407
  94.0 7.9 %all-to-all-done.2.windows = f32[16,16,128]{2,1,0:T(8,128)S(1)} async-done(((f32[16,16,128]{2,1,0:T(8,128)}), f32[16,16,128]{2,1,0:T(8,128)S(1)}, u32[]{:S(2)}, u32[]{:S(2)}) %all-to-all-start.2) | async-done | bytes 131104 | tf_op jit(solution)/shard_map/all_to_all | solution.py:407
  102.8 2.9 join.1.refs_1_
  105.7 7.3 %all-to-all-start.3 = ((f32[128,8,16,128]{3,2,1,0:T(8,128)}), f32[128,8,16,128]{3,2,1,0:T(8,128)}, u32[]{:S(2)}, u32[]{:S(2)}) async-start(f32[128,8,16,128]{3,2,1,0:T(8,128)} %after.8), calls=%async_computation.3 | async-start | bytes 16777216 | tf_op jit(solution)/shard_map/all_to_all | solution.py:411
  113.8 108.6 %all-to-all-done.3.tiles.refs_1_ = f32[128,8,16,128]{3,2,1,0:T(8,128)} async-done(((f32[128,8,16,128]{3,2,1,0:T(8,128)}), f32[128,8,16,128]{3,2,1,0:T(8,128)}, u32[]{:S(2)}, u32[]{:S(2)}) %all-to-all-start.3) | async-done | bytes 8388640 | tf_op jit(solution)/shard_map/all_to_all | solution.py:411
  222.4 16.9 %all-to-all-start.4 = ((f32[128,8,16,128]{3,2,1,0:T(8,128)}), f32[128,8,16,128]{3,2,1,0:T(8,128)}, u32[]{:S(2)}, u32[]{:S(2)}) async-start(f32[128,8,16,128]{3,2,1,0:T(8,128)} %after.9), calls=%async_computation.4 | async-start | bytes 16777216 | tf_op jit(solution)/shard_map/all_to_all | solution.py:413
  239.3 138.8 %all-gather.3.cloned.1.call-done = f32[512,16,128]{2,1,0:T(8,128)} async-done(((f32[64,16,128]{2,1,0:T(8,128)}), f32[512,16,128]{2,1,0:T(8,128)}) %all-gather.3.cloned.1.call-update) | async-done | bytes 4194320 | tf_op jit(solution)/shard_map/all_gather | solution.py:410
  379.3 11.7 %cholesky.14 = f32[128,128]{1,0:T(8,128)S(1)} custom-call(f32[128,128]{1,0:T(8,128)S(1)} %fusion.3), custom_call_target="Cholesky" | custom-call | tf_op jit(solution)/shard_map/jit(cholesky)/cholesky | solution.py:423
  392.3 9.8 %custom-call.7 = f32[1,128,128]{1,2,0:T(8,128)S(1)} custom-call(f32[1,128,128]{2,1,0:T(8,128)S(1)} %fusion), custom_call_target="InvertDiagBlocksLowerTriangular" | custom-call | tf_op jit(solution)/shard_map/jit(_solve_triangular)/triangular_solve | solution.py:424
  403.7 9.7 %add_tiles.2.front = f32[12288,128]{1,0:T(8,128)} custom-call(s32[128]{0:T(128)} %get-tuple-element.31.places, f32[12288,128]{1,0:T(8,128)} %bitcast.80, f32[128,8,16,128]{3,2,1,0:T(8,128)} %all-to-all-done.3.tiles.refs_1_), custom_call_target="tpu_custom_call" | custom-call | tf_op jit(solution)/shard_map/add_tiles/pallas_call | solution.py:298
  413.3 31.5 %update_front.1.base = f32[12288,128]{1,0:T(8,128)} custom-call(s32[6]{0:T(128)} %pad_add_fusion.local.where, f32[12288,128]{1,0:T(8,128)} %add_tiles.2.front, f32[128,128]{1,0:T(8,128)} %fusion.1.inverse_t, f32[256,128]{1,0:T(8,128)} %pad_maximum_fusion.window, f32[8,64,16,128]{3,2,1,0:T(8,128)} %bitcast.83), custom_call_target="tpu_custom_call" | custom-call | tf_op jit(solution)/shard_map/update_front/pallas_call | solution.py:349
  444.8 9.7 %add_tiles.3 = f32[12288,128]{1,0:T(8,128)} custom-call(s32[128]{0:T(128)} %get-tuple-element.32.places, f32[12288,128]{1,0:T(8,128)} %update_front.1.base, f32[128,8,16,128]{3,2,1,0:T(8,128)} %all-to-all-done.4.tiles), custom_call_target="tpu_custom_call" | custom-call | tf_op jit(solution)/shard_map/add_tiles/pallas_call | solution.py:298
  (70 shorter events, 16.5 us)
Async XLA Ops:
  7.4 7.1 %copy-start.7 = (s32[128]{0:T(128)}, s32[128]{0:T(128)S(1)}, u32[]{:S(2)}) copy-start(s32[128]{0:T(128)S(1)} %multiply_add_fusion.slot) | copy-start | bytes 1540
  14.5 41.5 %all-to-all-start.1 = ((f32[128,2,16,128]{3,2,1,0:T(8,128)}), f32[128,2,16,128]{3,2,1,0:T(8,128)S(1)}, u32[]{:S(2)}, u32[]{:S(2)}) async-start(f32[128,2,16,128]{3,2,1,0:T(8,128)} %bitcast.81), calls=%async_computation.1 | async-start | bytes 4194304 | tf_op jit(solution)/shard_map/all_to_all | solution.py:398
  25.6 16.9 %copy-start.8 = (s32[1,1,128]{2,1,0:T(1,128)S(1)}, s32[1,1,128]{2,1,0:T(1,128)}, u32[]{:S(2)}) copy-start(s32[1,1,128]{2,1,0:T(1,128)} %param.7) | copy-start | bytes 1540
  25.6 16.9 %copy-start.9 = (s32[1,1,128]{2,1,0:T(1,128)S(1)}, s32[1,1,128]{2,1,0:T(1,128)}, u32[]{:S(2)}) copy-start(s32[1,1,128]{2,1,0:T(1,128)} %param.6) | copy-start | bytes 1540
  32.0 25.4 %collective-permute-start = (f32[48,16,128]{2,1,0:T(8,128)}, f32[48,16,128]{2,1,0:T(8,128)S(1)}, u32[]{:S(2)}, u32[]{:S(2)}) collective-permute-start(f32[48,16,128]{2,1,0:T(8,128)} %get-tuple-element.21), channel_id=1, source_target_pairs={{0,1},{8,9},{16,17},{24,25},{32,33},{40,41},{48,49},{56,57},{64,65... | collective-permute-start | bytes 1179656 | tf_op jit(solution)/shard_map/ppermute | solution.py:404
  35.0 24.1 %collective-permute-start.1 = (f32[48,16,128]{2,1,0:T(8,128)}, f32[48,16,128]{2,1,0:T(8,128)S(1)}, u32[]{:S(2)}, u32[]{:S(2)}) collective-permute-start(f32[48,16,128]{2,1,0:T(8,128)} %get-tuple-element.22), channel_id=1, source_target_pairs={{0,2},{8,10},{16,18},{24,26},{32,34},{40,42},{48,50},{56,58},{64,6... | collective-permute-start | bytes 1179656 | tf_op jit(solution)/shard_map/ppermute | solution.py:404
  36.3 57.6 %collective-permute-start.3 = (f32[48,16,128]{2,1,0:T(8,128)}, f32[48,16,128]{2,1,0:T(8,128)S(1)}, u32[]{:S(2)}, u32[]{:S(2)}) collective-permute-start(f32[48,16,128]{2,1,0:T(8,128)} %get-tuple-element.24), channel_id=1, source_target_pairs={{0,4},{8,12},{16,20},{24,28},{32,36},{40,44},{48,52},{56,60},{64,6... | collective-permute-start | bytes 1179656 | tf_op jit(solution)/shard_map/ppermute | solution.py:404
  37.8 56.1 %collective-permute-start.4 = (f32[48,16,128]{2,1,0:T(8,128)}, f32[48,16,128]{2,1,0:T(8,128)}, u32[]{:S(2)}, u32[]{:S(2)}) collective-permute-start(f32[48,16,128]{2,1,0:T(8,128)} %get-tuple-element.25), channel_id=1, source_target_pairs={{0,5},{8,13},{16,21},{24,29},{32,37},{40,45},{48,53},{56,61},{64,6... | collective-permute-start | bytes 1179656 | tf_op jit(solution)/shard_map/ppermute | solution.py:404
  40.4 53.6 %collective-permute-start.6 = (f32[48,16,128]{2,1,0:T(8,128)}, f32[48,16,128]{2,1,0:T(8,128)}, u32[]{:S(2)}, u32[]{:S(2)}) collective-permute-start(f32[48,16,128]{2,1,0:T(8,128)} %get-tuple-element.27), channel_id=1, source_target_pairs={{0,7},{8,15},{16,23},{24,31},{32,39},{40,47},{48,55},{56,63},{64,7... | collective-permute-start | bytes 1179656 | tf_op jit(solution)/shard_map/ppermute | solution.py:404
  56.0 1.3 copy-start
  57.4 25.1 %copy-start.2 = (f32[48,16,128]{2,1,0:T(8,128)}, f32[48,16,128]{2,1,0:T(8,128)S(1)}, u32[]{:S(2)}) copy-start(f32[48,16,128]{2,1,0:T(8,128)S(1)} %collective-permute-done.refs_1_) | copy-start | bytes 1179652
  57.4 44.5 %collective-permute-start.2 = (f32[48,16,128]{2,1,0:T(8,128)}, f32[48,16,128]{2,1,0:T(8,128)S(1)}, u32[]{:S(2)}, u32[]{:S(2)}) collective-permute-start(f32[48,16,128]{2,1,0:T(8,128)} %after.6), channel_id=1, source_target_pairs={{0,3},{8,11},{16,19},{24,27},{32,35},{40,43},{48,51},{56,59},{64,6... | collective-permute-start | bytes 1179656 | tf_op jit(solution)/shard_map/ppermute | solution.py:404
  59.1 23.4 %copy-start.3 = (f32[48,16,128]{2,1,0:T(8,128)}, f32[48,16,128]{2,1,0:T(8,128)S(1)}, u32[]{:S(2)}) copy-start(f32[48,16,128]{2,1,0:T(8,128)S(1)} %collective-permute-done.1.refs_2_) | copy-start | bytes 1179652
  59.2 42.7 %collective-permute-start.5 = (f32[48,16,128]{2,1,0:T(8,128)}, f32[48,16,128]{2,1,0:T(8,128)S(1)}, u32[]{:S(2)}, u32[]{:S(2)}) collective-permute-start(f32[48,16,128]{2,1,0:T(8,128)} %after.7), channel_id=1, source_target_pairs={{0,6},{8,14},{16,22},{24,30},{32,38},{40,46},{48,54},{56,62},{64,7... | collective-permute-start | bytes 1179656 | tf_op jit(solution)/shard_map/ppermute | solution.py:404
  61.7 20.0 %all-to-all-start = ((s32[128,1,4]{2,1,0:T(1,128)}), s32[128,1,4]{2,1,0:T(1,128)S(1)}, u32[]{:S(2)}, u32[]{:S(2)}) async-start(s32[128,1,4]{2,1,0:T(1,128)} %copy.19), calls=%async_computation | async-start | bytes 131072 | tf_op jit(solution)/shard_map/all_to_all | solution.py:394
  86.5 15.4 %all-to-all-start.2 = ((f32[16,16,128]{2,1,0:T(8,128)}), f32[16,16,128]{2,1,0:T(8,128)S(1)}, u32[]{:S(2)}, u32[]{:S(2)}) async-start(f32[16,16,128]{2,1,0:T(8,128)} %get-tuple-element.18), calls=%async_computation.2 | async-start | bytes 262144 | tf_op jit(solution)/shard_map/all_to_all | solution.py:407
  93.9 8.0 %copy-start.4 = (f32[48,16,128]{2,1,0:T(8,128)}, f32[48,16,128]{2,1,0:T(8,128)S(1)}, u32[]{:S(2)}) copy-start(f32[48,16,128]{2,1,0:T(8,128)S(1)} %collective-permute-done.3.refs_4_) | copy-start | bytes 1179652
  101.9 0.6 copy-start.1
  101.9 0.8 copy-start.5
  101.9 0.9 copy-start.6
  105.7 116.6 %all-to-all-start.3 = ((f32[128,8,16,128]{3,2,1,0:T(8,128)}), f32[128,8,16,128]{3,2,1,0:T(8,128)}, u32[]{:S(2)}, u32[]{:S(2)}) async-start(f32[128,8,16,128]{3,2,1,0:T(8,128)} %after.8), calls=%async_computation.3 | async-start | bytes 16777216 | tf_op jit(solution)/shard_map/all_to_all | solution.py:411
  113.0 265.1 %all-gather.3.cloned.1.call-start = ((), (), s32[]{:S(2)}) async-start(), calls=%async_computation.5 | async-start | bytes 4718592 | tf_op jit(solution)/shard_map/all_gather | solution.py:410
  222.4 222.4 %all-to-all-start.4 = ((f32[128,8,16,128]{3,2,1,0:T(8,128)}), f32[128,8,16,128]{3,2,1,0:T(8,128)}, u32[]{:S(2)}, u32[]{:S(2)}) async-start(f32[128,8,16,128]{3,2,1,0:T(8,128)} %after.9), calls=%async_computation.4 | async-start | bytes 16777216 | tf_op jit(solution)/shard_map/all_to_all | solution.py:413
Sparse Core Ops, SparseCore 0:
  115.5 262.5 all-gather.2

commit v8 on v6

--- a/solution.py
+++ b/solution.py
@@ -45,11 +45,15 @@
     return slot, panel_tiles, message, jnp.concatenate([where, stay_tiles, stay_blocks])
 
 
-def pack_panel_kernel(panel_tiles, local, tiles, front, out, held, corner, block, load_sem, corner_sem, sem):
-    parts, rows, size = block.shape
+def pack_panel_kernel(
+    panel_tiles, local, places, tiles, front, out, held, corner, block, load_sem, corner_sem, sem
+):
+    size = block.shape[-1]
     slots = held.shape[0]
     row_count = out.shape[0]
-    load_corner = pltpu.make_async_copy(front.at[pl.ds(0, 2 * parts * rows)], corner, corner_sem)
+    groups = block.shape[1]
+    pltpu.make_async_copy(places, out.at[:, :, CAP * groups], sem).start()
+    load_corner = pltpu.make_async_copy(front.at[pl.ds(0, 2 * size)], corner, corner_sem)
     load_corner.start()
     loads = [
         pltpu.make_async_copy(tiles.at[panel_tiles[i]], held.at[i], load_sem.at[i])
@@ -58,7 +62,7 @@
     for load in loads:
         load.start()
     load_corner.wait()
-    block[...] = corner[pl.ds(0, parts * rows, stride=2), :].reshape(block.shape)
+    block[...] = corner[pl.ds(0, size, stride=2), :].reshape(block.shape)
     for r in range(row_count):
         mine = (local[0] == r) & (local[1] == 0)
         for s in range(CAP):
@@ -75,30 +79,42 @@
             held[r * CAP] = block[...]
 
         for s in range(CAP):
-            pltpu.make_async_copy(held.at[r * CAP + s], out.at[r, :, s], sem).start()
-    whole = pltpu.make_async_copy(out, out, sem)
-    whole.wait()
-
-
-def pack_panel(panel_tiles, local, tiles, front, row_count):
-    count, parts, rows, size = tiles.shape
+            pltpu.make_async_copy(
+                held.at[r * CAP + s], out.at[r, :, pl.ds(s * groups, groups)], sem
+            ).start()
+    pltpu.make_async_copy(out, out, sem).wait()
+
+
+def pack_panel(panel_tiles, local, message, tiles, front, row_count, col_count):
+    size = tiles.shape[-1]
+    rows = size // col_count
+    groups = rows // 8
     slots = row_count * CAP
-    return pl.pallas_call(
+    view = (col_count, groups, 8, size)
+    places = jnp.pad(
+        message.astype(jnp.float32)[:, None, :], ((0, 0), (0, 7), (0, size - message.shape[1]))
+    ).reshape(row_count, col_count, 8, size)
+    sent = pl.pallas_call(
         pack_panel_kernel,
-        out_shape=jax.ShapeDtypeStruct((row_count, parts, CAP, rows, size), jnp.float32),
-        in_specs=[pl.BlockSpec(memory_space=SMEM)] * 2 + [pl.BlockSpec(memory_space=ANY)] * 2,
+        out_shape=jax.ShapeDtypeStruct(
+            (row_count, col_count, CAP * groups + 1, 8, size), jnp.float32
+        ),
+        in_specs=[pl.BlockSpec(memory_space=SMEM)] * 2
+        + [pl.BlockSpec(memory_space=VMEM)]
+        + [pl.BlockSpec(memory_space=ANY)] * 2,
         out_specs=pl.BlockSpec(memory_space=ANY),
         scratch_shapes=[
-            VMEM((slots, parts, rows, size), jnp.float32),
-            VMEM((2 * parts * rows, size), jnp.float32),
-            VMEM((parts, rows, size), jnp.float32),
+            VMEM((slots,) + view, jnp.float32),
+            VMEM((2 * size, size), jnp.float32),
+            VMEM(view, jnp.float32),
             pltpu.SemaphoreType.DMA((slots,)),
             pltpu.SemaphoreType.DMA,
             pltpu.SemaphoreType.DMA,
         ],
         compiler_params=LIMIT,
         name="pack_panel",
-    )(panel_tiles, local, tiles, front)
+    )(panel_tiles, local, places, tiles.reshape((-1,) + view), front)
+    return sent.reshape((row_count * col_count,) + sent.shape[2:])
 
 
 def pack_kernel(chunks, slot, tiles, first, second, held, load_sem, main_sem):
@@ -200,11 +216,14 @@
 def slices_kernel(row_blocks, part_0, part_1, arrived, windows, column, total):
     total[...] = jnp.zeros_like(total)
     parts = (part_0, part_1)
+    groups = arrived.shape[1] // CAP
+    rows, size = total.shape[1:]
 
     def source(d, carry):
         for s in range(CAP):
             block = parts[s][d]
-            total[jnp.where(block < 0, row_blocks, block)] += arrived[d, s]
+            piece = arrived[d, pl.ds(s * groups, groups)].reshape(rows, size)
+            total[jnp.where(block < 0, row_blocks, block)] += piece
         return carry
 
     lax.fori_loop(0, arrived.shape[0], source, 0, unroll=8)
@@ -213,7 +232,9 @@
 
 
 def sum_slices(parts, arrived, row_count, row_blocks):
-    devices, _, rows, size = arrived.shape
+    devices, groups, _, size = arrived.shape
+    groups = groups // CAP
+    rows = groups * 8
     outs = [
         jax.ShapeDtypeStruct((row_count, rows, size), jnp.float32),
         jax.ShapeDtypeStruct((row_blocks, rows, size), jnp.float32),
@@ -223,7 +244,7 @@
         out_shape=outs,
         grid=(1,),
         in_specs=[pl.BlockSpec(memory_space=SMEM)] * 2
-        + [pl.BlockSpec((devices, CAP, rows, size), lambda i: (0, 0, 0, 0))],
+        + [pl.BlockSpec((devices, CAP * groups, 8, size), lambda i: (0, 0, 0, 0))],
         out_specs=[pl.BlockSpec(out.shape, lambda i: (0, 0, 0)) for out in outs],
         scratch_shapes=[VMEM((row_blocks + 1, rows, size), jnp.float32)],
         compiler_params=LIMIT,
@@ -232,36 +253,56 @@
 
 
 def spread_kernel(local, windows, column, *refs):
-    col_count = len(refs) - 3
-    own, (out, held, sem) = refs[:col_count], refs[col_count:]
+    own, (out, held, load_sem, sem, few_sem) = refs[:-5], refs[-5:]
+    col_count = len(own)
     row_blocks = column.shape[0]
+    few = []
+    for k in range(col_count):
+        for i, j in enumerate((0, *range(k, windows.shape[0], col_count))):
+            few.append(
+                pltpu.make_async_copy(
+                    windows.at[j], out.at[k, row_blocks + i], few_sem.at[len(few)]
+                )
+            )
+    for copy in few:
+        copy.start()
     for k in range(col_count):
 
         @pl.when(local[1] == k)
         def _():
-            copy = pltpu.make_async_copy(own[k], held, sem)
-            copy.start()
-            copy.wait()
-
-    total = column[...] + held[...]
-    for k in range(col_count):
-        out[k, pl.ds(0, row_blocks)] = total
-        for i, j in enumerate((0, *range(k, windows.shape[0], col_count))):
-            out[k, row_blocks + i] = windows[j]
+            load = pltpu.make_async_copy(own[k], held, load_sem)
+            load.start()
+            load.wait()
+
+    held[...] += column[...]
+    copies = [
+        pltpu.make_async_copy(held, out.at[k, pl.ds(0, row_blocks)], sem.at[k])
+        for k in range(col_count)
+    ]
+    for copy in copies:
+        copy.start()
+    for copy in copies + few:
+        copy.wait()
 
 
 def spread(local, windows, column, own):
     row_blocks, rows, size = column.shape
-    extra = 1 + windows.shape[0] // len(own)
-    out = jax.ShapeDtypeStruct((len(own), row_blocks + extra, rows, size), jnp.float32)
+    col_count = len(own)
+    extra = 1 + windows.shape[0] // col_count
+    out = jax.ShapeDtypeStruct((col_count, row_blocks + extra, rows, size), jnp.float32)
     return pl.pallas_call(
         spread_kernel,
         out_shape=out,
         in_specs=[pl.BlockSpec(memory_space=SMEM)]
         + [pl.BlockSpec(memory_space=VMEM)] * 2
-        + [pl.BlockSpec(memory_space=ANY)] * len(own),
-        out_specs=pl.BlockSpec(memory_space=VMEM),
-        scratch_shapes=[VMEM(column.shape, jnp.float32), pltpu.SemaphoreType.DMA],
+        + [pl.BlockSpec(memory_space=ANY)] * col_count,
+        out_specs=pl.BlockSpec(memory_space=ANY),
+        scratch_shapes=[
+            VMEM(column.shape, jnp.float32),
+            pltpu.SemaphoreType.DMA,
+            pltpu.SemaphoreType.DMA((col_count,)),
+            pltpu.SemaphoreType.DMA((col_count * extra,)),
+        ],
         compiler_params=LIMIT,
         name="spread",
     )(local, windows, column, *own)
@@ -396,21 +437,21 @@
         col_count,
         size,
     )
-    message = lax.all_to_all(message, both, split_axis=0, concat_axis=0, tiled=True)
+    first, second = pack(slot, tiles, devices)
+    first = lax.all_to_all(first, both, split_axis=0, concat_axis=0, tiled=True)
+    own = list(split_front(local, flat_front, tiles, row_blocks))
+    for k in (7, 2, 4, 5, 3):
+        own[k] = lax.ppermute(own[k], "col", [(0, k)])
+    sliced = pack_panel(panel_tiles, local, message, tiles, flat_front, row_count, col_count)
+    sliced = after(sliced, first)
+    sliced = lax.all_to_all(sliced, both, split_axis=0, concat_axis=0, tiled=True)
+    message = sliced[:, -1, 0, : 2 * CAP].astype(jnp.int32)
     main, part = ([message[:, h * CAP + s] for s in range(CAP)] for h in range(2))
-    sliced = pack_panel(panel_tiles, local, tiles, flat_front, row_count)
-    sliced = sliced.reshape((devices,) + sliced.shape[2:])
-    sliced = lax.all_to_all(sliced, both, split_axis=0, concat_axis=0, tiled=True)
-    first, second = pack(slot, tiles, devices)
-    own = list(split_front(local, flat_front, tiles, row_blocks))
-    order = (1, 7, 4, 5, 2, 3, 6)
-    for k in order:
-        own[k] = lax.ppermute(own[k], "col", [(0, k)])
     windows, column = sum_slices(part, sliced, row_count, row_blocks)
+    for k in (1, 6):
+        own[k] = lax.ppermute(after(own[k], column), "col", [(0, k)])
     windows = lax.all_to_all(windows, "row", split_axis=0, concat_axis=0, tiled=True)
-    first = after(first, windows, *(own[k] for k in order))
-    first = lax.all_to_all(first, both, split_axis=0, concat_axis=0, tiled=True)
-    column = after(spread(local, windows, column, own), first)
+    column = spread(local, windows, column, own)
     column = lax.all_to_all(column, "col", split_axis=0, concat_axis=0, tiled=True)
     second = lax.all_to_all(
         after(second, column), both, split_axis=0, concat_axis=0, tiled=True

time: 377 us -> 373 us (0.989)
  starting transfers between devices: 60.4 us -> 49 us
  waiting for transfers between devices: 161 us -> 167 us
    all_to_all x1, waiting for transfers between devices: 0.01 us -> 18.5 us  [per_device(): lax.all_to_all(sliced, both, split_axis=0, concat_axis=0, tiled=True)]
    all_to_all x1 -> x0, starting transfers between devices: 11.2 us -> none  [per_device(): lax.all_to_all(message, both, split_axis=0, concat_axis=0, tiled=True)]
    ppermute x7 -> x5, waiting for transfers between devices: 13.9 us -> 8.76 us  [per_device(): own[k] = lax.ppermute(own[k], 'col', [(0, k)])]
    all_to_all x1, starting transfers between devices: 6.11 us -> 10.6 us  [per_device(): lax.all_to_all(after(second, column), both, split_axis=0, concat_axis=0,...]
    ppermute x7 -> x5, starting transfers between devices: 15.5 us -> 11.1 us  [per_device(): own[k] = lax.ppermute(own[k], 'col', [(0, k)])]
    all_to_all x1, waiting for transfers between devices: 105 us -> 100 us  [per_device(): first = lax.all_to_all(first, both, split_axis=0, concat_axis=0, tiled=True)]
    ppermute x0 -> x2, starting transfers between devices: none -> 4.07 us  [per_device(): own[k] = lax.ppermute(after(own[k], column), 'col', [(0, k)])]
  transfers between devices with their start and end apart: 12 -> 11, of which waited for: 5 -> 7; matrix products, arithmetic and copies ran while one was open for 8% -> 8% of each run, Pallas kernels for 18% -> 15%
where the time goes in v8:
time: 373 us; the launch traced here: 372 us
  waiting for transfers between devices  167 us (45%)
  Pallas kernels  77.5 us (21%)
  starting transfers between devices  49 us (13%)
  blocking collectives  45.1 us (12%)
  other arithmetic  26.4 us (7%)
  local copies, waits for them, and re-layouts  6.03 us (2%)
    all_to_all x1, waiting for transfers between devices, per_device(): first = lax.all_to_all(first, both, split_axis=0, concat_axis=0, tiled=True)  100 us
    all_to_all x1, blocking collectives, per_device(): lax.all_to_all(column, 'col', split_axis=0, concat_axis=0, tiled=True)  45.1 us
    all_to_all x1, waiting for transfers between devices, per_device(): lax.all_to_all(after(second, column), both, split_axis=0, concat_axis=0,...  38.6 us
    pallas_call x1, Pallas kernels, update_front(): pl.pallas_call(functools.partial(update_kernel, (row_count, row_blocks)),...  31.2 us
    pallas_call x2, Pallas kernels, add_tiles(): pl.pallas_call(functools.partial(add_kernel, chunks), out_shape=jax.Shape...  19.4 us
    all_to_all x1, waiting for transfers between devices, per_device(): lax.all_to_all(sliced, both, split_axis=0, concat_axis=0, tiled=True)  18.5 us
    another operation x3, other arithmetic, per_device(): factor = jnp.linalg.cholesky(0.5 * (corner + corner.T))  12.5 us
    all_to_all x1, starting transfers between devices, per_device(): first = lax.all_to_all(first, both, split_axis=0, concat_axis=0, tiled=True)  11.7 us
  transfers between devices with their start and end apart: 11, of which 7 were waited for; matrix products, arithmetic and copies ran while one was open for 8% of the time, Pallas kernels for 15%

profile of v8, /device:TPU:0, one launch (start us, length us, event | category | flops | bytes accessed | tf_op | source)
XLA Modules:
  0.0 372.0 jit_solution(10418520540313131946)
XLA Ops:
  1.4 7.0 %pack.1 = (f32[128,8,16,128]{3,2,1,0:T(8,128)}, f32[128,8,16,128]{3,2,1,0:T(8,128)}) custom-call(s32[128]{0:T(128)} %get-tuple-element.44.slot, f32[128,8,16,128]{3,2,1,0:T(8,128)} %bitcast.79), custom_call_target="tpu_custom_call" | custom-call | tf_op jit(solution)/shard_map/pack/pallas_call | solution.py:154
  8.5 11.7 %all-to-all-start = ((f32[128,8,16,128]{3,2,1,0:T(8,128)}), f32[128,8,16,128]{3,2,1,0:T(8,128)}, u32[]{:S(2)}, u32[]{:S(2)}) async-start(f32[128,8,16,128]{3,2,1,0:T(8,128)} %get-tuple-element.17), calls=%async_computation | async-start | bytes 16777216 | tf_op jit(solution)/shard_map/all_to_all | solution.py:441
  23.3 5.2 %pack_panel.1 = f32[16,8,5,8,128]{4,3,2,1,0:T(8,128)} custom-call(s32[32]{0:T(128)} %select_reduce_fusion.1.panel_tiles, s32[6]{0:T(128)} %pad_add_fusion.local.where, f32[16,8,8,128]{3,2,1,0:T(8,128)} %bitcast.86, f32[128,8,2,8,128]{4,3,2,1,0:T(8,128)} %bitcast.80, f32[12288,128]{1,0:T(8,128)} %bitcast.82), custom_call_target="tpu_custom_call" | custom-call | tf_op jit(solution)/shard_map/pack_panel/pallas_call | solution.py:97
  28.5 100.5 %all-to-all-done.refs_1_.tiles = f32[128,8,16,128]{3,2,1,0:T(8,128)} async-done(((f32[128,8,16,128]{3,2,1,0:T(8,128)}), f32[128,8,16,128]{3,2,1,0:T(8,128)}, u32[]{:S(2)}, u32[]{:S(2)}) %all-to-all-start) | async-done | bytes 8388640 | tf_op jit(solution)/shard_map/all_to_all | solution.py:441
  129.0 4.9 %all-to-all-start.1 = ((f32[128,5,8,128]{3,2,1,0:T(8,128)}), f32[128,5,8,128]{3,2,1,0:T(8,128)S(1)}, u32[]{:S(2)}, u32[]{:S(2)}) async-start(f32[128,5,8,128]{3,2,1,0:T(8,128)} %after.4), calls=%async_computation.1 | async-start | bytes 5242880 | tf_op jit(solution)/shard_map/all_to_all | solution.py:447
  133.9 6.4 %split_front.1 = (f32[48,16,128]{2,1,0:T(8,128)}, f32[48,16,128]{2,1,0:T(8,128)}, f32[48,16,128]{2,1,0:T(8,128)}, f32[48,16,128]{2,1,0:T(8,128)}, f32[48,16,128]...) custom-call(s32[6]{0:T(128)} %pad_add_fusion.local.where, ...), custom_call_target="tpu_custom_call" | custom-call | tf_op jit(solution)/shard_map/split_front/pallas_call | solution.py:198
  140.3 2.9 collective-permute-start.1
  145.0 2.0 collective-permute-start.3
  147.0 2.3 collective-permute-start.4
  149.4 2.0 collective-permute-start.6
  151.4 18.5 %all-to-all-done.1.arrived = f32[128,5,8,128]{3,2,1,0:T(8,128)S(1)} async-done(((f32[128,5,8,128]{3,2,1,0:T(8,128)}), f32[128,5,8,128]{3,2,1,0:T(8,128)S(1)}, u32[]{:S(2)}, u32[]{:S(2)}) %all-to-all-start.1) | async-done | bytes 2621472 | tf_op jit(solution)/shard_map/all_to_all | solution.py:447
  171.4 4.0 %sum_slices.1 = (f32[16,16,128]{2,1,0:T(8,128)}, f32[48,16,128]{2,1,0:T(8,128)}) custom-call(s32[128]{0:T(128)} %get-tuple-element.30.part_0, s32[128]{0:T(128)} %get-tuple-element.29.part_1, f32[128,5,8,128]{3,2,1,0:T(8,128)} %copy-done), custom_call_target="tpu_custom_call" | custom-call | tf_op jit(solution)/shard_map/sum_slices/pallas_call | solution.py:242
  175.5 2.8 collective-permute-start
  180.6 6.6 %all-to-all-start.2 = ((f32[16,16,128]{2,1,0:T(8,128)}), f32[16,16,128]{2,1,0:T(8,128)S(1)}, u32[]{:S(2)}, u32[]{:S(2)}) async-start(f32[16,16,128]{2,1,0:T(8,128)} %get-tuple-element.18), calls=%async_computation.2 | async-start | bytes 262144 | tf_op jit(solution)/shard_map/all_to_all | solution.py:453
  187.7 7.2 %collective-permute-done.4.refs_5_ = f32[48,16,128]{2,1,0:T(8,128)} collective-permute-done((f32[48,16,128]{2,1,0:T(8,128)}, f32[48,16,128]{2,1,0:T(8,128)}, u32[]{:S(2)}, u32[]{:S(2)}) %collective-permute-start.4) | collective-permute-done | bytes 393248 | tf_op jit(solution)/shard_map/ppermute | solution.py:444
  196.2 4.2 %spread.1 = f32[8,51,16,128]{3,2,1,0:T(8,128)} custom-call(s32[6]{0:T(128)} %pad_add_fusion.local.where, f32[16,16,128]{2,1,0:T(8,128)} %copy-done.1, f32[48,16,128]{2,1,0:T(8,128)} %get-tuple-element.19.refs_1_.column, f32[48,16,128]{2,1,0:T(8,128)} %get-tuple-element.20.refs_0_, f32[48,16,128]{2,1,0:T(8,128)} %copy-done.4, f32[48,16,128]{2,1,0:T(8,128)} %copy-done.2, ...), custom_call_target="tpu_custom_call" | custom-call | tf_op jit(solution)/shard_map/spread/pallas_call | solution.py:293
  200.4 45.1 %all_to_all.25.column.refs_1_ = f32[8,51,16,128]{3,2,1,0:T(8,128)} all-to-all(f32[8,51,16,128]{3,2,1,0:T(8,128)} %spread.1), channel_id=1, replica_groups=mesh['row'=16,'col'=8] {'col'}, dimensions={0} | all-to-all | bytes 6684672 | tf_op jit(solution)/shard_map/all_to_all | solution.py:455
  245.5 10.6 %all-to-all-start.4 = ((f32[128,8,16,128]{3,2,1,0:T(8,128)}), f32[128,8,16,128]{3,2,1,0:T(8,128)}, u32[]{:S(2)}, u32[]{:S(2)}) async-start(f32[128,8,16,128]{3,2,1,0:T(8,128)} %after.7), calls=%async_computation.4 | async-start | bytes 16777216 | tf_op jit(solution)/shard_map/all_to_all | solution.py:456
  256.1 9.7 %add_tiles.2.front = f32[12288,128]{1,0:T(8,128)} custom-call(s32[128]{0:T(128)} %get-tuple-element.31.places, f32[12288,128]{1,0:T(8,128)} %bitcast.84, f32[128,8,16,128]{3,2,1,0:T(8,128)} %all-to-all-done.refs_1_.tiles), custom_call_target="tpu_custom_call" | custom-call | tf_op jit(solution)/shard_map/add_tiles/pallas_call | solution.py:344
  266.9 11.7 %cholesky.14 = f32[128,128]{1,0:T(8,128)S(1)} custom-call(f32[128,128]{1,0:T(8,128)S(1)} %fusion.3), custom_call_target="Cholesky" | custom-call | tf_op jit(solution)/shard_map/jit(cholesky)/cholesky | solution.py:461
  280.0 9.8 %custom-call.7 = f32[1,128,128]{1,2,0:T(8,128)S(1)} custom-call(f32[1,128,128]{2,1,0:T(8,128)S(1)} %fusion), custom_call_target="InvertDiagBlocksLowerTriangular" | custom-call | tf_op jit(solution)/shard_map/jit(_solve_triangular)/triangular_solve | solution.py:462
  292.3 31.2 %update_front.1.base = f32[12288,128]{1,0:T(8,128)} custom-call(s32[6]{0:T(128)} %pad_add_fusion.local.where, f32[12288,128]{1,0:T(8,128)} %add_tiles.2.front, f32[128,128]{1,0:T(8,128)} %fusion.1.inverse_t, f32[256,128]{1,0:T(8,128)} %bitcast.89, f32[8,51,16,128]{3,2,1,0:T(8,128)} %all_to_all.25.column.refs_1_), custom_call_target="tpu_custom_call" | custom-call | tf_op jit(solution)/shard_map/update_front/pallas_call | solution.py:395
  323.5 38.6 %all-to-all-done.4.tiles = f32[128,8,16,128]{3,2,1,0:T(8,128)} async-done(((f32[128,8,16,128]{3,2,1,0:T(8,128)}), f32[128,8,16,128]{3,2,1,0:T(8,128)}, u32[]{:S(2)}, u32[]{:S(2)}) %all-to-all-start.4) | async-done | bytes 8388640 | tf_op jit(solution)/shard_map/all_to_all | solution.py:456
  362.1 9.7 %add_tiles.3 = f32[12288,128]{1,0:T(8,128)} custom-call(s32[128]{0:T(128)} %get-tuple-element.32.places, f32[12288,128]{1,0:T(8,128)} %update_front.1.base, f32[128,8,16,128]{3,2,1,0:T(8,128)} %all-to-all-done.4.tiles), custom_call_target="tpu_custom_call" | custom-call | tf_op jit(solution)/shard_map/add_tiles/pallas_call | solution.py:344
  (65 shorter events, 16.6 us)
Async XLA Ops:
  8.4 11.8 %copy-start.7 = (s32[1,1,128]{2,1,0:T(1,128)S(1)}, s32[1,1,128]{2,1,0:T(1,128)}, u32[]{:S(2)}) copy-start(s32[1,1,128]{2,1,0:T(1,128)} %param.7) | copy-start | bytes 1540
  8.4 11.8 %copy-start.8 = (s32[1,1,128]{2,1,0:T(1,128)S(1)}, s32[1,1,128]{2,1,0:T(1,128)}, u32[]{:S(2)}) copy-start(s32[1,1,128]{2,1,0:T(1,128)} %param.6) | copy-start | bytes 1540
  8.5 13.3 %copy-start.6 = (s32[128]{0:T(128)S(1)}, s32[128]{0:T(128)}, u32[]{:S(2)}) copy-start(s32[128]{0:T(128)} %get-tuple-element.44.slot) | copy-start | bytes 1540
  8.5 120.5 %all-to-all-start = ((f32[128,8,16,128]{3,2,1,0:T(8,128)}), f32[128,8,16,128]{3,2,1,0:T(8,128)}, u32[]{:S(2)}, u32[]{:S(2)}) async-start(f32[128,8,16,128]{3,2,1,0:T(8,128)} %get-tuple-element.17), calls=%async_computation | async-start | bytes 16777216 | tf_op jit(solution)/shard_map/all_to_all | solution.py:441
  129.0 40.9 %all-to-all-start.1 = ((f32[128,5,8,128]{3,2,1,0:T(8,128)}), f32[128,5,8,128]{3,2,1,0:T(8,128)S(1)}, u32[]{:S(2)}, u32[]{:S(2)}) async-start(f32[128,5,8,128]{3,2,1,0:T(8,128)} %after.4), calls=%async_computation.1 | async-start | bytes 5242880 | tf_op jit(solution)/shard_map/all_to_all | solution.py:447
  140.3 35.2 %collective-permute-start.1 = (f32[48,16,128]{2,1,0:T(8,128)}, f32[48,16,128]{2,1,0:T(8,128)S(1)}, u32[]{:S(2)}, u32[]{:S(2)}) collective-permute-start(f32[48,16,128]{2,1,0:T(8,128)} %get-tuple-element.22), channel_id=1, source_target_pairs={{0,2},{8,10},{16,18},{24,26},{32,34},{40,42},{48,50},{56,58},{64,6... | collective-permute-start | bytes 1179656 | tf_op jit(solution)/shard_map/ppermute | solution.py:444
  143.2 36.1 %collective-permute-start.2 = (f32[48,16,128]{2,1,0:T(8,128)}, f32[48,16,128]{2,1,0:T(8,128)S(1)}, u32[]{:S(2)}, u32[]{:S(2)}) collective-permute-start(f32[48,16,128]{2,1,0:T(8,128)} %get-tuple-element.23), channel_id=1, source_target_pairs={{0,3},{8,11},{16,19},{24,27},{32,35},{40,43},{48,51},{56,59},{64,6... | collective-permute-start | bytes 1179656 | tf_op jit(solution)/shard_map/ppermute | solution.py:444
  145.0 42.7 %collective-permute-start.3 = (f32[48,16,128]{2,1,0:T(8,128)}, f32[48,16,128]{2,1,0:T(8,128)}, u32[]{:S(2)}, u32[]{:S(2)}) collective-permute-start(f32[48,16,128]{2,1,0:T(8,128)} %get-tuple-element.24), channel_id=1, source_target_pairs={{0,4},{8,12},{16,20},{24,28},{32,36},{40,44},{48,52},{56,60},{64,6... | collective-permute-start | bytes 1179656 | tf_op jit(solution)/shard_map/ppermute | solution.py:444
  147.0 47.9 %collective-permute-start.4 = (f32[48,16,128]{2,1,0:T(8,128)}, f32[48,16,128]{2,1,0:T(8,128)}, u32[]{:S(2)}, u32[]{:S(2)}) collective-permute-start(f32[48,16,128]{2,1,0:T(8,128)} %get-tuple-element.25), channel_id=1, source_target_pairs={{0,5},{8,13},{16,21},{24,29},{32,37},{40,45},{48,53},{56,61},{64,6... | collective-permute-start | bytes 1179656 | tf_op jit(solution)/shard_map/ppermute | solution.py:444
  149.4 45.6 %collective-permute-start.6 = (f32[48,16,128]{2,1,0:T(8,128)}, f32[48,16,128]{2,1,0:T(8,128)}, u32[]{:S(2)}, u32[]{:S(2)}) collective-permute-start(f32[48,16,128]{2,1,0:T(8,128)} %get-tuple-element.27), channel_id=1, source_target_pairs={{0,7},{8,15},{16,23},{24,31},{32,39},{40,47},{48,55},{56,63},{64,7... | collective-permute-start | bytes 1179656 | tf_op jit(solution)/shard_map/ppermute | solution.py:444
  169.9 1.5 copy-start
  175.5 19.8 %copy-start.2 = (f32[48,16,128]{2,1,0:T(8,128)}, f32[48,16,128]{2,1,0:T(8,128)S(1)}, u32[]{:S(2)}) copy-start(f32[48,16,128]{2,1,0:T(8,128)S(1)} %collective-permute-done.1.refs_2_) | copy-start | bytes 1179652
  175.5 19.7 %collective-permute-start = (f32[48,16,128]{2,1,0:T(8,128)}, f32[48,16,128]{2,1,0:T(8,128)S(1)}, u32[]{:S(2)}, u32[]{:S(2)}) collective-permute-start(f32[48,16,128]{2,1,0:T(8,128)} %after.5), channel_id=1, source_target_pairs={{0,1},{8,9},{16,17},{24,25},{32,33},{40,41},{48,49},{56,57},{64,65... | collective-permute-start | bytes 1179656 | tf_op jit(solution)/shard_map/ppermute | solution.py:452
  179.3 15.9 %copy-start.3 = (f32[48,16,128]{2,1,0:T(8,128)}, f32[48,16,128]{2,1,0:T(8,128)S(1)}, u32[]{:S(2)}) copy-start(f32[48,16,128]{2,1,0:T(8,128)S(1)} %collective-permute-done.2.refs_3_) | copy-start | bytes 1179652
  179.3 15.9 %collective-permute-start.5 = (f32[48,16,128]{2,1,0:T(8,128)}, f32[48,16,128]{2,1,0:T(8,128)S(1)}, u32[]{:S(2)}, u32[]{:S(2)}) collective-permute-start(f32[48,16,128]{2,1,0:T(8,128)} %after.6), channel_id=1, source_target_pairs={{0,6},{8,14},{16,22},{24,30},{32,38},{40,46},{48,54},{56,62},{64,7... | collective-permute-start | bytes 1179656 | tf_op jit(solution)/shard_map/ppermute | solution.py:452
  180.6 14.6 %all-to-all-start.2 = ((f32[16,16,128]{2,1,0:T(8,128)}), f32[16,16,128]{2,1,0:T(8,128)S(1)}, u32[]{:S(2)}, u32[]{:S(2)}) async-start(f32[16,16,128]{2,1,0:T(8,128)} %get-tuple-element.18), calls=%async_computation.2 | async-start | bytes 262144 | tf_op jit(solution)/shard_map/all_to_all | solution.py:453
  195.2 0.7 copy-start.1
  195.2 0.8 copy-start.4
  195.2 0.9 copy-start.5
  245.5 116.6 %all-to-all-start.4 = ((f32[128,8,16,128]{3,2,1,0:T(8,128)}), f32[128,8,16,128]{3,2,1,0:T(8,128)}, u32[]{:S(2)}, u32[]{:S(2)}) async-start(f32[128,8,16,128]{3,2,1,0:T(8,128)} %after.7), calls=%async_computation.4 | async-start | bytes 16777216 | tf_op jit(solution)/shard_map/all_to_all | solution.py:456

commit v9 on v8

--- a/solution.py
+++ b/solution.py
@@ -45,125 +45,123 @@
     return slot, panel_tiles, message, jnp.concatenate([where, stay_tiles, stay_blocks])
 
 
-def pack_panel_kernel(
-    panel_tiles, local, places, tiles, front, out, held, corner, block, load_sem, corner_sem, sem
+def pack_kernel(
+    chunks, slot, panel_tiles, local, places, tiles, cut_tiles, front, first, second, *scratch
 ):
+    held, cut, corner, block, load_sem, cut_sem, corner_sem, main_sem, sem = scratch
+    count, whole = held.shape[:2]
+    step = count // chunks
     size = block.shape[-1]
-    slots = held.shape[0]
-    row_count = out.shape[0]
-    groups = block.shape[1]
-    pltpu.make_async_copy(places, out.at[:, :, CAP * groups], sem).start()
+    slots, groups = cut.shape[0], block.shape[1]
+    row_count, col_count = first.shape[:2]
+    main_part = pl.ds(CAP * groups, whole)
+
+    def load(i):
+        part = pl.ds(i * step, step)
+        return pltpu.make_async_copy(tiles.at[part], held.at[part], load_sem.at[i])
+
     load_corner = pltpu.make_async_copy(front.at[pl.ds(0, 2 * size)], corner, corner_sem)
-    load_corner.start()
     loads = [
-        pltpu.make_async_copy(tiles.at[panel_tiles[i]], held.at[i], load_sem.at[i])
+        pltpu.make_async_copy(cut_tiles.at[panel_tiles[i]], cut.at[i], cut_sem.at[i])
         for i in range(slots)
     ]
-    for load in loads:
-        load.start()
+    for i in range(chunks):
+        load(i).start()
+    load_corner.start()
+    for copy in loads:
+        copy.start()
+    all_places = pltpu.make_async_copy(places, first.at[:, :, CAP * groups + whole], sem)
+    all_places.start()
+    for i in range(chunks):
+        load(i).wait()
+
+        def send(k, carry):
+            where = slot[k]
+            owner = where // CAP
+
+            @pl.when(where % CAP == 0)
+            def _():
+                pltpu.make_async_copy(
+                    held.at[k], first.at[owner // col_count, owner % col_count, main_part], main_sem
+                ).start()
+
+            @pl.when(where % CAP == 1)
+            def _():
+                pltpu.make_async_copy(held.at[k], second.at[owner], main_sem).start()
+
+            return carry
+
+        lax.fori_loop(i * step, (i + 1) * step, send, 0)
     load_corner.wait()
     block[...] = corner[pl.ds(0, size, stride=2), :].reshape(block.shape)
     for r in range(row_count):
-        mine = (local[0] == r) & (local[1] == 0)
         for s in range(CAP):
             loads[r * CAP + s].wait()
 
-        @pl.when(mine)
+        @pl.when((local[0] == r) & (local[1] == 0))
         def _():
             for s in range(CAP):
 
                 @pl.when(local[2 + CAP + s] == 0)
                 def _():
-                    block[...] += held[r * CAP + s]
-
-            held[r * CAP] = block[...]
+                    block[...] += cut[r * CAP + s]
+
+            cut[r * CAP] = block[...]
 
         for s in range(CAP):
             pltpu.make_async_copy(
-                held.at[r * CAP + s], out.at[r, :, pl.ds(s * groups, groups)], sem
+                cut.at[r * CAP + s], first.at[r, :, pl.ds(s * groups, groups)], sem
             ).start()
-    pltpu.make_async_copy(out, out, sem).wait()
-
-
-def pack_panel(panel_tiles, local, message, tiles, front, row_count, col_count):
-    size = tiles.shape[-1]
-    rows = size // col_count
-    groups = rows // 8
+    pltpu.make_async_copy(held, second, main_sem).wait()
+    panel_part = first.at[:, :, pl.ds(0, CAP * groups + 1)]
+    pltpu.make_async_copy(panel_part, panel_part, sem).wait()
+
+
+def pack(slot, panel_tiles, local, message, tiles, front, row_count, col_count):
+    count, size = tiles.shape[0], tiles.shape[-1]
+    groups = size // 8 // col_count
+    whole = size // 8
     slots = row_count * CAP
+    chunks = 8
     view = (col_count, groups, 8, size)
     places = jnp.pad(
         message.astype(jnp.float32)[:, None, :], ((0, 0), (0, 7), (0, size - message.shape[1]))
     ).reshape(row_count, col_count, 8, size)
-    sent = pl.pallas_call(
-        pack_panel_kernel,
-        out_shape=jax.ShapeDtypeStruct(
-            (row_count, col_count, CAP * groups + 1, 8, size), jnp.float32
-        ),
-        in_specs=[pl.BlockSpec(memory_space=SMEM)] * 2
+    first, second = pl.pallas_call(
+        functools.partial(pack_kernel, chunks),
+        out_shape=[
+            jax.ShapeDtypeStruct(
+                (row_count, col_count, CAP * groups + whole + 1, 8, size), jnp.float32
+            ),
+            jax.ShapeDtypeStruct((row_count * col_count, whole, 8, size), jnp.float32),
+        ],
+        in_specs=[pl.BlockSpec(memory_space=SMEM)] * 3
         + [pl.BlockSpec(memory_space=VMEM)]
-        + [pl.BlockSpec(memory_space=ANY)] * 2,
-        out_specs=pl.BlockSpec(memory_space=ANY),
+        + [pl.BlockSpec(memory_space=ANY)] * 3,
+        out_specs=[pl.BlockSpec(memory_space=ANY)] * 2,
         scratch_shapes=[
+            VMEM((count, whole, 8, size), jnp.float32),
             VMEM((slots,) + view, jnp.float32),
             VMEM((2 * size, size), jnp.float32),
             VMEM(view, jnp.float32),
+            pltpu.SemaphoreType.DMA((chunks,)),
             pltpu.SemaphoreType.DMA((slots,)),
             pltpu.SemaphoreType.DMA,
             pltpu.SemaphoreType.DMA,
-        ],
-        compiler_params=LIMIT,
-        name="pack_panel",
-    )(panel_tiles, local, places, tiles.reshape((-1,) + view), front)
-    return sent.reshape((row_count * col_count,) + sent.shape[2:])
-
-
-def pack_kernel(chunks, slot, tiles, first, second, held, load_sem, main_sem):
-    count = tiles.shape[0]
-    step = count // chunks
-
-    def load(i):
-        part = pl.ds(i * step, step)
-        return pltpu.make_async_copy(tiles.at[part], held.at[part], load_sem.at[i])
-
-    for i in range(chunks):
-        load(i).start()
-    for i in range(chunks):
-        load(i).wait()
-
-        def send(k, carry):
-            where = slot[k]
-            owner = where // CAP
-
-            @pl.when(where % CAP == 0)
-            def _():
-                pltpu.make_async_copy(held.at[k], first.at[owner], main_sem).start()
-
-            @pl.when(where % CAP == 1)
-            def _():
-                pltpu.make_async_copy(held.at[k], second.at[owner], main_sem).start()
-
-            return carry
-
-        lax.fori_loop(i * step, (i + 1) * step, send, 0)
-    pltpu.make_async_copy(held, second, main_sem).wait()
-
-
-def pack(slot, tiles, devices):
-    chunks = 8
-    out = jax.ShapeDtypeStruct((devices,) + tiles.shape[1:], jnp.float32)
-    return pl.pallas_call(
-        functools.partial(pack_kernel, chunks),
-        out_shape=[out, out],
-        in_specs=[pl.BlockSpec(memory_space=SMEM), pl.BlockSpec(memory_space=ANY)],
-        out_specs=[pl.BlockSpec(memory_space=ANY)] * 2,
-        scratch_shapes=[
-            VMEM(tiles.shape, jnp.float32),
-            pltpu.SemaphoreType.DMA((chunks,)),
             pltpu.SemaphoreType.DMA,
         ],
         compiler_params=LIMIT,
         name="pack",
-    )(slot, tiles)
+    )(
+        slot,
+        panel_tiles,
+        local,
+        places,
+        tiles.reshape(count, whole, 8, size),
+        tiles.reshape((count,) + view),
+        front,
+    )
+    return first.reshape((row_count * col_count,) + first.shape[2:]), second
 
 
 def split_kernel(rows, local, front, tiles, *refs):
@@ -231,9 +229,8 @@
     windows[...] = jnp.broadcast_to(total[0][None], windows.shape)
 
 
-def sum_slices(parts, arrived, row_count, row_blocks):
-    devices, groups, _, size = arrived.shape
-    groups = groups // CAP
+def sum_slices(parts, arrived, row_count, row_blocks, groups):
+    devices, _, _, size = arrived.shape
     rows = groups * 8
     outs = [
         jax.ShapeDtypeStruct((row_count, rows, size), jnp.float32),
@@ -308,7 +305,7 @@
     )(local, windows, column, *own)
 
 
-def add_kernel(chunks, places, base, tiles, out, total, held, base_sem, tile_sem):
+def add_kernel(chunks, skip, places, base, tiles, out, total, held, base_sem, tile_sem):
     slots, parts, rows, size = held.shape
     step = slots // chunks
     last = base.shape[0]
@@ -318,7 +315,8 @@
 
     def load(i):
         some = pl.ds(i * step, step)
-        return pltpu.make_async_copy(tiles.at[some], held.at[some], tile_sem.at[i])
+        inner = pl.ds(skip, parts)
+        return pltpu.make_async_copy(tiles.at[some, inner], held.at[some], tile_sem.at[i])
 
     for i in range(chunks):
         load(i).start()
@@ -338,11 +336,11 @@
     store.wait()
 
 
-def add_tiles(places, base, tiles):
-    slots, parts, rows, size = tiles.shape
+def add_tiles(places, base, tiles, skip):
+    slots, _, rows, size = tiles.shape
     chunks = 8
     return pl.pallas_call(
-        functools.partial(add_kernel, chunks),
+        functools.partial(add_kernel, chunks, skip),
         out_shape=jax.ShapeDtypeStruct(base.shape, jnp.float32),
         in_specs=[
             pl.BlockSpec(memory_space=SMEM),
@@ -352,7 +350,7 @@
         out_specs=pl.BlockSpec(memory_space=ANY),
         scratch_shapes=[
             VMEM((base.shape[0] + 2 * size, size), jnp.float32),
-            VMEM(tiles.shape, jnp.float32),
+            VMEM((slots, size // rows, rows, size), jnp.float32),
             pltpu.SemaphoreType.DMA,
             pltpu.SemaphoreType.DMA((chunks,)),
         ],
@@ -437,19 +435,17 @@
         col_count,
         size,
     )
-    first, second = pack(slot, tiles, devices)
+    first, second = pack(
+        slot, panel_tiles, local, message, tiles, flat_front, row_count, col_count
+    )
     first = lax.all_to_all(first, both, split_axis=0, concat_axis=0, tiled=True)
     own = list(split_front(local, flat_front, tiles, row_blocks))
-    for k in (7, 2, 4, 5, 3):
+    for k in (7, 2, 4, 5, 3, 1, 6):
         own[k] = lax.ppermute(own[k], "col", [(0, k)])
-    sliced = pack_panel(panel_tiles, local, message, tiles, flat_front, row_count, col_count)
-    sliced = after(sliced, first)
-    sliced = lax.all_to_all(sliced, both, split_axis=0, concat_axis=0, tiled=True)
-    message = sliced[:, -1, 0, : 2 * CAP].astype(jnp.int32)
+    message = first[:, -1, 0, : 2 * CAP].astype(jnp.int32)
     main, part = ([message[:, h * CAP + s] for s in range(CAP)] for h in range(2))
-    windows, column = sum_slices(part, sliced, row_count, row_blocks)
-    for k in (1, 6):
-        own[k] = lax.ppermute(after(own[k], column), "col", [(0, k)])
+    groups = rows // 8
+    windows, column = sum_slices(part, first, row_count, row_blocks, groups)
     windows = lax.all_to_all(windows, "row", split_axis=0, concat_axis=0, tiled=True)
     column = spread(local, windows, column, own)
     column = lax.all_to_all(column, "col", split_axis=0, concat_axis=0, tiled=True)
@@ -462,9 +458,9 @@
     inverse = jax.scipy.linalg.solve_triangular(
         factor, jnp.eye(size, dtype=jnp.float32), lower=True
     )
-    total = add_tiles(main[0], flat_front, first)
+    total = add_tiles(main[0], flat_front, first, CAP * groups)
     base = update_front(local, total, inverse.T, window, column, row_count, row_blocks)
-    return add_tiles(main[1], base, second).reshape(front.shape)
+    return add_tiles(main[1], base, second, 0).reshape(front.shape)
 
 
 def solution(mesh):

time: 373 us -> 377 us (1.011)
  waiting for transfers between devices: 167 us -> 172 us
    ppermute x5 -> x7, waiting for transfers between devices: 8.76 us -> 124 us  [per_device(): own[k] = lax.ppermute(own[k], 'col', [(0, k)])]
    all_to_all x1, waiting for transfers between devices: 100 us -> 3.45 us  [per_device(): first = lax.all_to_all(first, both, split_axis=0, concat_axis=0, tiled=True)]
    all_to_all x1 -> x0, waiting for transfers between devices: 18.5 us -> none  [per_device(): lax.all_to_all(sliced, both, split_axis=0, concat_axis=0, tiled=True)]
    all_to_all x1, waiting for transfers between devices: 0.25 us -> 5.36 us  [per_device(): lax.all_to_all(windows, 'row', split_axis=0, concat_axis=0, tiled=True)]
    all_to_all x1, starting transfers between devices: 6.63 us -> 11.6 us  [per_device(): lax.all_to_all(windows, 'row', split_axis=0, concat_axis=0, tiled=True)]
    all_to_all x1 -> x0, starting transfers between devices: 4.9 us -> none  [per_device(): lax.all_to_all(sliced, both, split_axis=0, concat_axis=0, tiled=True)]
    ppermute x2 -> x0, starting transfers between devices: 4.07 us -> none  [per_device(): own[k] = lax.ppermute(after(own[k], column), 'col', [(0, k)])]
    all_to_all x1, starting transfers between devices: 10.6 us -> 14.6 us  [per_device(): lax.all_to_all(after(second, column), both, split_axis=0, concat_axis=0,...]
  transfers between devices with their start and end apart: 11 -> 10, of which waited for: 7 -> 6; matrix products, arithmetic and copies ran while one was open for 8% -> 8% of each run, Pallas kernels for 15% -> 14%
where the time goes in v9:
time: 377 us; the launch traced here: 376 us
  waiting for transfers between devices  172 us (46%)
  Pallas kernels  75.1 us (20%)
  starting transfers between devices  48.7 us (13%)
  blocking collectives  45 us (12%)
  other arithmetic  28.8 us (8%)
  local copies, waits for them, and re-layouts  5.01 us (1%)
    ppermute x7, waiting for transfers between devices, per_device(): own[k] = lax.ppermute(own[k], 'col', [(0, k)])  124 us
    all_to_all x1, blocking collectives, per_device(): lax.all_to_all(column, 'col', split_axis=0, concat_axis=0, tiled=True)  45 us
    all_to_all x1, waiting for transfers between devices, per_device(): lax.all_to_all(after(second, column), both, split_axis=0, concat_axis=0,...  38.7 us
    pallas_call x1, Pallas kernels, update_front(): pl.pallas_call(functools.partial(update_kernel, (row_count, row_blocks)),...  31.2 us
    pallas_call x2, Pallas kernels, add_tiles(): pl.pallas_call(functools.partial(add_kernel, chunks, skip), out_shape=jax...  19.4 us
    all_to_all x1, starting transfers between devices, per_device(): lax.all_to_all(after(second, column), both, split_axis=0, concat_axis=0,...  14.6 us
    another operation x3, other arithmetic, per_device(): factor = jnp.linalg.cholesky(0.5 * (corner + corner.T))  12.4 us
    all_to_all x1, starting transfers between devices, per_device(): lax.all_to_all(windows, 'row', split_axis=0, concat_axis=0, tiled=True)  11.6 us
  transfers between devices with their start and end apart: 10, of which 6 were waited for; matrix products, arithmetic and copies ran while one was open for 8% of the time, Pallas kernels for 14%

profile of v9, /device:TPU:0, one launch (start us, length us, event | category | flops | bytes accessed | tf_op | source)
XLA Modules:
  0.0 375.6 jit_solution(18429589451277468008)
XLA Ops:
  5.9 9.9 %pack.1 = (f32[16,8,21,8,128]{4,3,2,1,0:T(8,128)}, f32[128,16,8,128]{3,2,1,0:T(8,128)}) custom-call(s32[128]{0:T(128)} %copy-done.8, s32[32]{0:T(128)} %select_reduce_fusion.1.panel_tiles, s32[6]{0:T(128)} %pad_add_fusion.local.where, f32[16,8,8,128]{3,2,1,0:T(8,128)} %bitcast.87, f32[128,16,8,128]{3,2,1,0:T(8,128)} %bitcast.80, ...), custom_call_target="tpu_custom_call" | custom-call | tf_op jit(solution)/shard_map/pack/pallas_call | solution.py:130
  15.8 11.6 %all-to-all-start = ((f32[128,21,8,128]{3,2,1,0:T(8,128)}), f32[128,21,8,128]{3,2,1,0:T(8,128)}, u32[]{:S(2)}, u32[]{:S(2)}) async-start(f32[128,21,8,128]{3,2,1,0:T(8,128)} %bitcast.86), calls=%async_computation | async-start | bytes 22020096 | tf_op jit(solution)/shard_map/all_to_all | solution.py:441
  27.4 6.4 %split_front.1 = (f32[48,16,128]{2,1,0:T(8,128)}, f32[48,16,128]{2,1,0:T(8,128)}, f32[48,16,128]{2,1,0:T(8,128)}, f32[48,16,128]{2,1,0:T(8,128)}, f32[48,16,128]...) custom-call(s32[6]{0:T(128)} %pad_add_fusion.local.where, ...), custom_call_target="tpu_custom_call" | custom-call | tf_op jit(solution)/shard_map/split_front/pallas_call | solution.py:196
  33.8 2.9 collective-permute-start
  36.8 1.3 collective-permute-start.1
  38.1 1.3 collective-permute-start.2
  39.4 1.3 collective-permute-start.3
  40.7 1.3 collective-permute-start.4
  42.1 113.1 %collective-permute-done.refs_1_ = f32[48,16,128]{2,1,0:T(8,128)S(1)} collective-permute-done((f32[48,16,128]{2,1,0:T(8,128)}, f32[48,16,128]{2,1,0:T(8,128)S(1)}, u32[]{:S(2)}, u32[]{:S(2)}) %collective-permute-start) | collective-permute-done | bytes 393248 | tf_op jit(solution)/shard_map/ppermute | solution.py:444
  156.5 8.5 %collective-permute-done.1.refs_2_ = f32[48,16,128]{2,1,0:T(8,128)S(1)} collective-permute-done((f32[48,16,128]{2,1,0:T(8,128)}, f32[48,16,128]{2,1,0:T(8,128)S(1)}, u32[]{:S(2)}, u32[]{:S(2)}) %collective-permute-start.1) | collective-permute-done | bytes 393248 | tf_op jit(solution)/shard_map/ppermute | solution.py:444
  166.3 3.5 all-to-all-done.tiles.arrived
  171.6 3.9 %sum_slices.1 = (f32[16,16,128]{2,1,0:T(8,128)}, f32[48,16,128]{2,1,0:T(8,128)}) custom-call(s32[128]{0:T(128)} %get-tuple-element.30.part_0, s32[128]{0:T(128)} %get-tuple-element.29.part_1, f32[128,21,8,128]{3,2,1,0:T(8,128)} %all-to-all-done.tiles.arrived), custom_call_target="tpu_custom_call" | custom-call | tf_op jit(solution)/shard_map/sum_slices/pallas_call | solution.py:239
  175.6 11.6 %all-to-all-start.1 = ((f32[16,16,128]{2,1,0:T(8,128)}), f32[16,16,128]{2,1,0:T(8,128)S(1)}, u32[]{:S(2)}, u32[]{:S(2)}) async-start(f32[16,16,128]{2,1,0:T(8,128)} %get-tuple-element.18), calls=%async_computation.1 | async-start | bytes 262144 | tf_op jit(solution)/shard_map/all_to_all | solution.py:449
  187.2 2.5 collective-permute-done.4.refs_5_
  189.8 5.4 %all-to-all-done.1.windows = f32[16,16,128]{2,1,0:T(8,128)S(1)} async-done(((f32[16,16,128]{2,1,0:T(8,128)}), f32[16,16,128]{2,1,0:T(8,128)S(1)}, u32[]{:S(2)}, u32[]{:S(2)}) %all-to-all-start.1) | async-done | bytes 131104 | tf_op jit(solution)/shard_map/all_to_all | solution.py:449
  195.8 4.2 %spread.1 = f32[8,51,16,128]{3,2,1,0:T(8,128)} custom-call(s32[6]{0:T(128)} %pad_add_fusion.local.where, f32[16,16,128]{2,1,0:T(8,128)} %copy-done, f32[48,16,128]{2,1,0:T(8,128)} %get-tuple-element.19.column, f32[48,16,128]{2,1,0:T(8,128)} %get-tuple-element.20.refs_0_, f32[48,16,128]{2,1,0:T(8,128)} %copy-done.1, f32[48,16,128]{2,1,0:T(8,128)} %copy-done.2, ...), custom_call_target="tpu_custom_call" | custom-call | tf_op jit(solution)/shard_map/spread/pallas_call | solution.py:290
  200.0 45.0 %all_to_all.20.column.refs_1_ = f32[8,51,16,128]{3,2,1,0:T(8,128)} all-to-all(f32[8,51,16,128]{3,2,1,0:T(8,128)} %spread.1), channel_id=1, replica_groups=mesh['row'=16,'col'=8] {'col'}, dimensions={0} | all-to-all | bytes 6684672 | tf_op jit(solution)/shard_map/all_to_all | solution.py:451
  245.1 14.6 %all-to-all-start.3 = ((f32[128,16,8,128]{3,2,1,0:T(8,128)}), f32[128,16,8,128]{3,2,1,0:T(8,128)}, u32[]{:S(2)}, u32[]{:S(2)}) async-start(f32[128,16,8,128]{3,2,1,0:T(8,128)} %after.1), calls=%async_computation.3 | async-start | bytes 16777216 | tf_op jit(solution)/shard_map/all_to_all | solution.py:452
  259.7 9.7 %add_tiles.2.front = f32[12288,128]{1,0:T(8,128)} custom-call(s32[128]{0:T(128)} %get-tuple-element.31.places, f32[12288,128]{1,0:T(8,128)} %bitcast.85, f32[128,21,8,128]{3,2,1,0:T(8,128)} %all-to-all-done.tiles.arrived), custom_call_target="tpu_custom_call" | custom-call | tf_op jit(solution)/shard_map/add_tiles/pallas_call | solution.py:342
  270.5 11.7 %cholesky.14 = f32[128,128]{1,0:T(8,128)S(1)} custom-call(f32[128,128]{1,0:T(8,128)S(1)} %fusion.3), custom_call_target="Cholesky" | custom-call | tf_op jit(solution)/shard_map/jit(cholesky)/cholesky | solution.py:457
  283.5 9.8 %custom-call.7 = f32[1,128,128]{1,2,0:T(8,128)S(1)} custom-call(f32[1,128,128]{2,1,0:T(8,128)S(1)} %fusion), custom_call_target="InvertDiagBlocksLowerTriangular" | custom-call | tf_op jit(solution)/shard_map/jit(_solve_triangular)/triangular_solve | solution.py:458
  295.8 31.2 %update_front.1.base = f32[12288,128]{1,0:T(8,128)} custom-call(s32[6]{0:T(128)} %pad_add_fusion.local.where, f32[12288,128]{1,0:T(8,128)} %add_tiles.2.front, f32[128,128]{1,0:T(8,128)} %fusion.1.inverse_t, f32[256,128]{1,0:T(8,128)} %bitcast.90, f32[8,51,16,128]{3,2,1,0:T(8,128)} %all_to_all.20.column.refs_1_), custom_call_target="tpu_custom_call" | custom-call | tf_op jit(solution)/shard_map/update_front/pallas_call | solution.py:393
  327.0 38.7 %all-to-all-done.3.tiles = f32[128,16,8,128]{3,2,1,0:T(8,128)} async-done(((f32[128,16,8,128]{3,2,1,0:T(8,128)}), f32[128,16,8,128]{3,2,1,0:T(8,128)}, u32[]{:S(2)}, u32[]{:S(2)}) %all-to-all-start.3) | async-done | bytes 8388640 | tf_op jit(solution)/shard_map/all_to_all | solution.py:452
  365.7 9.7 %add_tiles.3 = f32[12288,128]{1,0:T(8,128)} custom-call(s32[128]{0:T(128)} %get-tuple-element.32.places, f32[12288,128]{1,0:T(8,128)} %update_front.1.base, f32[128,16,8,128]{3,2,1,0:T(8,128)} %all-to-all-done.3.tiles), custom_call_target="tpu_custom_call" | custom-call | tf_op jit(solution)/shard_map/add_tiles/pallas_call | solution.py:342
  (59 shorter events, 15.8 us)
Async XLA Ops:
  2.3 3.6 copy-start.8
  15.8 154.0 %all-to-all-start = ((f32[128,21,8,128]{3,2,1,0:T(8,128)}), f32[128,21,8,128]{3,2,1,0:T(8,128)}, u32[]{:S(2)}, u32[]{:S(2)}) async-start(f32[128,21,8,128]{3,2,1,0:T(8,128)} %bitcast.86), calls=%async_computation | async-start | bytes 22020096 | tf_op jit(solution)/shard_map/all_to_all | solution.py:441
  33.8 121.4 %collective-permute-start = (f32[48,16,128]{2,1,0:T(8,128)}, f32[48,16,128]{2,1,0:T(8,128)S(1)}, u32[]{:S(2)}, u32[]{:S(2)}) collective-permute-start(f32[48,16,128]{2,1,0:T(8,128)} %get-tuple-element.21), channel_id=1, source_target_pairs={{0,1},{8,9},{16,17},{24,25},{32,33},{40,41},{48,49},{56,57},{64,65... | collective-permute-start | bytes 1179656 | tf_op jit(solution)/shard_map/ppermute | solution.py:444
  36.8 128.2 %collective-permute-start.1 = (f32[48,16,128]{2,1,0:T(8,128)}, f32[48,16,128]{2,1,0:T(8,128)S(1)}, u32[]{:S(2)}, u32[]{:S(2)}) collective-permute-start(f32[48,16,128]{2,1,0:T(8,128)} %get-tuple-element.22), channel_id=1, source_target_pairs={{0,2},{8,10},{16,18},{24,26},{32,34},{40,42},{48,50},{56,58},{64,6... | collective-permute-start | bytes 1179656 | tf_op jit(solution)/shard_map/ppermute | solution.py:444
  38.1 149.1 %collective-permute-start.2 = (f32[48,16,128]{2,1,0:T(8,128)}, f32[48,16,128]{2,1,0:T(8,128)S(1)}, u32[]{:S(2)}, u32[]{:S(2)}) collective-permute-start(f32[48,16,128]{2,1,0:T(8,128)} %get-tuple-element.23), channel_id=1, source_target_pairs={{0,3},{8,11},{16,19},{24,27},{32,35},{40,43},{48,51},{56,59},{64,6... | collective-permute-start | bytes 1179656 | tf_op jit(solution)/shard_map/ppermute | solution.py:444
  39.4 147.8 %collective-permute-start.3 = (f32[48,16,128]{2,1,0:T(8,128)}, f32[48,16,128]{2,1,0:T(8,128)S(1)}, u32[]{:S(2)}, u32[]{:S(2)}) collective-permute-start(f32[48,16,128]{2,1,0:T(8,128)} %get-tuple-element.24), channel_id=1, source_target_pairs={{0,4},{8,12},{16,20},{24,28},{32,36},{40,44},{48,52},{56,60},{64,6... | collective-permute-start | bytes 1179656 | tf_op jit(solution)/shard_map/ppermute | solution.py:444
  40.7 149.0 %collective-permute-start.4 = (f32[48,16,128]{2,1,0:T(8,128)}, f32[48,16,128]{2,1,0:T(8,128)S(1)}, u32[]{:S(2)}, u32[]{:S(2)}) collective-permute-start(f32[48,16,128]{2,1,0:T(8,128)} %get-tuple-element.25), channel_id=1, source_target_pairs={{0,5},{8,13},{16,21},{24,29},{32,37},{40,45},{48,53},{56,61},{64,6... | collective-permute-start | bytes 1179656 | tf_op jit(solution)/shard_map/ppermute | solution.py:444
  155.2 40.0 %copy-start.1 = (f32[48,16,128]{2,1,0:T(8,128)}, f32[48,16,128]{2,1,0:T(8,128)S(1)}, u32[]{:S(2)}) copy-start(f32[48,16,128]{2,1,0:T(8,128)S(1)} %collective-permute-done.refs_1_) | copy-start | bytes 1179652
  155.2 34.6 %collective-permute-start.5 = (f32[48,16,128]{2,1,0:T(8,128)}, f32[48,16,128]{2,1,0:T(8,128)S(1)}, u32[]{:S(2)}, u32[]{:S(2)}) collective-permute-start(f32[48,16,128]{2,1,0:T(8,128)} %get-tuple-element.26), channel_id=1, source_target_pairs={{0,6},{8,14},{16,22},{24,30},{32,38},{40,46},{48,54},{56,62},{64,7... | collective-permute-start | bytes 1179656 | tf_op jit(solution)/shard_map/ppermute | solution.py:444
  165.0 30.2 %copy-start.2 = (f32[48,16,128]{2,1,0:T(8,128)}, f32[48,16,128]{2,1,0:T(8,128)S(1)}, u32[]{:S(2)}) copy-start(f32[48,16,128]{2,1,0:T(8,128)S(1)} %collective-permute-done.1.refs_2_) | copy-start | bytes 1179652
  165.0 24.8 %collective-permute-start.6 = (f32[48,16,128]{2,1,0:T(8,128)}, f32[48,16,128]{2,1,0:T(8,128)S(1)}, u32[]{:S(2)}, u32[]{:S(2)}) collective-permute-start(f32[48,16,128]{2,1,0:T(8,128)} %get-tuple-element.27), channel_id=1, source_target_pairs={{0,7},{8,15},{16,23},{24,31},{32,39},{40,47},{48,55},{56,63},{64,7... | collective-permute-start | bytes 1179656 | tf_op jit(solution)/shard_map/ppermute | solution.py:444
  175.6 19.6 %all-to-all-start.1 = ((f32[16,16,128]{2,1,0:T(8,128)}), f32[16,16,128]{2,1,0:T(8,128)S(1)}, u32[]{:S(2)}, u32[]{:S(2)}) async-start(f32[16,16,128]{2,1,0:T(8,128)} %get-tuple-element.18), calls=%async_computation.1 | async-start | bytes 262144 | tf_op jit(solution)/shard_map/all_to_all | solution.py:449
  187.2 8.0 %copy-start.3 = (f32[48,16,128]{2,1,0:T(8,128)}, f32[48,16,128]{2,1,0:T(8,128)S(1)}, u32[]{:S(2)}) copy-start(f32[48,16,128]{2,1,0:T(8,128)S(1)} %collective-permute-done.2.refs_3_) | copy-start | bytes 1179652
  187.2 7.9 %copy-start.4 = (f32[48,16,128]{2,1,0:T(8,128)}, f32[48,16,128]{2,1,0:T(8,128)S(1)}, u32[]{:S(2)}) copy-start(f32[48,16,128]{2,1,0:T(8,128)S(1)} %collective-permute-done.3.refs_4_) | copy-start | bytes 1179652
  189.8 5.4 %copy-start.5 = (f32[48,16,128]{2,1,0:T(8,128)}, f32[48,16,128]{2,1,0:T(8,128)S(1)}, u32[]{:S(2)}) copy-start(f32[48,16,128]{2,1,0:T(8,128)S(1)} %collective-permute-done.4.refs_5_) | copy-start | bytes 1179652
  189.8 5.4 %copy-start.6 = (f32[48,16,128]{2,1,0:T(8,128)}, f32[48,16,128]{2,1,0:T(8,128)S(1)}, u32[]{:S(2)}) copy-start(f32[48,16,128]{2,1,0:T(8,128)S(1)} %collective-permute-done.5.refs_6_) | copy-start | bytes 1179652
  189.8 5.4 %copy-start.7 = (f32[48,16,128]{2,1,0:T(8,128)}, f32[48,16,128]{2,1,0:T(8,128)S(1)}, u32[]{:S(2)}) copy-start(f32[48,16,128]{2,1,0:T(8,128)S(1)} %collective-permute-done.6.refs_7_) | copy-start | bytes 1179652
  195.2 0.7 copy-start
  245.1 120.7 %all-to-all-start.3 = ((f32[128,16,8,128]{3,2,1,0:T(8,128)}), f32[128,16,8,128]{3,2,1,0:T(8,128)}, u32[]{:S(2)}, u32[]{:S(2)}) async-start(f32[128,16,8,128]{3,2,1,0:T(8,128)} %after.1), calls=%async_computation.3 | async-start | bytes 16777216 | tf_op jit(solution)/shard_map/all_to_all | solution.py:452

commit v10 on v8

--- a/solution.py
+++ b/solution.py
@@ -440,16 +440,14 @@
     first, second = pack(slot, tiles, devices)
     first = lax.all_to_all(first, both, split_axis=0, concat_axis=0, tiled=True)
     own = list(split_front(local, flat_front, tiles, row_blocks))
-    for k in (7, 2, 4, 5, 3):
+    for k in (4, 5, 2, 3, 7, 6, 1):
         own[k] = lax.ppermute(own[k], "col", [(0, k)])
     sliced = pack_panel(panel_tiles, local, message, tiles, flat_front, row_count, col_count)
-    sliced = after(sliced, first)
+    sliced = after(sliced, first, own[4], own[5])
     sliced = lax.all_to_all(sliced, both, split_axis=0, concat_axis=0, tiled=True)
     message = sliced[:, -1, 0, : 2 * CAP].astype(jnp.int32)
     main, part = ([message[:, h * CAP + s] for s in range(CAP)] for h in range(2))
     windows, column = sum_slices(part, sliced, row_count, row_blocks)
-    for k in (1, 6):
-        own[k] = lax.ppermute(after(own[k], column), "col", [(0, k)])
     windows = lax.all_to_all(windows, "row", split_axis=0, concat_axis=0, tiled=True)
     column = spread(local, windows, column, own)
     column = lax.all_to_all(column, "col", split_axis=0, concat_axis=0, tiled=True)

time: 373 us -> 371 us (level)
    all_to_all x1, waiting for transfers between devices: 100 us -> 0.01 us  [per_device(): first = lax.all_to_all(first, both, split_axis=0, concat_axis=0, tiled=True)]
    ppermute x5 -> x7, waiting for transfers between devices: 8.76 us -> 92.8 us  [per_device(): own[k] = lax.ppermute(own[k], 'col', [(0, k)])]
    all_to_all x1, waiting for transfers between devices: 0.25 us -> 7.85 us  [per_device(): lax.all_to_all(windows, 'row', split_axis=0, concat_axis=0, tiled=True)]
    all_to_all x1, waiting for transfers between devices: 18.5 us -> 25.6 us  [per_device(): lax.all_to_all(sliced, both, split_axis=0, concat_axis=0, tiled=True)]
    all_to_all x1, starting transfers between devices: 4.9 us -> 10.6 us  [per_device(): lax.all_to_all(sliced, both, split_axis=0, concat_axis=0, tiled=True)]
    ppermute x5 -> x7, starting transfers between devices: 11.1 us -> 16.6 us  [per_device(): own[k] = lax.ppermute(own[k], 'col', [(0, k)])]
    all_to_all x1, starting transfers between devices: 10.6 us -> 6.1 us  [per_device(): lax.all_to_all(after(second, column), both, split_axis=0, concat_axis=0,...]
    ppermute x2 -> x0, starting transfers between devices: 4.07 us -> none  [per_device(): own[k] = lax.ppermute(after(own[k], column), 'col', [(0, k)])]
  transfers between devices with their start and end apart: 11 -> 11, of which waited for: 7 -> 5; matrix products, arithmetic and copies ran while one was open for 8% -> 8% of each run, Pallas kernels for 15% -> 15%
where the time goes in v10:
time: 371 us; the launch traced here: 370 us
  waiting for transfers between devices  165 us (44%)
  Pallas kernels  76.9 us (21%)
  starting transfers between devices  48.4 us (13%)
  blocking collectives  45.1 us (12%)
  other arithmetic  26.4 us (7%)
  local copies, waits for them, and re-layouts  6.5 us (2%)
    ppermute x7, waiting for transfers between devices, per_device(): own[k] = lax.ppermute(own[k], 'col', [(0, k)])  92.8 us
    all_to_all x1, blocking collectives, per_device(): lax.all_to_all(column, 'col', split_axis=0, concat_axis=0, tiled=True)  45.1 us
    all_to_all x1, waiting for transfers between devices, per_device(): lax.all_to_all(after(second, column), both, split_axis=0, concat_axis=0,...  38.7 us
    pallas_call x1, Pallas kernels, update_front(): pl.pallas_call(functools.partial(update_kernel, (row_count, row_blocks)),...  31.2 us
    all_to_all x1, waiting for transfers between devices, per_device(): lax.all_to_all(sliced, both, split_axis=0, concat_axis=0, tiled=True)  25.6 us
    pallas_call x2, Pallas kernels, add_tiles(): pl.pallas_call(functools.partial(add_kernel, chunks), out_shape=jax.Shape...  19.3 us
    ppermute x7, starting transfers between devices, per_device(): own[k] = lax.ppermute(own[k], 'col', [(0, k)])  16.6 us
    another operation x3, other arithmetic, per_device(): factor = jnp.linalg.cholesky(0.5 * (corner + corner.T))  12.4 us
  transfers between devices with their start and end apart: 11, of which 5 were waited for; matrix products, arithmetic and copies ran while one was open for 8% of the time, Pallas kernels for 15%

profile of v10, /device:TPU:0, one launch (start us, length us, event | category | flops | bytes accessed | tf_op | source)
XLA Modules:
  0.0 369.7 jit_solution(11683552578130325401)
XLA Ops:
  1.4 7.2 %pack.1 = (f32[128,8,16,128]{3,2,1,0:T(8,128)}, f32[128,8,16,128]{3,2,1,0:T(8,128)}) custom-call(s32[128]{0:T(128)} %get-tuple-element.44.slot, f32[128,8,16,128]{3,2,1,0:T(8,128)} %bitcast.79), custom_call_target="tpu_custom_call" | custom-call | tf_op jit(solution)/shard_map/pack/pallas_call | solution.py:154
  8.6 11.6 %all-to-all-start = ((f32[128,8,16,128]{3,2,1,0:T(8,128)}), f32[128,8,16,128]{3,2,1,0:T(8,128)}, u32[]{:S(2)}, u32[]{:S(2)}) async-start(f32[128,8,16,128]{3,2,1,0:T(8,128)} %get-tuple-element.17), calls=%async_computation | async-start | bytes 16777216 | tf_op jit(solution)/shard_map/all_to_all | solution.py:441
  21.1 6.5 %split_front.1 = (f32[48,16,128]{2,1,0:T(8,128)}, f32[48,16,128]{2,1,0:T(8,128)}, f32[48,16,128]{2,1,0:T(8,128)}, f32[48,16,128]{2,1,0:T(8,128)}, f32[48,16,128]...) custom-call(s32[6]{0:T(128)} %pad_add_fusion.local.where, ...), custom_call_target="tpu_custom_call" | custom-call | tf_op jit(solution)/shard_map/split_front/pallas_call | solution.py:198
  27.5 4.3 %collective-permute-start = (f32[48,16,128]{2,1,0:T(8,128)}, f32[48,16,128]{2,1,0:T(8,128)S(1)}, u32[]{:S(2)}, u32[]{:S(2)}) collective-permute-start(f32[48,16,128]{2,1,0:T(8,128)} %get-tuple-element.18), channel_id=1, source_target_pairs={{0,4},{8,12},{16,20},{24,28},{32,36},{40,44},{48,52},{56,60},{64,6... | collective-permute-start | bytes 1179656 | tf_op jit(solution)/shard_map/ppermute | solution.py:444
  36.0 5.1 %pack_panel.1 = f32[16,8,5,8,128]{4,3,2,1,0:T(8,128)} custom-call(s32[32]{0:T(128)} %select_reduce_fusion.1.panel_tiles, s32[6]{0:T(128)} %pad_add_fusion.local.where, f32[16,8,8,128]{3,2,1,0:T(8,128)} %bitcast.86, f32[128,8,2,8,128]{4,3,2,1,0:T(8,128)} %bitcast.81, f32[12288,128]{1,0:T(8,128)} %bitcast.83), custom_call_target="tpu_custom_call" | custom-call | tf_op jit(solution)/shard_map/pack_panel/pallas_call | solution.py:97
  41.1 85.6 %collective-permute-done.refs_2_.refs_4_ = f32[48,16,128]{2,1,0:T(8,128)S(1)} collective-permute-done((f32[48,16,128]{2,1,0:T(8,128)}, f32[48,16,128]{2,1,0:T(8,128)S(1)}, u32[]{:S(2)}, u32[]{:S(2)}) %collective-permute-start) | collective-permute-done | bytes 393248 | tf_op jit(solution)/shard_map/ppermute | solution.py:444
  126.7 7.2 %collective-permute-done.1.refs_3_.refs_5_ = f32[48,16,128]{2,1,0:T(8,128)S(1)} collective-permute-done((f32[48,16,128]{2,1,0:T(8,128)}, f32[48,16,128]{2,1,0:T(8,128)S(1)}, u32[]{:S(2)}, u32[]{:S(2)}) %collective-permute-start.1) | collective-permute-done | bytes 393248 | tf_op jit(solution)/shard_map/ppermute | solution.py:444
  134.7 10.6 %all-to-all-start.1 = ((f32[128,5,8,128]{3,2,1,0:T(8,128)}), f32[128,5,8,128]{3,2,1,0:T(8,128)S(1)}, u32[]{:S(2)}, u32[]{:S(2)}) async-start(f32[128,5,8,128]{3,2,1,0:T(8,128)} %after.2), calls=%async_computation.1 | async-start | bytes 5242880 | tf_op jit(solution)/shard_map/all_to_all | solution.py:447
  145.3 3.0 collective-permute-start.2
  149.6 2.1 collective-permute-start.4
  151.6 2.0 collective-permute-start.5
  155.7 25.6 %all-to-all-done.1.arrived = f32[128,5,8,128]{3,2,1,0:T(8,128)S(1)} async-done(((f32[128,5,8,128]{3,2,1,0:T(8,128)}), f32[128,5,8,128]{3,2,1,0:T(8,128)S(1)}, u32[]{:S(2)}, u32[]{:S(2)}) %all-to-all-start.1) | async-done | bytes 2621472 | tf_op jit(solution)/shard_map/all_to_all | solution.py:447
  182.8 3.5 sum_slices.1
  186.3 3.5 all-to-all-start.2
  189.9 7.8 %all-to-all-done.2.windows = f32[16,16,128]{2,1,0:T(8,128)S(1)} async-done(((f32[16,16,128]{2,1,0:T(8,128)}), f32[16,16,128]{2,1,0:T(8,128)S(1)}, u32[]{:S(2)}, u32[]{:S(2)}) %all-to-all-start.2) | async-done | bytes 131104 | tf_op jit(solution)/shard_map/all_to_all | solution.py:451
  198.4 4.2 %spread.1 = f32[8,51,16,128]{3,2,1,0:T(8,128)} custom-call(s32[6]{0:T(128)} %pad_add_fusion.local.where, f32[16,16,128]{2,1,0:T(8,128)} %copy-done.3, f32[48,16,128]{2,1,0:T(8,128)} %get-tuple-element.21.column, f32[48,16,128]{2,1,0:T(8,128)} %get-tuple-element.22.refs_0_, f32[48,16,128]{2,1,0:T(8,128)} %copy-done.4, f32[48,16,128]{2,1,0:T(8,128)} %copy-done.5, ...), custom_call_target="tpu_custom_call" | custom-call | tf_op jit(solution)/shard_map/spread/pallas_call | solution.py:293
  202.6 45.1 %all_to_all.25.column.refs_1_ = f32[8,51,16,128]{3,2,1,0:T(8,128)} all-to-all(f32[8,51,16,128]{3,2,1,0:T(8,128)} %spread.1), channel_id=1, replica_groups=mesh['row'=16,'col'=8] {'col'}, dimensions={0} | all-to-all | bytes 6684672 | tf_op jit(solution)/shard_map/all_to_all | solution.py:453
  247.7 6.1 %all-to-all-start.4 = ((f32[128,8,16,128]{3,2,1,0:T(8,128)}), f32[128,8,16,128]{3,2,1,0:T(8,128)}, u32[]{:S(2)}, u32[]{:S(2)}) async-start(f32[128,8,16,128]{3,2,1,0:T(8,128)} %after.3), calls=%async_computation.4 | async-start | bytes 16777216 | tf_op jit(solution)/shard_map/all_to_all | solution.py:454
  253.8 9.7 %add_tiles.2.front = f32[12288,128]{1,0:T(8,128)} custom-call(s32[128]{0:T(128)} %get-tuple-element.31.places, f32[12288,128]{1,0:T(8,128)} %bitcast.84, f32[128,8,16,128]{3,2,1,0:T(8,128)} %all-to-all-done.refs_1_.tiles), custom_call_target="tpu_custom_call" | custom-call | tf_op jit(solution)/shard_map/add_tiles/pallas_call | solution.py:344
  264.6 11.7 %cholesky.14 = f32[128,128]{1,0:T(8,128)S(1)} custom-call(f32[128,128]{1,0:T(8,128)S(1)} %fusion.3), custom_call_target="Cholesky" | custom-call | tf_op jit(solution)/shard_map/jit(cholesky)/cholesky | solution.py:459
  277.6 9.8 %custom-call.7 = f32[1,128,128]{1,2,0:T(8,128)S(1)} custom-call(f32[1,128,128]{2,1,0:T(8,128)S(1)} %fusion), custom_call_target="InvertDiagBlocksLowerTriangular" | custom-call | tf_op jit(solution)/shard_map/jit(_solve_triangular)/triangular_solve | solution.py:460
  289.9 31.2 %update_front.1.base = f32[12288,128]{1,0:T(8,128)} custom-call(s32[6]{0:T(128)} %pad_add_fusion.local.where, f32[12288,128]{1,0:T(8,128)} %add_tiles.2.front, f32[128,128]{1,0:T(8,128)} %fusion.1.inverse_t, f32[256,128]{1,0:T(8,128)} %bitcast.89, f32[8,51,16,128]{3,2,1,0:T(8,128)} %all_to_all.25.column.refs_1_), custom_call_target="tpu_custom_call" | custom-call | tf_op jit(solution)/shard_map/update_front/pallas_call | solution.py:395
  321.1 38.7 %all-to-all-done.4.tiles = f32[128,8,16,128]{3,2,1,0:T(8,128)} async-done(((f32[128,8,16,128]{3,2,1,0:T(8,128)}), f32[128,8,16,128]{3,2,1,0:T(8,128)}, u32[]{:S(2)}, u32[]{:S(2)}) %all-to-all-start.4) | async-done | bytes 8388640 | tf_op jit(solution)/shard_map/all_to_all | solution.py:454
  359.8 9.7 %add_tiles.3 = f32[12288,128]{1,0:T(8,128)} custom-call(s32[128]{0:T(128)} %get-tuple-element.32.places, f32[12288,128]{1,0:T(8,128)} %update_front.1.base, f32[128,8,16,128]{3,2,1,0:T(8,128)} %all-to-all-done.4.tiles), custom_call_target="tpu_custom_call" | custom-call | tf_op jit(solution)/shard_map/add_tiles/pallas_call | solution.py:344
  (63 shorter events, 17.4 us)
Async XLA Ops:
  8.6 11.6 %copy-start.7 = (s32[1,1,128]{2,1,0:T(1,128)S(1)}, s32[1,1,128]{2,1,0:T(1,128)}, u32[]{:S(2)}) copy-start(s32[1,1,128]{2,1,0:T(1,128)} %param.7) | copy-start | bytes 1540
  8.6 11.6 %copy-start.6 = (s32[128]{0:T(128)S(1)}, s32[128]{0:T(128)}, u32[]{:S(2)}) copy-start(s32[128]{0:T(128)} %get-tuple-element.44.slot) | copy-start | bytes 1540
  8.6 125.3 %all-to-all-start = ((f32[128,8,16,128]{3,2,1,0:T(8,128)}), f32[128,8,16,128]{3,2,1,0:T(8,128)}, u32[]{:S(2)}, u32[]{:S(2)}) async-start(f32[128,8,16,128]{3,2,1,0:T(8,128)} %get-tuple-element.17), calls=%async_computation | async-start | bytes 16777216 | tf_op jit(solution)/shard_map/all_to_all | solution.py:441
  21.1 12.7 %copy-start.8 = (s32[1,1,128]{2,1,0:T(1,128)S(1)}, s32[1,1,128]{2,1,0:T(1,128)}, u32[]{:S(2)}) copy-start(s32[1,1,128]{2,1,0:T(1,128)} %param.6) | copy-start | bytes 1540
  27.5 99.2 %collective-permute-start = (f32[48,16,128]{2,1,0:T(8,128)}, f32[48,16,128]{2,1,0:T(8,128)S(1)}, u32[]{:S(2)}, u32[]{:S(2)}) collective-permute-start(f32[48,16,128]{2,1,0:T(8,128)} %get-tuple-element.18), channel_id=1, source_target_pairs={{0,4},{8,12},{16,20},{24,28},{32,36},{40,44},{48,52},{56,60},{64,6... | collective-permute-start | bytes 1179656 | tf_op jit(solution)/shard_map/ppermute | solution.py:444
  31.9 102.0 %collective-permute-start.1 = (f32[48,16,128]{2,1,0:T(8,128)}, f32[48,16,128]{2,1,0:T(8,128)S(1)}, u32[]{:S(2)}, u32[]{:S(2)}) collective-permute-start(f32[48,16,128]{2,1,0:T(8,128)} %get-tuple-element.19), channel_id=1, source_target_pairs={{0,5},{8,13},{16,21},{24,29},{32,37},{40,45},{48,53},{56,61},{64,6... | collective-permute-start | bytes 1179656 | tf_op jit(solution)/shard_map/ppermute | solution.py:444
  126.7 7.2 %copy-start.1 = (f32[48,16,128]{2,1,0:T(8,128)}, f32[48,16,128]{2,1,0:T(8,128)S(1)}, u32[]{:S(2)}) copy-start(f32[48,16,128]{2,1,0:T(8,128)S(1)} %collective-permute-done.refs_2_.refs_4_) | copy-start | bytes 1179652
  133.9 0.7 copy-start.2
  134.7 46.6 %all-to-all-start.1 = ((f32[128,5,8,128]{3,2,1,0:T(8,128)}), f32[128,5,8,128]{3,2,1,0:T(8,128)S(1)}, u32[]{:S(2)}, u32[]{:S(2)}) async-start(f32[128,5,8,128]{3,2,1,0:T(8,128)} %after.2), calls=%async_computation.1 | async-start | bytes 5242880 | tf_op jit(solution)/shard_map/all_to_all | solution.py:447
  145.3 44.6 %collective-permute-start.2 = (f32[48,16,128]{2,1,0:T(8,128)}, f32[48,16,128]{2,1,0:T(8,128)S(1)}, u32[]{:S(2)}, u32[]{:S(2)}) collective-permute-start(f32[48,16,128]{2,1,0:T(8,128)} %get-tuple-element.23), channel_id=1, source_target_pairs={{0,1},{8,9},{16,17},{24,25},{32,33},{40,41},{48,49},{56,57},{64,65... | collective-permute-start | bytes 1179656 | tf_op jit(solution)/shard_map/ppermute | solution.py:444
  148.3 41.6 %collective-permute-start.3 = (f32[48,16,128]{2,1,0:T(8,128)}, f32[48,16,128]{2,1,0:T(8,128)S(1)}, u32[]{:S(2)}, u32[]{:S(2)}) collective-permute-start(f32[48,16,128]{2,1,0:T(8,128)} %get-tuple-element.24), channel_id=1, source_target_pairs={{0,2},{8,10},{16,18},{24,26},{32,34},{40,42},{48,50},{56,58},{64,6... | collective-permute-start | bytes 1179656 | tf_op jit(solution)/shard_map/ppermute | solution.py:444
  149.6 40.3 %collective-permute-start.4 = (f32[48,16,128]{2,1,0:T(8,128)}, f32[48,16,128]{2,1,0:T(8,128)}, u32[]{:S(2)}, u32[]{:S(2)}) collective-permute-start(f32[48,16,128]{2,1,0:T(8,128)} %get-tuple-element.25), channel_id=1, source_target_pairs={{0,3},{8,11},{16,19},{24,27},{32,35},{40,43},{48,51},{56,59},{64,6... | collective-permute-start | bytes 1179656 | tf_op jit(solution)/shard_map/ppermute | solution.py:444
  151.6 38.2 %collective-permute-start.5 = (f32[48,16,128]{2,1,0:T(8,128)}, f32[48,16,128]{2,1,0:T(8,128)}, u32[]{:S(2)}, u32[]{:S(2)}) collective-permute-start(f32[48,16,128]{2,1,0:T(8,128)} %get-tuple-element.26), channel_id=1, source_target_pairs={{0,6},{8,14},{16,22},{24,30},{32,38},{40,46},{48,54},{56,62},{64,7... | collective-permute-start | bytes 1179656 | tf_op jit(solution)/shard_map/ppermute | solution.py:444
  153.7 36.2 %collective-permute-start.6 = (f32[48,16,128]{2,1,0:T(8,128)}, f32[48,16,128]{2,1,0:T(8,128)}, u32[]{:S(2)}, u32[]{:S(2)}) collective-permute-start(f32[48,16,128]{2,1,0:T(8,128)} %get-tuple-element.27), channel_id=1, source_target_pairs={{0,7},{8,15},{16,23},{24,31},{32,39},{40,47},{48,55},{56,63},{64,7... | collective-permute-start | bytes 1179656 | tf_op jit(solution)/shard_map/ppermute | solution.py:444
  181.3 1.5 copy-start
  186.3 11.4 %all-to-all-start.2 = ((f32[16,16,128]{2,1,0:T(8,128)}), f32[16,16,128]{2,1,0:T(8,128)S(1)}, u32[]{:S(2)}, u32[]{:S(2)}) async-start(f32[16,16,128]{2,1,0:T(8,128)} %get-tuple-element.20), calls=%async_computation.2 | async-start | bytes 262144 | tf_op jit(solution)/shard_map/all_to_all | solution.py:451
  189.8 7.9 %copy-start.4 = (f32[48,16,128]{2,1,0:T(8,128)}, f32[48,16,128]{2,1,0:T(8,128)S(1)}, u32[]{:S(2)}) copy-start(f32[48,16,128]{2,1,0:T(8,128)S(1)} %collective-permute-done.2.refs_1_) | copy-start | bytes 1179652
  189.8 7.9 %copy-start.5 = (f32[48,16,128]{2,1,0:T(8,128)}, f32[48,16,128]{2,1,0:T(8,128)S(1)}, u32[]{:S(2)}) copy-start(f32[48,16,128]{2,1,0:T(8,128)S(1)} %collective-permute-done.3.refs_2_) | copy-start | bytes 1179652
  197.7 0.7 copy-start.3
  247.7 112.1 %all-to-all-start.4 = ((f32[128,8,16,128]{3,2,1,0:T(8,128)}), f32[128,8,16,128]{3,2,1,0:T(8,128)}, u32[]{:S(2)}, u32[]{:S(2)}) async-start(f32[128,8,16,128]{3,2,1,0:T(8,128)} %after.3), calls=%async_computation.4 | async-start | bytes 16777216 | tf_op jit(solution)/shard_map/all_to_all | solution.py:454

commit v11 on v8

--- a/solution.py
+++ b/solution.py
@@ -437,21 +437,22 @@
         col_count,
         size,
     )
-    first, second = pack(slot, tiles, devices)
-    first = lax.all_to_all(first, both, split_axis=0, concat_axis=0, tiled=True)
+    sliced = pack_panel(panel_tiles, local, message, tiles, flat_front, row_count, col_count)
+    sliced = lax.all_to_all(sliced, both, split_axis=0, concat_axis=0, tiled=True)
     own = list(split_front(local, flat_front, tiles, row_blocks))
     for k in (7, 2, 4, 5, 3):
         own[k] = lax.ppermute(own[k], "col", [(0, k)])
-    sliced = pack_panel(panel_tiles, local, message, tiles, flat_front, row_count, col_count)
+    first, second = pack(slot, tiles, devices)
     sliced = after(sliced, first)
-    sliced = lax.all_to_all(sliced, both, split_axis=0, concat_axis=0, tiled=True)
     message = sliced[:, -1, 0, : 2 * CAP].astype(jnp.int32)
     main, part = ([message[:, h * CAP + s] for s in range(CAP)] for h in range(2))
     windows, column = sum_slices(part, sliced, row_count, row_blocks)
-    for k in (1, 6):
+    for k in (6, 1):
         own[k] = lax.ppermute(after(own[k], column), "col", [(0, k)])
     windows = lax.all_to_all(windows, "row", split_axis=0, concat_axis=0, tiled=True)
-    column = spread(local, windows, column, own)
+    first = after(first, windows, *(own[k] for k in (7, 2, 4, 5, 3, 6, 1)))
+    first = lax.all_to_all(first, both, split_axis=0, concat_axis=0, tiled=True)
+    column = after(spread(local, windows, column, own), first)
     column = lax.all_to_all(column, "col", split_axis=0, concat_axis=0, tiled=True)
     second = lax.all_to_all(
         after(second, column), both, split_axis=0, concat_axis=0, tiled=True

time: 373 us -> 371 us (level)
  waiting for transfers between devices: 167 us -> 163 us
    all_to_all x1, waiting for transfers between devices: 18.5 us -> 9.7 us  [per_device(): lax.all_to_all(sliced, both, split_axis=0, concat_axis=0, tiled=True)]
    all_to_all x1, starting transfers between devices: 4.9 us -> 11.2 us  [per_device(): lax.all_to_all(sliced, both, split_axis=0, concat_axis=0, tiled=True)]
    all_to_all x1, starting transfers between devices: 10.6 us -> 6.12 us  [per_device(): lax.all_to_all(after(second, column), both, split_axis=0, concat_axis=0,...]
    all_to_all x1, waiting for transfers between devices: 100 us -> 105 us  [per_device(): first = lax.all_to_all(first, both, split_axis=0, concat_axis=0, tiled=True)]
  transfers between devices with their start and end apart: 11 -> 11, of which waited for: 7 -> 5; matrix products, arithmetic and copies ran while one was open for 8% -> 8% of each run, Pallas kernels for 15% -> 17%
where the time goes in v11:
time: 371 us; the launch traced here: 370 us
  waiting for transfers between devices  163 us (44%)
  Pallas kernels  76.9 us (21%)
  starting transfers between devices  49.6 us (13%)
  blocking collectives  42.9 us (12%)
  other arithmetic  29 us (8%)
  local copies, waits for them, and re-layouts  7.43 us (2%)
    all_to_all x1, waiting for transfers between devices, per_device(): first = lax.all_to_all(first, both, split_axis=0, concat_axis=0, tiled=True)  105 us
    all_to_all x1, blocking collectives, per_device(): lax.all_to_all(column, 'col', split_axis=0, concat_axis=0, tiled=True)  42.9 us
    all_to_all x1, waiting for transfers between devices, per_device(): lax.all_to_all(after(second, column), both, split_axis=0, concat_axis=0,...  38.6 us
    pallas_call x1, Pallas kernels, update_front(): pl.pallas_call(functools.partial(update_kernel, (row_count, row_blocks)),...  31.2 us
    pallas_call x2, Pallas kernels, add_tiles(): pl.pallas_call(functools.partial(add_kernel, chunks), out_shape=jax.Shape...  19.3 us
    ppermute x5, starting transfers between devices, per_device(): own[k] = lax.ppermute(own[k], 'col', [(0, k)])  12.8 us
    another operation x3, other arithmetic, per_device(): factor = jnp.linalg.cholesky(0.5 * (corner + corner.T))  12.5 us
    all_to_all x1, starting transfers between devices, per_device(): lax.all_to_all(sliced, both, split_axis=0, concat_axis=0, tiled=True)  11.2 us
  transfers between devices with their start and end apart: 11, of which 5 were waited for; matrix products, arithmetic and copies ran while one was open for 8% of the time, Pallas kernels for 17%

profile of v11, /device:TPU:0, one launch (start us, length us, event | category | flops | bytes accessed | tf_op | source)
XLA Modules:
  0.0 370.2 jit_solution(15804109932045729036)
XLA Ops:
  6.0 5.2 %pack_panel.1 = f32[16,8,5,8,128]{4,3,2,1,0:T(8,128)} custom-call(s32[32]{0:T(128)} %select_reduce_fusion.1.panel_tiles, s32[6]{0:T(128)} %pad_add_fusion.local.where, f32[16,8,8,128]{3,2,1,0:T(8,128)} %bitcast.86, f32[128,8,2,8,128]{4,3,2,1,0:T(8,128)} %bitcast.79, f32[12288,128]{1,0:T(8,128)} %bitcast.82), custom_call_target="tpu_custom_call" | custom-call | tf_op jit(solution)/shard_map/pack_panel/pallas_call | solution.py:97
  11.2 11.2 %all-to-all-start = ((f32[128,5,8,128]{3,2,1,0:T(8,128)}), f32[128,5,8,128]{3,2,1,0:T(8,128)S(1)}, u32[]{:S(2)}, u32[]{:S(2)}) async-start(f32[128,5,8,128]{3,2,1,0:T(8,128)} %bitcast.85), calls=%async_computation | async-start | bytes 5242880 | tf_op jit(solution)/shard_map/all_to_all | solution.py:441
  22.4 6.4 %split_front.1 = (f32[48,16,128]{2,1,0:T(8,128)}, f32[48,16,128]{2,1,0:T(8,128)}, f32[48,16,128]{2,1,0:T(8,128)}, f32[48,16,128]{2,1,0:T(8,128)}, f32[48,16,128]...) custom-call(s32[6]{0:T(128)} %pad_add_fusion.local.where, ...), custom_call_target="tpu_custom_call" | custom-call | tf_op jit(solution)/shard_map/split_front/pallas_call | solution.py:198
  28.9 5.3 %collective-permute-start = (f32[48,16,128]{2,1,0:T(8,128)}, f32[48,16,128]{2,1,0:T(8,128)S(1)}, u32[]{:S(2)}, u32[]{:S(2)}) collective-permute-start(f32[48,16,128]{2,1,0:T(8,128)} %get-tuple-element.19), channel_id=1, source_target_pairs={{0,7},{8,15},{16,23},{24,31},{32,39},{40,47},{48,55},{56,63},{64,7... | collective-permute-start | bytes 1179656 | tf_op jit(solution)/shard_map/ppermute | solution.py:444
  35.5 2.1 collective-permute-start.2
  37.6 2.1 collective-permute-start.3
  41.7 7.1 %pack.1 = (f32[128,8,16,128]{3,2,1,0:T(8,128)}, f32[128,8,16,128]{3,2,1,0:T(8,128)}) custom-call(s32[128]{0:T(128)} %copy-done.6, f32[128,8,16,128]{3,2,1,0:T(8,128)} %bitcast.81), custom_call_target="tpu_custom_call" | custom-call | tf_op jit(solution)/shard_map/pack/pallas_call | solution.py:154
  48.8 9.7 %all-to-all-done.refs_0_ = f32[128,5,8,128]{3,2,1,0:T(8,128)S(1)} async-done(((f32[128,5,8,128]{3,2,1,0:T(8,128)}), f32[128,5,8,128]{3,2,1,0:T(8,128)S(1)}, u32[]{:S(2)}, u32[]{:S(2)}) %all-to-all-start) | async-done | bytes 2621472 | tf_op jit(solution)/shard_map/all_to_all | solution.py:441
  61.9 3.5 sum_slices.1
  65.4 3.1 collective-permute-start.5
  69.8 3.8 %all-to-all-start.1 = ((f32[16,16,128]{2,1,0:T(8,128)}), f32[16,16,128]{2,1,0:T(8,128)S(1)}, u32[]{:S(2)}, u32[]{:S(2)}) async-start(f32[16,16,128]{2,1,0:T(8,128)} %get-tuple-element.18), calls=%async_computation.1 | async-start | bytes 262144 | tf_op jit(solution)/shard_map/all_to_all | solution.py:452
  73.7 2.9 collective-permute-done.3.refs_5_
  76.5 7.2 %collective-permute-done.4.refs_6_.refs_3_ = f32[48,16,128]{2,1,0:T(8,128)} collective-permute-done((f32[48,16,128]{2,1,0:T(8,128)}, f32[48,16,128]{2,1,0:T(8,128)}, u32[]{:S(2)}, u32[]{:S(2)}) %collective-permute-start.4) | collective-permute-done | bytes 393248 | tf_op jit(solution)/shard_map/ppermute | solution.py:444
  85.4 11.2 %all-to-all-start.2 = ((f32[128,8,16,128]{3,2,1,0:T(8,128)}), f32[128,8,16,128]{3,2,1,0:T(8,128)}, u32[]{:S(2)}, u32[]{:S(2)}) async-start(f32[128,8,16,128]{3,2,1,0:T(8,128)} %after.9), calls=%async_computation.2 | async-start | bytes 16777216 | tf_op jit(solution)/shard_map/all_to_all | solution.py:454
  96.5 4.2 %spread.1.refs_0_ = f32[8,51,16,128]{3,2,1,0:T(8,128)} custom-call(s32[6]{0:T(128)} %pad_add_fusion.local.where, f32[16,16,128]{2,1,0:T(8,128)} %copy-done.5, f32[48,16,128]{2,1,0:T(8,128)} %get-tuple-element.25.refs_1_.column, f32[48,16,128]{2,1,0:T(8,128)} %get-tuple-element.27.refs_0_, f32[48,16,128]{2,1,0:T(8,128)} %copy-done.4, ...), custom_call_target="tpu_custom_call" | custom-call | tf_op jit(solution)/shard_map/spread/pallas_call | solution.py:293
  100.7 104.6 %all-to-all-done.2.tiles.refs_1_ = f32[128,8,16,128]{3,2,1,0:T(8,128)} async-done(((f32[128,8,16,128]{3,2,1,0:T(8,128)}), f32[128,8,16,128]{3,2,1,0:T(8,128)}, u32[]{:S(2)}, u32[]{:S(2)}) %all-to-all-start.2) | async-done | bytes 8388640 | tf_op jit(solution)/shard_map/all_to_all | solution.py:454
  205.3 42.9 %all_to_all.25.column.refs_1_ = f32[8,51,16,128]{3,2,1,0:T(8,128)} all-to-all(f32[8,51,16,128]{3,2,1,0:T(8,128)} %after.10), channel_id=1, replica_groups=mesh['row'=16,'col'=8] {'col'}, dimensions={0} | all-to-all | bytes 6684672 | tf_op jit(solution)/shard_map/all_to_all | solution.py:456
  248.2 6.1 %all-to-all-start.4 = ((f32[128,8,16,128]{3,2,1,0:T(8,128)}), f32[128,8,16,128]{3,2,1,0:T(8,128)}, u32[]{:S(2)}, u32[]{:S(2)}) async-start(f32[128,8,16,128]{3,2,1,0:T(8,128)} %after.11), calls=%async_computation.4 | async-start | bytes 16777216 | tf_op jit(solution)/shard_map/all_to_all | solution.py:457
  254.3 9.7 %add_tiles.2.front = f32[12288,128]{1,0:T(8,128)} custom-call(s32[128]{0:T(128)} %get-tuple-element.31.places, f32[12288,128]{1,0:T(8,128)} %bitcast.84, f32[128,8,16,128]{3,2,1,0:T(8,128)} %all-to-all-done.2.tiles.refs_1_), custom_call_target="tpu_custom_call" | custom-call | tf_op jit(solution)/shard_map/add_tiles/pallas_call | solution.py:344
  265.1 11.7 %cholesky.14 = f32[128,128]{1,0:T(8,128)S(1)} custom-call(f32[128,128]{1,0:T(8,128)S(1)} %fusion.3), custom_call_target="Cholesky" | custom-call | tf_op jit(solution)/shard_map/jit(cholesky)/cholesky | solution.py:462
  278.2 9.8 %custom-call.7 = f32[1,128,128]{1,2,0:T(8,128)S(1)} custom-call(f32[1,128,128]{2,1,0:T(8,128)S(1)} %fusion), custom_call_target="InvertDiagBlocksLowerTriangular" | custom-call | tf_op jit(solution)/shard_map/jit(_solve_triangular)/triangular_solve | solution.py:463
  290.5 31.2 %update_front.1.base = f32[12288,128]{1,0:T(8,128)} custom-call(s32[6]{0:T(128)} %pad_add_fusion.local.where, f32[12288,128]{1,0:T(8,128)} %add_tiles.2.front, f32[128,128]{1,0:T(8,128)} %fusion.1.inverse_t, f32[256,128]{1,0:T(8,128)} %bitcast.89, f32[8,51,16,128]{3,2,1,0:T(8,128)} %all_to_all.25.column.refs_1_), custom_call_target="tpu_custom_call" | custom-call | tf_op jit(solution)/shard_map/update_front/pallas_call | solution.py:395
  321.7 38.6 %all-to-all-done.4.tiles = f32[128,8,16,128]{3,2,1,0:T(8,128)} async-done(((f32[128,8,16,128]{3,2,1,0:T(8,128)}), f32[128,8,16,128]{3,2,1,0:T(8,128)}, u32[]{:S(2)}, u32[]{:S(2)}) %all-to-all-start.4) | async-done | bytes 8388640 | tf_op jit(solution)/shard_map/all_to_all | solution.py:457
  360.3 9.7 %add_tiles.3 = f32[12288,128]{1,0:T(8,128)} custom-call(s32[128]{0:T(128)} %get-tuple-element.32.places, f32[12288,128]{1,0:T(8,128)} %update_front.1.base, f32[128,8,16,128]{3,2,1,0:T(8,128)} %all-to-all-done.4.tiles), custom_call_target="tpu_custom_call" | custom-call | tf_op jit(solution)/shard_map/add_tiles/pallas_call | solution.py:344
  (63 shorter events, 20.5 us)
Async XLA Ops:
  2.9 8.2 %copy-start.6 = (s32[128]{0:T(128)}, s32[128]{0:T(128)S(1)}, u32[]{:S(2)}) copy-start(s32[128]{0:T(128)S(1)} %get-tuple-element.44.slot) | copy-start | bytes 1540
  11.2 47.3 %all-to-all-start = ((f32[128,5,8,128]{3,2,1,0:T(8,128)}), f32[128,5,8,128]{3,2,1,0:T(8,128)S(1)}, u32[]{:S(2)}, u32[]{:S(2)}) async-start(f32[128,5,8,128]{3,2,1,0:T(8,128)} %bitcast.85), calls=%async_computation | async-start | bytes 5242880 | tf_op jit(solution)/shard_map/all_to_all | solution.py:441
  28.9 36.5 %collective-permute-start = (f32[48,16,128]{2,1,0:T(8,128)}, f32[48,16,128]{2,1,0:T(8,128)S(1)}, u32[]{:S(2)}, u32[]{:S(2)}) collective-permute-start(f32[48,16,128]{2,1,0:T(8,128)} %get-tuple-element.19), channel_id=1, source_target_pairs={{0,7},{8,15},{16,23},{24,31},{32,39},{40,47},{48,55},{56,63},{64,7... | collective-permute-start | bytes 1179656 | tf_op jit(solution)/shard_map/ppermute | solution.py:444
  34.2 34.3 %collective-permute-start.1 = (f32[48,16,128]{2,1,0:T(8,128)}, f32[48,16,128]{2,1,0:T(8,128)S(1)}, u32[]{:S(2)}, u32[]{:S(2)}) collective-permute-start(f32[48,16,128]{2,1,0:T(8,128)} %get-tuple-element.20), channel_id=1, source_target_pairs={{0,2},{8,10},{16,18},{24,26},{32,34},{40,42},{48,50},{56,58},{64,6... | collective-permute-start | bytes 1179656 | tf_op jit(solution)/shard_map/ppermute | solution.py:444
  35.5 38.2 %collective-permute-start.2 = (f32[48,16,128]{2,1,0:T(8,128)}, f32[48,16,128]{2,1,0:T(8,128)}, u32[]{:S(2)}, u32[]{:S(2)}) collective-permute-start(f32[48,16,128]{2,1,0:T(8,128)} %get-tuple-element.21), channel_id=1, source_target_pairs={{0,4},{8,12},{16,20},{24,28},{32,36},{40,44},{48,52},{56,60},{64,6... | collective-permute-start | bytes 1179656 | tf_op jit(solution)/shard_map/ppermute | solution.py:444
  37.6 38.9 %collective-permute-start.3 = (f32[48,16,128]{2,1,0:T(8,128)}, f32[48,16,128]{2,1,0:T(8,128)}, u32[]{:S(2)}, u32[]{:S(2)}) collective-permute-start(f32[48,16,128]{2,1,0:T(8,128)} %get-tuple-element.22), channel_id=1, source_target_pairs={{0,5},{8,13},{16,21},{24,29},{32,37},{40,45},{48,53},{56,61},{64,6... | collective-permute-start | bytes 1179656 | tf_op jit(solution)/shard_map/ppermute | solution.py:444
  39.6 44.1 %collective-permute-start.4 = (f32[48,16,128]{2,1,0:T(8,128)}, f32[48,16,128]{2,1,0:T(8,128)}, u32[]{:S(2)}, u32[]{:S(2)}) collective-permute-start(f32[48,16,128]{2,1,0:T(8,128)} %get-tuple-element.23), channel_id=1, source_target_pairs={{0,3},{8,11},{16,19},{24,27},{32,35},{40,43},{48,51},{56,59},{64,6... | collective-permute-start | bytes 1179656 | tf_op jit(solution)/shard_map/ppermute | solution.py:444
  58.5 1.5 copy-start
  65.4 18.4 %copy-start.1 = (f32[48,16,128]{2,1,0:T(8,128)}, f32[48,16,128]{2,1,0:T(8,128)S(1)}, u32[]{:S(2)}) copy-start(f32[48,16,128]{2,1,0:T(8,128)S(1)} %collective-permute-done.refs_2_.refs_7_) | copy-start | bytes 1179652
  65.4 18.4 %collective-permute-start.5 = (f32[48,16,128]{2,1,0:T(8,128)}, f32[48,16,128]{2,1,0:T(8,128)S(1)}, u32[]{:S(2)}, u32[]{:S(2)}) collective-permute-start(f32[48,16,128]{2,1,0:T(8,128)} %after.7), channel_id=1, source_target_pairs={{0,6},{8,14},{16,22},{24,30},{32,38},{40,46},{48,54},{56,62},{64,7... | collective-permute-start | bytes 1179656 | tf_op jit(solution)/shard_map/ppermute | solution.py:451
  68.5 15.3 %copy-start.2 = (f32[48,16,128]{2,1,0:T(8,128)}, f32[48,16,128]{2,1,0:T(8,128)S(1)}, u32[]{:S(2)}) copy-start(f32[48,16,128]{2,1,0:T(8,128)S(1)} %collective-permute-done.1.refs_3_.refs_2_) | copy-start | bytes 1179652
  68.5 15.3 %collective-permute-start.6 = (f32[48,16,128]{2,1,0:T(8,128)}, f32[48,16,128]{2,1,0:T(8,128)S(1)}, u32[]{:S(2)}, u32[]{:S(2)}) collective-permute-start(f32[48,16,128]{2,1,0:T(8,128)} %after.8), channel_id=1, source_target_pairs={{0,1},{8,9},{16,17},{24,25},{32,33},{40,41},{48,49},{56,57},{64,65... | collective-permute-start | bytes 1179656 | tf_op jit(solution)/shard_map/ppermute | solution.py:451
  69.8 13.9 %all-to-all-start.1 = ((f32[16,16,128]{2,1,0:T(8,128)}), f32[16,16,128]{2,1,0:T(8,128)S(1)}, u32[]{:S(2)}, u32[]{:S(2)}) async-start(f32[16,16,128]{2,1,0:T(8,128)} %get-tuple-element.18), calls=%async_computation.1 | async-start | bytes 262144 | tf_op jit(solution)/shard_map/all_to_all | solution.py:452
  83.8 0.7 copy-start.5
  83.8 0.8 copy-start.3
  84.6 0.8 copy-start.4
  85.4 120.0 %all-to-all-start.2 = ((f32[128,8,16,128]{3,2,1,0:T(8,128)}), f32[128,8,16,128]{3,2,1,0:T(8,128)}, u32[]{:S(2)}, u32[]{:S(2)}) async-start(f32[128,8,16,128]{3,2,1,0:T(8,128)} %after.9), calls=%async_computation.2 | async-start | bytes 16777216 | tf_op jit(solution)/shard_map/all_to_all | solution.py:454
  248.2 112.1 %all-to-all-start.4 = ((f32[128,8,16,128]{3,2,1,0:T(8,128)}), f32[128,8,16,128]{3,2,1,0:T(8,128)}, u32[]{:S(2)}, u32[]{:S(2)}) async-start(f32[128,8,16,128]{3,2,1,0:T(8,128)} %after.11), calls=%async_computation.4 | async-start | bytes 16777216 | tf_op jit(solution)/shard_map/all_to_all | solution.py:457

commit v12 on v11

--- a/solution.py
+++ b/solution.py
@@ -12,6 +12,7 @@
 SMEM = pltpu.SMEM
 VMEM = pltpu.VMEM
 ANY = pl.ANY
+RELAY = {5: 7, 3: 1}
 LIMIT = pltpu.CompilerParams(vmem_limit_bytes=58 << 20)
 
 
@@ -166,44 +167,48 @@
     )(slot, tiles)
 
 
-def split_kernel(rows, local, front, tiles, *refs):
+def split_kernel(rows, row_blocks, local, front, tiles, *refs):
     outs, (held, sem) = refs[:-2], refs[-2:]
-    col_count = len(outs)
+    col_count = len(outs) + len(RELAY)
+    kept = [q for q in range(col_count) if q not in RELAY]
+    target = {q: (outs[kept.index(RELAY.get(q, q))], row_blocks * (q in RELAY)) for q in range(col_count)}
     for s in range(CAP):
         copy = pltpu.make_async_copy(tiles.at[local[2 + s]], held.at[s], sem.at[s])
         copy.start()
         copy.wait()
 
     def block(a, carry):
-        for q in range(col_count):
+        for q, (out, base) in target.items():
             start = (a * col_count + q) * rows * 2
-            outs[q][a] = front[pl.ds(start, rows, stride=2), :]
+            out[base + a] = front[pl.ds(start, rows, stride=2), :]
         return carry
 
-    lax.fori_loop(0, outs[0].shape[0], block, 0, unroll=4)
+    lax.fori_loop(0, row_blocks, block, 0, unroll=4)
     for s in range(CAP):
         place = local[2 + CAP + s]
 
         @pl.when(place >= 0)
         def _():
-            for q in range(col_count):
-                outs[q][place] += held[s, q]
-
-    for q in range(col_count):
-        outs[q][0] = jnp.zeros_like(outs[q][0])
+            for q, (out, base) in target.items():
+                out[base + place] += held[s, q]
+
+    for out, base in target.values():
+        out[base] = jnp.zeros_like(out[base])
 
 
 def split_front(local, front, tiles, row_blocks):
     col_count, rows, size = tiles.shape[1:]
-    return pl.pallas_call(
-        functools.partial(split_kernel, rows),
-        out_shape=[jax.ShapeDtypeStruct((row_blocks, rows, size), jnp.float32)] * col_count,
+    kept = [q for q in range(col_count) if q not in RELAY]
+    depth = [row_blocks * (1 + list(RELAY.values()).count(q)) for q in kept]
+    outs = pl.pallas_call(
+        functools.partial(split_kernel, rows, row_blocks),
+        out_shape=[jax.ShapeDtypeStruct((d, rows, size), jnp.float32) for d in depth],
         in_specs=[
             pl.BlockSpec(memory_space=SMEM),
             pl.BlockSpec(memory_space=VMEM),
             pl.BlockSpec(memory_space=ANY),
         ],
-        out_specs=[pl.BlockSpec(memory_space=VMEM)] * col_count,
+        out_specs=[pl.BlockSpec(memory_space=VMEM)] * len(kept),
         scratch_shapes=[
             VMEM((CAP, col_count, rows, size), jnp.float32),
             pltpu.SemaphoreType.DMA((CAP,)),
@@ -211,6 +216,7 @@
         compiler_params=LIMIT,
         name="split_front",
     )(local, front, tiles)
+    return dict(zip(kept, outs))
 
 
 def slices_kernel(row_blocks, part_0, part_1, arrived, windows, column, total):
@@ -270,7 +276,7 @@
 
         @pl.when(local[1] == k)
         def _():
-            load = pltpu.make_async_copy(own[k], held, load_sem)
+            load = pltpu.make_async_copy(own[k].at[pl.ds(0, row_blocks)], held, load_sem)
             load.start()
             load.wait()
 
@@ -439,19 +445,21 @@
     )
     sliced = pack_panel(panel_tiles, local, message, tiles, flat_front, row_count, col_count)
     sliced = lax.all_to_all(sliced, both, split_axis=0, concat_axis=0, tiled=True)
-    own = list(split_front(local, flat_front, tiles, row_blocks))
-    for k in (7, 2, 4, 5, 3):
+    own = split_front(local, flat_front, tiles, row_blocks)
+    for k in (7, 1, 2, 4, 6):
         own[k] = lax.ppermute(own[k], "col", [(0, k)])
     first, second = pack(slot, tiles, devices)
     sliced = after(sliced, first)
     message = sliced[:, -1, 0, : 2 * CAP].astype(jnp.int32)
     main, part = ([message[:, h * CAP + s] for s in range(CAP)] for h in range(2))
     windows, column = sum_slices(part, sliced, row_count, row_blocks)
-    for k in (6, 1):
-        own[k] = lax.ppermute(after(own[k], column), "col", [(0, k)])
+    handed = own[7][row_blocks:] + own[1][row_blocks:]
+    handed = lax.ppermute(after(handed, column), "col", [(via, k) for k, via in RELAY.items()])
+    own.update({k: handed for k in RELAY})
     windows = lax.all_to_all(windows, "row", split_axis=0, concat_axis=0, tiled=True)
-    first = after(first, windows, *(own[k] for k in (7, 2, 4, 5, 3, 6, 1)))
+    first = after(first, windows, *(own[k] for k in (7, 1, 2, 4, 6, 5)))
     first = lax.all_to_all(first, both, split_axis=0, concat_axis=0, tiled=True)
+    own = [own[k] for k in range(col_count)]
     column = after(spread(local, windows, column, own), first)
     column = lax.all_to_all(column, "col", split_axis=0, concat_axis=0, tiled=True)
     second = lax.all_to_all(

time: 371 us -> 376 us (1.013)
  waiting for transfers between devices: 163 us -> 171 us
  starting transfers between devices: 49.6 us -> 45.3 us
    all_to_all x1, waiting for transfers between devices: 9.7 us -> 0.01 us  [per_device(): lax.all_to_all(sliced, both, split_axis=0, concat_axis=0, tiled=True)]
    ppermute x5, waiting for transfers between devices: 10.1 us -> 19.5 us  [per_device(): own[k] = lax.ppermute(own[k], 'col', [(0, k)])]
    all_to_all x1, waiting for transfers between devices: 0.01 us -> 7.93 us  [per_device(): lax.all_to_all(windows, 'row', split_axis=0, concat_axis=0, tiled=True)]
  transfers between devices with their start and end apart: 11 -> 10, of which waited for: 5 -> 5; matrix products, arithmetic and copies ran while one was open for 8% -> 8% of each run, Pallas kernels for 17% -> 17%
where the time goes in v12:
time: 376 us; the launch traced here: 375 us
  waiting for transfers between devices  171 us (45%)
  Pallas kernels  77.1 us (21%)
  starting transfers between devices  45.3 us (12%)
  blocking collectives  42.9 us (11%)
  other arithmetic  29.7 us (8%)
  local copies, waits for them, and re-layouts  8.27 us (2%)
    all_to_all x1, waiting for transfers between devices, per_device(): first = lax.all_to_all(first, both, split_axis=0, concat_axis=0, tiled=True)  105 us
    all_to_all x1, blocking collectives, per_device(): lax.all_to_all(column, 'col', split_axis=0, concat_axis=0, tiled=True)  42.9 us
    all_to_all x1, waiting for transfers between devices, per_device(): lax.all_to_all(after(second, column), both, split_axis=0, concat_axis=0,...  38.7 us
    pallas_call x1, Pallas kernels, update_front(): pl.pallas_call(functools.partial(update_kernel, (row_count, row_blocks)),...  31.2 us
    ppermute x5, waiting for transfers between devices, per_device(): own[k] = lax.ppermute(own[k], 'col', [(0, k)])  19.5 us
    pallas_call x2, Pallas kernels, add_tiles(): pl.pallas_call(functools.partial(add_kernel, chunks), out_shape=jax.Shape...  19.4 us
    ppermute x5, starting transfers between devices, per_device(): own[k] = lax.ppermute(own[k], 'col', [(0, k)])  12.9 us
    another operation x3, other arithmetic, per_device(): factor = jnp.linalg.cholesky(0.5 * (corner + corner.T))  12.5 us
  transfers between devices with their start and end apart: 10, of which 5 were waited for; matrix products, arithmetic and copies ran while one was open for 8% of the time, Pallas kernels for 17%

profile of v12, /device:TPU:0, one launch (start us, length us, event | category | flops | bytes accessed | tf_op | source)
XLA Modules:
  0.0 375.2 jit_solution(3172518084853697015)
XLA Ops:
  5.9 5.0 %pack_panel.1 = f32[16,8,5,8,128]{4,3,2,1,0:T(8,128)} custom-call(s32[32]{0:T(128)} %select_reduce_fusion.1.panel_tiles, s32[6]{0:T(128)} %pad_add_fusion.local.where, f32[16,8,8,128]{3,2,1,0:T(8,128)} %bitcast.86, f32[128,8,2,8,128]{4,3,2,1,0:T(8,128)} %bitcast.79, f32[12288,128]{1,0:T(8,128)} %bitcast.82), custom_call_target="tpu_custom_call" | custom-call | tf_op jit(solution)/shard_map/pack_panel/pallas_call | solution.py:98
  10.9 11.1 %all-to-all-start = ((f32[128,5,8,128]{3,2,1,0:T(8,128)}), f32[128,5,8,128]{3,2,1,0:T(8,128)S(1)}, u32[]{:S(2)}, u32[]{:S(2)}) async-start(f32[128,5,8,128]{3,2,1,0:T(8,128)} %bitcast.85), calls=%async_computation | async-start | bytes 5242880 | tf_op jit(solution)/shard_map/all_to_all | solution.py:447
  22.0 6.4 %split_front.1 = (f32[48,16,128]{2,1,0:T(8,128)}, f32[96,16,128]{2,1,0:T(8,128)}, f32[48,16,128]{2,1,0:T(8,128)}, f32[48,16,128]{2,1,0:T(8,128)}, f32[48,16,128]{2,1,0:T(8,128)}, /*index=5*/f32[96,16,128]{2,1,0:T(8,128)}) custom-call(s32[6]{0:T(128)} %pad_add_fusion.local.where, f32[12288,128]{1,0:T(8,128)} %bitcast.83, f32[128,8,16,128]{3,2,1,0:T(8,128)} %bitcast.80), custom_call_target="tpu_custom_call" | custom-call | tf_op jit(solution)/shard_map/split_front/pallas_call | solution.py:203
  28.5 5.3 %collective-permute-start = (f32[96,16,128]{2,1,0:T(8,128)}, f32[96,16,128]{2,1,0:T(8,128)S(1)}, u32[]{:S(2)}, u32[]{:S(2)}) collective-permute-start(f32[96,16,128]{2,1,0:T(8,128)} %get-tuple-element.17), channel_id=1, source_target_pairs={{0,7},{8,15},{16,23},{24,31},{32,39},{40,47},{48,55},{56,63},{64,7... | collective-permute-start | bytes 2359304 | tf_op jit(solution)/shard_map/ppermute | solution.py:450
  35.2 2.1 collective-permute-start.2
  37.2 2.1 collective-permute-start.3
  39.3 2.0 collective-permute-start.4
  41.3 7.0 %pack.1 = (f32[128,8,16,128]{3,2,1,0:T(8,128)}, f32[128,8,16,128]{3,2,1,0:T(8,128)}) custom-call(s32[128]{0:T(128)} %copy-done.5, f32[128,8,16,128]{3,2,1,0:T(8,128)} %bitcast.81), custom_call_target="tpu_custom_call" | custom-call | tf_op jit(solution)/shard_map/pack/pallas_call | solution.py:155
  48.3 19.4 %collective-permute-done.refs_2_.refs_7_ = f32[96,16,128]{2,1,0:T(8,128)S(1)} collective-permute-done((f32[96,16,128]{2,1,0:T(8,128)}, f32[96,16,128]{2,1,0:T(8,128)S(1)}, u32[]{:S(2)}, u32[]{:S(2)}) %collective-permute-start) | collective-permute-done | bytes 786464 | tf_op jit(solution)/shard_map/ppermute | solution.py:450
  69.7 1.5 copy-done
  73.0 3.8 %sum_slices.1 = (f32[16,16,128]{2,1,0:T(8,128)}, f32[48,16,128]{2,1,0:T(8,128)}) custom-call(s32[128]{0:T(128)} %get-tuple-element.26.part_0, s32[128]{0:T(128)} %get-tuple-element.25.part_1, f32[128,5,8,128]{3,2,1,0:T(8,128)} %after.5.arrived), custom_call_target="tpu_custom_call" | custom-call | tf_op jit(solution)/shard_map/sum_slices/pallas_call | solution.py:248
  77.5 6.9 %all-to-all-start.1 = ((f32[16,16,128]{2,1,0:T(8,128)}), f32[16,16,128]{2,1,0:T(8,128)S(1)}, u32[]{:S(2)}, u32[]{:S(2)}) async-start(f32[16,16,128]{2,1,0:T(8,128)} %get-tuple-element.16), calls=%async_computation.1 | async-start | bytes 262144 | tf_op jit(solution)/shard_map/all_to_all | solution.py:459
  84.5 7.9 %all-to-all-done.1.refs_1_.windows = f32[16,16,128]{2,1,0:T(8,128)S(1)} async-done(((f32[16,16,128]{2,1,0:T(8,128)}), f32[16,16,128]{2,1,0:T(8,128)S(1)}, u32[]{:S(2)}, u32[]{:S(2)}) %all-to-all-start.1) | async-done | bytes 131104 | tf_op jit(solution)/shard_map/all_to_all | solution.py:459
  93.8 7.6 %all-to-all-start.2 = ((f32[128,8,16,128]{3,2,1,0:T(8,128)}), f32[128,8,16,128]{3,2,1,0:T(8,128)}, u32[]{:S(2)}, u32[]{:S(2)}) async-start(f32[128,8,16,128]{3,2,1,0:T(8,128)} %after.7), calls=%async_computation.2 | async-start | bytes 16777216 | tf_op jit(solution)/shard_map/all_to_all | solution.py:461
  101.5 4.2 %spread.1.refs_0_ = f32[8,51,16,128]{3,2,1,0:T(8,128)} custom-call(s32[6]{0:T(128)} %pad_add_fusion.local.where, f32[16,16,128]{2,1,0:T(8,128)} %copy-done.4, f32[48,16,128]{2,1,0:T(8,128)} %get-tuple-element.22.refs_1_.column, f32[48,16,128]{2,1,0:T(8,128)} %get-tuple-element.23.refs_0_, f32[96,16,128]{2,1,0:T(8,128)} %copy-done.2, ...), custom_call_target="tpu_custom_call" | custom-call | tf_op jit(solution)/shard_map/spread/pallas_call | solution.py:299
  105.7 104.6 %all-to-all-done.2.tiles.refs_1_ = f32[128,8,16,128]{3,2,1,0:T(8,128)} async-done(((f32[128,8,16,128]{3,2,1,0:T(8,128)}), f32[128,8,16,128]{3,2,1,0:T(8,128)}, u32[]{:S(2)}, u32[]{:S(2)}) %all-to-all-start.2) | async-done | bytes 8388640 | tf_op jit(solution)/shard_map/all_to_all | solution.py:461
  210.3 42.9 %all_to_all.25.column.refs_1_ = f32[8,51,16,128]{3,2,1,0:T(8,128)} all-to-all(f32[8,51,16,128]{3,2,1,0:T(8,128)} %after.8), channel_id=1, replica_groups=mesh['row'=16,'col'=8] {'col'}, dimensions={0} | all-to-all | bytes 6684672 | tf_op jit(solution)/shard_map/all_to_all | solution.py:464
  253.1 6.1 %all-to-all-start.4 = ((f32[128,8,16,128]{3,2,1,0:T(8,128)}), f32[128,8,16,128]{3,2,1,0:T(8,128)}, u32[]{:S(2)}, u32[]{:S(2)}) async-start(f32[128,8,16,128]{3,2,1,0:T(8,128)} %after.9), calls=%async_computation.4 | async-start | bytes 16777216 | tf_op jit(solution)/shard_map/all_to_all | solution.py:465
  259.2 9.7 %add_tiles.2.front = f32[12288,128]{1,0:T(8,128)} custom-call(s32[128]{0:T(128)} %get-tuple-element.27.places, f32[12288,128]{1,0:T(8,128)} %bitcast.84, f32[128,8,16,128]{3,2,1,0:T(8,128)} %all-to-all-done.2.tiles.refs_1_), custom_call_target="tpu_custom_call" | custom-call | tf_op jit(solution)/shard_map/add_tiles/pallas_call | solution.py:350
  270.0 11.7 %cholesky.14 = f32[128,128]{1,0:T(8,128)S(1)} custom-call(f32[128,128]{1,0:T(8,128)S(1)} %fusion.3), custom_call_target="Cholesky" | custom-call | tf_op jit(solution)/shard_map/jit(cholesky)/cholesky | solution.py:470
  283.1 9.8 %custom-call.7 = f32[1,128,128]{1,2,0:T(8,128)S(1)} custom-call(f32[1,128,128]{2,1,0:T(8,128)S(1)} %fusion), custom_call_target="InvertDiagBlocksLowerTriangular" | custom-call | tf_op jit(solution)/shard_map/jit(_solve_triangular)/triangular_solve | solution.py:471
  295.4 31.2 %update_front.1.base = f32[12288,128]{1,0:T(8,128)} custom-call(s32[6]{0:T(128)} %pad_add_fusion.local.where, f32[12288,128]{1,0:T(8,128)} %add_tiles.2.front, f32[128,128]{1,0:T(8,128)} %fusion.1.inverse_t, f32[256,128]{1,0:T(8,128)} %bitcast.89, f32[8,51,16,128]{3,2,1,0:T(8,128)} %all_to_all.25.column.refs_1_), custom_call_target="tpu_custom_call" | custom-call | tf_op jit(solution)/shard_map/update_front/pallas_call | solution.py:401
  326.6 38.7 %all-to-all-done.4.tiles = f32[128,8,16,128]{3,2,1,0:T(8,128)} async-done(((f32[128,8,16,128]{3,2,1,0:T(8,128)}), f32[128,8,16,128]{3,2,1,0:T(8,128)}, u32[]{:S(2)}, u32[]{:S(2)}) %all-to-all-start.4) | async-done | bytes 8388640 | tf_op jit(solution)/shard_map/all_to_all | solution.py:465
  365.3 9.7 %add_tiles.3 = f32[12288,128]{1,0:T(8,128)} custom-call(s32[128]{0:T(128)} %get-tuple-element.28.places, f32[12288,128]{1,0:T(8,128)} %update_front.1.base, f32[128,8,16,128]{3,2,1,0:T(8,128)} %all-to-all-done.4.tiles), custom_call_target="tpu_custom_call" | custom-call | tf_op jit(solution)/shard_map/add_tiles/pallas_call | solution.py:350
  (59 shorter events, 17.9 us)
Async XLA Ops:
  2.9 8.0 %copy-start.5 = (s32[128]{0:T(128)}, s32[128]{0:T(128)S(1)}, u32[]{:S(2)}) copy-start(s32[128]{0:T(128)S(1)} %get-tuple-element.40.slot) | copy-start | bytes 1540
  10.9 58.7 %all-to-all-start = ((f32[128,5,8,128]{3,2,1,0:T(8,128)}), f32[128,5,8,128]{3,2,1,0:T(8,128)S(1)}, u32[]{:S(2)}, u32[]{:S(2)}) async-start(f32[128,5,8,128]{3,2,1,0:T(8,128)} %bitcast.85), calls=%async_computation | async-start | bytes 5242880 | tf_op jit(solution)/shard_map/all_to_all | solution.py:447
  28.5 39.2 %collective-permute-start = (f32[96,16,128]{2,1,0:T(8,128)}, f32[96,16,128]{2,1,0:T(8,128)S(1)}, u32[]{:S(2)}, u32[]{:S(2)}) collective-permute-start(f32[96,16,128]{2,1,0:T(8,128)} %get-tuple-element.17), channel_id=1, source_target_pairs={{0,7},{8,15},{16,23},{24,31},{32,39},{40,47},{48,55},{56,63},{64,7... | collective-permute-start | bytes 2359304 | tf_op jit(solution)/shard_map/ppermute | solution.py:450
  33.8 34.0 %collective-permute-start.1 = (f32[96,16,128]{2,1,0:T(8,128)}, f32[96,16,128]{2,1,0:T(8,128)S(1)}, u32[]{:S(2)}, u32[]{:S(2)}) collective-permute-start(f32[96,16,128]{2,1,0:T(8,128)} %get-tuple-element.18), channel_id=1, source_target_pairs={{0,1},{8,9},{16,17},{24,25},{32,33},{40,41},{48,49},{56,57},{64,65... | collective-permute-start | bytes 2359304 | tf_op jit(solution)/shard_map/ppermute | solution.py:450
  35.2 49.3 %collective-permute-start.2 = (f32[48,16,128]{2,1,0:T(8,128)}, f32[48,16,128]{2,1,0:T(8,128)}, u32[]{:S(2)}, u32[]{:S(2)}) collective-permute-start(f32[48,16,128]{2,1,0:T(8,128)} %get-tuple-element.19), channel_id=1, source_target_pairs={{0,2},{8,10},{16,18},{24,26},{32,34},{40,42},{48,50},{56,58},{64,6... | collective-permute-start | bytes 1179656 | tf_op jit(solution)/shard_map/ppermute | solution.py:450
  37.2 47.3 %collective-permute-start.3 = (f32[48,16,128]{2,1,0:T(8,128)}, f32[48,16,128]{2,1,0:T(8,128)}, u32[]{:S(2)}, u32[]{:S(2)}) collective-permute-start(f32[48,16,128]{2,1,0:T(8,128)} %get-tuple-element.20), channel_id=1, source_target_pairs={{0,4},{8,12},{16,20},{24,28},{32,36},{40,44},{48,52},{56,60},{64,6... | collective-permute-start | bytes 1179656 | tf_op jit(solution)/shard_map/ppermute | solution.py:450
  39.3 45.2 %collective-permute-start.4 = (f32[48,16,128]{2,1,0:T(8,128)}, f32[48,16,128]{2,1,0:T(8,128)}, u32[]{:S(2)}, u32[]{:S(2)}) collective-permute-start(f32[48,16,128]{2,1,0:T(8,128)} %get-tuple-element.21), channel_id=1, source_target_pairs={{0,6},{8,14},{16,22},{24,30},{32,38},{40,46},{48,54},{56,62},{64,7... | collective-permute-start | bytes 1179656 | tf_op jit(solution)/shard_map/ppermute | solution.py:450
  67.7 3.5 copy-start.1
  67.8 1.1 copy-start.2
  69.7 1.5 copy-start
  76.8 15.6 %collective-permute-start.5 = (f32[48,16,128]{2,1,0:T(8,128)}, f32[48,16,128]{2,1,0:T(8,128)S(1)}, u32[]{:S(2)}, u32[]{:S(2)}) collective-permute-start(f32[48,16,128]{2,1,0:T(8,128)} %after.6), channel_id=1, source_target_pairs={{7,5},{1,3},{15,13},{9,11},{23,21},{17,19},{31,29},{25,27},{39,37}... | collective-permute-start | bytes 1179656 | tf_op jit(solution)/shard_map/ppermute | solution.py:457
  77.5 14.9 %all-to-all-start.1 = ((f32[16,16,128]{2,1,0:T(8,128)}), f32[16,16,128]{2,1,0:T(8,128)S(1)}, u32[]{:S(2)}, u32[]{:S(2)}) async-start(f32[16,16,128]{2,1,0:T(8,128)} %get-tuple-element.16), calls=%async_computation.1 | async-start | bytes 262144 | tf_op jit(solution)/shard_map/all_to_all | solution.py:459
  92.4 0.6 copy-start.4
  93.1 0.8 copy-start.3
  93.8 116.4 %all-to-all-start.2 = ((f32[128,8,16,128]{3,2,1,0:T(8,128)}), f32[128,8,16,128]{3,2,1,0:T(8,128)}, u32[]{:S(2)}, u32[]{:S(2)}) async-start(f32[128,8,16,128]{3,2,1,0:T(8,128)} %after.7), calls=%async_computation.2 | async-start | bytes 16777216 | tf_op jit(solution)/shard_map/all_to_all | solution.py:461
  253.1 112.1 %all-to-all-start.4 = ((f32[128,8,16,128]{3,2,1,0:T(8,128)}), f32[128,8,16,128]{3,2,1,0:T(8,128)}, u32[]{:S(2)}, u32[]{:S(2)}) async-start(f32[128,8,16,128]{3,2,1,0:T(8,128)} %after.9), calls=%async_computation.4 | async-start | bytes 16777216 | tf_op jit(solution)/shard_map/all_to_all | solution.py:465

commit v13 on v5

--- a/solution.py
+++ b/solution.py
@@ -12,6 +12,7 @@
 SMEM = pltpu.SMEM
 VMEM = pltpu.VMEM
 ANY = pl.ANY
+RELAY = {5: 7, 3: 1}
 LIMIT = pltpu.CompilerParams(vmem_limit_bytes=58 << 20)
 
 
@@ -134,44 +135,48 @@
     )(slot, panel_tiles, local, tiles, front)
 
 
-def split_kernel(rows, local, front, tiles, *refs):
+def split_kernel(rows, row_blocks, local, front, tiles, *refs):
     outs, (held, sem) = refs[:-2], refs[-2:]
-    col_count = len(outs)
+    col_count = len(outs) + len(RELAY)
+    kept = [q for q in range(col_count) if q not in RELAY]
+    target = {q: (outs[kept.index(RELAY.get(q, q))], row_blocks * (q in RELAY)) for q in range(col_count)}
     for s in range(CAP):
         copy = pltpu.make_async_copy(tiles.at[local[2 + s]], held.at[s], sem.at[s])
         copy.start()
         copy.wait()
 
     def block(a, carry):
-        for q in range(col_count):
+        for q, (out, base) in target.items():
             start = (a * col_count + q) * rows * 2
-            outs[q][a] = front[pl.ds(start, rows, stride=2), :]
+            out[base + a] = front[pl.ds(start, rows, stride=2), :]
         return carry
 
-    lax.fori_loop(0, outs[0].shape[0], block, 0, unroll=4)
+    lax.fori_loop(0, row_blocks, block, 0, unroll=4)
     for s in range(CAP):
         place = local[2 + CAP + s]
 
         @pl.when(place >= 0)
         def _():
-            for q in range(col_count):
-                outs[q][place] += held[s, q]
-
-    for q in range(col_count):
-        outs[q][0] = jnp.zeros_like(outs[q][0])
+            for q, (out, base) in target.items():
+                out[base + place] += held[s, q]
+
+    for out, base in target.values():
+        out[base] = jnp.zeros_like(out[base])
 
 
 def split_front(local, front, tiles, row_blocks):
     col_count, rows, size = tiles.shape[1:]
-    return pl.pallas_call(
-        functools.partial(split_kernel, rows),
-        out_shape=[jax.ShapeDtypeStruct((row_blocks, rows, size), jnp.float32)] * col_count,
+    kept = [q for q in range(col_count) if q not in RELAY]
+    depth = [row_blocks * (1 + list(RELAY.values()).count(q)) for q in kept]
+    outs = pl.pallas_call(
+        functools.partial(split_kernel, rows, row_blocks),
+        out_shape=[jax.ShapeDtypeStruct((d, rows, size), jnp.float32) for d in depth],
         in_specs=[
             pl.BlockSpec(memory_space=SMEM),
             pl.BlockSpec(memory_space=VMEM),
             pl.BlockSpec(memory_space=ANY),
         ],
-        out_specs=[pl.BlockSpec(memory_space=VMEM)] * col_count,
+        out_specs=[pl.BlockSpec(memory_space=VMEM)] * len(kept),
         scratch_shapes=[
             VMEM((CAP, col_count, rows, size), jnp.float32),
             pltpu.SemaphoreType.DMA((CAP,)),
@@ -179,6 +184,7 @@
         compiler_params=LIMIT,
         name="split_front",
     )(local, front, tiles)
+    return dict(zip(kept, outs))
 
 
 def slices_kernel(row_blocks, part_0, part_1, arrived, windows, column, total):
@@ -223,7 +229,7 @@
 
         @pl.when(local[1] == k)
         def _():
-            copy = pltpu.make_async_copy(own[k], held, sem)
+            copy = pltpu.make_async_copy(own[k].at[pl.ds(0, row_blocks)], held, sem)
             copy.start()
             copy.wait()
 
@@ -385,9 +391,13 @@
     main, part = ([message[:, h * CAP + s] for s in range(CAP)] for h in range(2))
     first, second = pack(slot, panel_tiles, local, tiles, flat_front, row_count, col_count)
     first = first.reshape((devices,) + first.shape[2:])
-    own = list(split_front(local, flat_front, tiles, row_blocks))
-    for k in (7, 2, 4, 5, 3, 1, 6):
+    own = split_front(local, flat_front, tiles, row_blocks)
+    for k in (7, 1, 2, 4, 6):
         own[k] = lax.ppermute(own[k], "col", [(0, k)])
+    handed = own[7][row_blocks:] + own[1][row_blocks:]
+    handed = lax.ppermute(handed, "col", [(via, k) for k, via in RELAY.items()])
+    own.update({k: handed for k in RELAY})
+    own = [own[k] for k in range(col_count)]
     arrived = lax.all_to_all(first, both, split_axis=0, concat_axis=0, tiled=True)
     windows, column = sum_slices(part, arrived, row_count, row_blocks)
     windows = lax.all_to_all(windows, "row", split_axis=0, concat_axis=0, tiled=True)

time: 368 us -> 371 us (level)
    all_to_all x1, waiting for transfers between devices: 0.01 us -> 7.88 us  [per_device(): lax.all_to_all(windows, 'row', split_axis=0, concat_axis=0, tiled=True)]
    all_to_all x1, starting transfers between devices: 10.2 us -> 6.1 us  [per_device(): lax.all_to_all(after(second, column), both, split_axis=0, concat_axis=0,...]
    all_to_all x1, starting transfers between devices: 4.22 us -> 8.32 us  [per_device(): lax.all_to_all(windows, 'row', split_axis=0, concat_axis=0, tiled=True)]
    ppermute x7 -> x5, waiting for transfers between devices: 127 us -> 123 us  [per_device(): own[k] = lax.ppermute(own[k], 'col', [(0, k)])]
    ppermute x7 -> x5, starting transfers between devices: 10.8 us -> 9.93 us  [per_device(): own[k] = lax.ppermute(own[k], 'col', [(0, k)])]
  transfers between devices with their start and end apart: 11 -> 10, of which waited for: 6 -> 4; matrix products, arithmetic and copies ran while one was open for 8% -> 8% of each run, Pallas kernels for 16% -> 16%
where the time goes in v13:
time: 371 us; the launch traced here: 370 us
  waiting for transfers between devices  169 us (46%)
  Pallas kernels  72.9 us (20%)
  starting transfers between devices  46.5 us (13%)
  blocking collectives  46.2 us (12%)
  other arithmetic  28.5 us (8%)
  local copies, waits for them, and re-layouts  4.79 us (1%)
    ppermute x5, waiting for transfers between devices, per_device(): own[k] = lax.ppermute(own[k], 'col', [(0, k)])  123 us
    all_to_all x1, blocking collectives, per_device(): lax.all_to_all(column, 'col', split_axis=0, concat_axis=0, tiled=True)  46.2 us
    all_to_all x1, waiting for transfers between devices, per_device(): lax.all_to_all(after(second, column), both, split_axis=0, concat_axis=0,...  38.7 us
    pallas_call x1, Pallas kernels, update_front(): pl.pallas_call(functools.partial(update_kernel, (row_count, row_blocks)),...  31.3 us
    pallas_call x2, Pallas kernels, add_tiles(): pl.pallas_call(functools.partial(add_kernel, chunks), out_shape=jax.Shape...  19.4 us
    another operation x3, other arithmetic, per_device(): factor = jnp.linalg.cholesky(0.5 * (corner + corner.T))  12.4 us
    all_to_all x1, starting transfers between devices, per_device(): lax.all_to_all(message, both, split_axis=0, concat_axis=0, tiled=True)  11.2 us
    another operation x2, other arithmetic, per_device(): jax.scipy.linalg.solve_triangular(factor, jnp.eye(size, dtype=jnp.float32...  10.4 us
  transfers between devices with their start and end apart: 10, of which 4 were waited for; matrix products, arithmetic and copies ran while one was open for 8% of the time, Pallas kernels for 16%

profile of v13, /device:TPU:0, one launch (start us, length us, event | category | flops | bytes accessed | tf_op | source)
XLA Modules:
  0.0 369.6 jit_solution(7879626155262478782)
XLA Ops:
  4.1 11.2 %all-to-all-start = ((s32[128,1,4]{2,1,0:T(1,128)}), s32[128,1,4]{2,1,0:T(1,128)S(1)}, u32[]{:S(2)}, u32[]{:S(2)}) async-start(s32[128,1,4]{2,1,0:T(1,128)} %copy.21), calls=%async_computation | async-start | bytes 131072 | tf_op jit(solution)/shard_map/all_to_all | solution.py:390
  16.8 7.8 %pack.1 = (f32[16,8,10,16,128]{4,3,2,1,0:T(8,128)}, f32[128,8,16,128]{3,2,1,0:T(8,128)}) custom-call(s32[128]{0:T(128)} %copy-done.7, s32[32]{0:T(128)} %select_reduce_fusion.1.panel_tiles, s32[6]{0:T(128)} %pad_add_fusion.local.where, f32[128,8,16,128]{3,2,1,0:T(8,128)} %bitcast.78, f32[12288,128]{1,0:T(8,128)} %bitcast.75), custom_call_target="tpu_custom_call" | custom-call | tf_op jit(solution)/shard_map/pack/pallas_call | solution.py:116
  24.6 10.3 %all-to-all-start.1 = ((f32[128,10,16,128]{3,2,1,0:T(8,128)}), f32[128,10,16,128]{3,2,1,0:T(8,128)}, u32[]{:S(2)}, u32[]{:S(2)}) async-start(f32[128,10,16,128]{3,2,1,0:T(8,128)} %bitcast.80), calls=%async_computation.1 | async-start | bytes 20971520 | tf_op jit(solution)/shard_map/all_to_all | solution.py:401
  34.9 6.4 %split_front.1 = (f32[48,16,128]{2,1,0:T(8,128)}, f32[96,16,128]{2,1,0:T(8,128)}, f32[48,16,128]{2,1,0:T(8,128)}, f32[48,16,128]{2,1,0:T(8,128)}, f32[48,16,128]{2,1,0:T(8,128)}, /*index=5*/f32[96,16,128]{2,1,0:T(8,128)}) custom-call(s32[6]{0:T(128)} %pad_add_fusion.local.where, f32[12288,128]{1,0:T(8,128)} %bitcast.76, f32[128,8,16,128]{3,2,1,0:T(8,128)} %bitcast.79), custom_call_target="tpu_custom_call" | custom-call | tf_op jit(solution)/shard_map/split_front/pallas_call | solution.py:171
  41.3 3.0 collective-permute-start
  44.3 3.0 collective-permute-start.2
  47.3 1.3 collective-permute-start.1
  48.7 1.3 collective-permute-start.4
  50.0 1.3 collective-permute-start.5
  51.3 116.0 %collective-permute-done.refs_1_ = f32[96,16,128]{2,1,0:T(8,128)S(1)} collective-permute-done((f32[96,16,128]{2,1,0:T(8,128)}, f32[96,16,128]{2,1,0:T(8,128)S(1)}, u32[]{:S(2)}, u32[]{:S(2)}) %collective-permute-start) | collective-permute-done | bytes 786464 | tf_op jit(solution)/shard_map/ppermute | solution.py:396
  167.3 6.7 %collective-permute-done.2.refs_7_ = f32[96,16,128]{2,1,0:T(8,128)S(1)} collective-permute-done((f32[96,16,128]{2,1,0:T(8,128)}, f32[96,16,128]{2,1,0:T(8,128)S(1)}, u32[]{:S(2)}, u32[]{:S(2)}) %collective-permute-start.2) | collective-permute-done | bytes 786464 | tf_op jit(solution)/shard_map/ppermute | solution.py:396
  176.3 4.0 %sum_slices.1 = (f32[16,16,128]{2,1,0:T(8,128)}, f32[48,16,128]{2,1,0:T(8,128)}) custom-call(s32[128]{0:T(128)} %get-tuple-element.26.part_0, s32[128]{0:T(128)} %get-tuple-element.25.part_1, f32[128,10,16,128]{3,2,1,0:T(8,128)} %all-to-all-done.1.tiles.arrived), custom_call_target="tpu_custom_call" | custom-call | tf_op jit(solution)/shard_map/sum_slices/pallas_call | solution.py:211
  180.4 8.3 %all-to-all-start.2 = ((f32[16,16,128]{2,1,0:T(8,128)}), f32[16,16,128]{2,1,0:T(8,128)S(1)}, u32[]{:S(2)}, u32[]{:S(2)}) async-start(f32[16,16,128]{2,1,0:T(8,128)} %get-tuple-element.16), calls=%async_computation.2 | async-start | bytes 262144 | tf_op jit(solution)/shard_map/all_to_all | solution.py:403
  188.8 7.9 %all-to-all-done.2.windows = f32[16,16,128]{2,1,0:T(8,128)S(1)} async-done(((f32[16,16,128]{2,1,0:T(8,128)}), f32[16,16,128]{2,1,0:T(8,128)S(1)}, u32[]{:S(2)}, u32[]{:S(2)}) %all-to-all-start.2) | async-done | bytes 131104 | tf_op jit(solution)/shard_map/all_to_all | solution.py:403
  197.3 4.0 %spread.1 = f32[8,51,16,128]{3,2,1,0:T(8,128)} custom-call(s32[6]{0:T(128)} %pad_add_fusion.local.where, f32[16,16,128]{2,1,0:T(8,128)} %copy-done.3, f32[48,16,128]{2,1,0:T(8,128)} %get-tuple-element.17.column, f32[48,16,128]{2,1,0:T(8,128)} %get-tuple-element.18.refs_0_, f32[96,16,128]{2,1,0:T(8,128)} %copy-done, f32[48,16,128]{2,1,0:T(8,128)} %copy-done.4, ...), custom_call_target="tpu_custom_call" | custom-call | tf_op jit(solution)/shard_map/spread/pallas_call | solution.py:247
  201.3 46.2 %all_to_all.29.column.refs_1_ = f32[8,51,16,128]{3,2,1,0:T(8,128)} all-to-all(f32[8,51,16,128]{3,2,1,0:T(8,128)} %spread.1), channel_id=1, replica_groups=mesh['row'=16,'col'=8] {'col'}, dimensions={0} | all-to-all | bytes 6684672 | tf_op jit(solution)/shard_map/all_to_all | solution.py:405
  247.6 6.1 %all-to-all-start.4 = ((f32[128,8,16,128]{3,2,1,0:T(8,128)}), f32[128,8,16,128]{3,2,1,0:T(8,128)}, u32[]{:S(2)}, u32[]{:S(2)}) async-start(f32[128,8,16,128]{3,2,1,0:T(8,128)} %after.1), calls=%async_computation.4 | async-start | bytes 16777216 | tf_op jit(solution)/shard_map/all_to_all | solution.py:406
  253.7 9.7 %add_tiles.2.front = f32[12288,128]{1,0:T(8,128)} custom-call(s32[128]{0:T(128)} %get-tuple-element.27.places, f32[12288,128]{1,0:T(8,128)} %bitcast.77, f32[128,10,16,128]{3,2,1,0:T(8,128)} %all-to-all-done.1.tiles.arrived), custom_call_target="tpu_custom_call" | custom-call | tf_op jit(solution)/shard_map/add_tiles/pallas_call | solution.py:294
  264.4 11.7 %cholesky.14 = f32[128,128]{1,0:T(8,128)S(1)} custom-call(f32[128,128]{1,0:T(8,128)S(1)} %fusion.3), custom_call_target="Cholesky" | custom-call | tf_op jit(solution)/shard_map/jit(cholesky)/cholesky | solution.py:411
  277.5 9.8 %custom-call.7 = f32[1,128,128]{1,2,0:T(8,128)S(1)} custom-call(f32[1,128,128]{2,1,0:T(8,128)S(1)} %fusion), custom_call_target="InvertDiagBlocksLowerTriangular" | custom-call | tf_op jit(solution)/shard_map/jit(_solve_triangular)/triangular_solve | solution.py:412
  287.3 0.9 slice_bitcast_fusion
  289.7 31.3 %update_front.1.base = f32[12288,128]{1,0:T(8,128)} custom-call(s32[6]{0:T(128)} %pad_add_fusion.local.where, f32[12288,128]{1,0:T(8,128)} %add_tiles.2.front, f32[128,128]{1,0:T(8,128)} %fusion.1.inverse_t, f32[256,128]{1,0:T(8,128)} %bitcast.83, f32[8,51,16,128]{3,2,1,0:T(8,128)} %all_to_all.29.column.refs_1_), custom_call_target="tpu_custom_call" | custom-call | tf_op jit(solution)/shard_map/update_front/pallas_call | solution.py:345
  321.0 38.7 %all-to-all-done.4.tiles = f32[128,8,16,128]{3,2,1,0:T(8,128)} async-done(((f32[128,8,16,128]{3,2,1,0:T(8,128)}), f32[128,8,16,128]{3,2,1,0:T(8,128)}, u32[]{:S(2)}, u32[]{:S(2)}) %all-to-all-start.4) | async-done | bytes 8388640 | tf_op jit(solution)/shard_map/all_to_all | solution.py:406
  359.7 9.7 %add_tiles.3 = f32[12288,128]{1,0:T(8,128)} custom-call(s32[128]{0:T(128)} %get-tuple-element.28.places, f32[12288,128]{1,0:T(8,128)} %update_front.1.base, f32[128,8,16,128]{3,2,1,0:T(8,128)} %all-to-all-done.4.tiles), custom_call_target="tpu_custom_call" | custom-call | tf_op jit(solution)/shard_map/add_tiles/pallas_call | solution.py:294
  (56 shorter events, 12.4 us)
Async XLA Ops:
  2.2 14.6 %copy-start.7 = (s32[128]{0:T(128)}, s32[128]{0:T(128)S(1)}, u32[]{:S(2)}) copy-start(s32[128]{0:T(128)S(1)} %get-tuple-element.40.slot) | copy-start | bytes 1540
  4.1 20.5 %all-to-all-start = ((s32[128,1,4]{2,1,0:T(1,128)}), s32[128,1,4]{2,1,0:T(1,128)S(1)}, u32[]{:S(2)}, u32[]{:S(2)}) async-start(s32[128,1,4]{2,1,0:T(1,128)} %copy.21), calls=%async_computation | async-start | bytes 131072 | tf_op jit(solution)/shard_map/all_to_all | solution.py:390
  24.6 151.8 %all-to-all-start.1 = ((f32[128,10,16,128]{3,2,1,0:T(8,128)}), f32[128,10,16,128]{3,2,1,0:T(8,128)}, u32[]{:S(2)}, u32[]{:S(2)}) async-start(f32[128,10,16,128]{3,2,1,0:T(8,128)} %bitcast.80), calls=%async_computation.1 | async-start | bytes 20971520 | tf_op jit(solution)/shard_map/all_to_all | solution.py:401
  41.3 126.0 %collective-permute-start = (f32[96,16,128]{2,1,0:T(8,128)}, f32[96,16,128]{2,1,0:T(8,128)S(1)}, u32[]{:S(2)}, u32[]{:S(2)}) collective-permute-start(f32[96,16,128]{2,1,0:T(8,128)} %get-tuple-element.19), channel_id=1, source_target_pairs={{0,1},{8,9},{16,17},{24,25},{32,33},{40,41},{48,49},{56,57},{64,65... | collective-permute-start | bytes 2359304 | tf_op jit(solution)/shard_map/ppermute | solution.py:396
  44.3 129.7 %collective-permute-start.2 = (f32[96,16,128]{2,1,0:T(8,128)}, f32[96,16,128]{2,1,0:T(8,128)S(1)}, u32[]{:S(2)}, u32[]{:S(2)}) collective-permute-start(f32[96,16,128]{2,1,0:T(8,128)} %get-tuple-element.21), channel_id=1, source_target_pairs={{0,7},{8,15},{16,23},{24,31},{32,39},{40,47},{48,55},{56,63},{64,7... | collective-permute-start | bytes 2359304 | tf_op jit(solution)/shard_map/ppermute | solution.py:396
  47.3 141.3 %collective-permute-start.1 = (f32[48,16,128]{2,1,0:T(8,128)}, f32[48,16,128]{2,1,0:T(8,128)S(1)}, u32[]{:S(2)}, u32[]{:S(2)}) collective-permute-start(f32[48,16,128]{2,1,0:T(8,128)} %get-tuple-element.20), channel_id=1, source_target_pairs={{0,2},{8,10},{16,18},{24,26},{32,34},{40,42},{48,50},{56,58},{64,6... | collective-permute-start | bytes 1179656 | tf_op jit(solution)/shard_map/ppermute | solution.py:396
  48.7 140.0 %collective-permute-start.4 = (f32[48,16,128]{2,1,0:T(8,128)}, f32[48,16,128]{2,1,0:T(8,128)S(1)}, u32[]{:S(2)}, u32[]{:S(2)}) collective-permute-start(f32[48,16,128]{2,1,0:T(8,128)} %get-tuple-element.22), channel_id=1, source_target_pairs={{0,4},{8,12},{16,20},{24,28},{32,36},{40,44},{48,52},{56,60},{64,6... | collective-permute-start | bytes 1179656 | tf_op jit(solution)/shard_map/ppermute | solution.py:396
  50.0 138.7 %collective-permute-start.5 = (f32[48,16,128]{2,1,0:T(8,128)}, f32[48,16,128]{2,1,0:T(8,128)S(1)}, u32[]{:S(2)}, u32[]{:S(2)}) collective-permute-start(f32[48,16,128]{2,1,0:T(8,128)} %get-tuple-element.23), channel_id=1, source_target_pairs={{0,6},{8,14},{16,22},{24,30},{32,38},{40,46},{48,54},{56,62},{64,7... | collective-permute-start | bytes 1179656 | tf_op jit(solution)/shard_map/ppermute | solution.py:396
  167.3 29.3 %copy-start = (f32[96,16,128]{2,1,0:T(8,128)}, f32[96,16,128]{2,1,0:T(8,128)S(1)}, u32[]{:S(2)}) copy-start(f32[96,16,128]{2,1,0:T(8,128)S(1)} %collective-permute-done.refs_1_) | copy-start | bytes 2359300
  174.0 22.7 %copy-start.1 = (f32[96,16,128]{2,1,0:T(8,128)}, f32[96,16,128]{2,1,0:T(8,128)S(1)}, u32[]{:S(2)}) copy-start(f32[96,16,128]{2,1,0:T(8,128)S(1)} %collective-permute-done.2.refs_7_) | copy-start | bytes 2359300
  174.8 13.9 %collective-permute-start.3 = (f32[48,16,128]{2,1,0:T(8,128)}, f32[48,16,128]{2,1,0:T(8,128)S(1)}, u32[]{:S(2)}, u32[]{:S(2)}) collective-permute-start(f32[48,16,128]{2,1,0:T(8,128)} %slice_add_fusion), channel_id=1, source_target_pairs={{7,5},{1,3},{15,13},{9,11},{23,21},{17,19},{31,29},{25,27},{39,37}... | collective-permute-start | bytes 1179656 | tf_op jit(solution)/shard_map/ppermute | solution.py:398
  180.4 16.3 %all-to-all-start.2 = ((f32[16,16,128]{2,1,0:T(8,128)}), f32[16,16,128]{2,1,0:T(8,128)S(1)}, u32[]{:S(2)}, u32[]{:S(2)}) async-start(f32[16,16,128]{2,1,0:T(8,128)} %get-tuple-element.16), calls=%async_computation.2 | async-start | bytes 262144 | tf_op jit(solution)/shard_map/all_to_all | solution.py:403
  188.7 8.0 %copy-start.4 = (f32[48,16,128]{2,1,0:T(8,128)}, f32[48,16,128]{2,1,0:T(8,128)S(1)}, u32[]{:S(2)}) copy-start(f32[48,16,128]{2,1,0:T(8,128)S(1)} %collective-permute-done.1.refs_2_) | copy-start | bytes 1179652
  188.7 7.9 %copy-start.5 = (f32[48,16,128]{2,1,0:T(8,128)}, f32[48,16,128]{2,1,0:T(8,128)S(1)}, u32[]{:S(2)}) copy-start(f32[48,16,128]{2,1,0:T(8,128)S(1)} %collective-permute-done.4.refs_4_) | copy-start | bytes 1179652
  188.7 7.9 %copy-start.6 = (f32[48,16,128]{2,1,0:T(8,128)}, f32[48,16,128]{2,1,0:T(8,128)S(1)}, u32[]{:S(2)}) copy-start(f32[48,16,128]{2,1,0:T(8,128)S(1)} %collective-permute-done.5.refs_6_) | copy-start | bytes 1179652
  188.8 7.9 %copy-start.2 = (f32[48,16,128]{2,1,0:T(8,128)}, f32[48,16,128]{2,1,0:T(8,128)S(1)}, u32[]{:S(2)}) copy-start(f32[48,16,128]{2,1,0:T(8,128)S(1)} %collective-permute-done.3.refs_3_.refs_5_) | copy-start | bytes 1179652
  196.6 0.7 copy-start.3
  247.6 112.1 %all-to-all-start.4 = ((f32[128,8,16,128]{3,2,1,0:T(8,128)}), f32[128,8,16,128]{3,2,1,0:T(8,128)}, u32[]{:S(2)}, u32[]{:S(2)}) async-start(f32[128,8,16,128]{3,2,1,0:T(8,128)} %after.1), calls=%async_computation.4 | async-start | bytes 16777216 | tf_op jit(solution)/shard_map/all_to_all | solution.py:406
